TPU v7x, 512 devices: a whole 4x8x8 slice. The times are simulated.
512 devices in a mesh: blk: 512 (over x, y, z, core).
Axes of the slice: x: 4, y: 8, z: 8, core: 2. Of those that a mesh axis runs over, the one named last changes fastest.
Arguments:
- images: float32 [131072, 768], P('blk'), may hold values from -6 to 6
- texts: float32 [131072, 768], P('blk'), may hold values from -6 to 6
Outputs:
- pair_loss: float32 [131072], P('blk')
- image_grad: float32 [131072, 768], P('blk')
- text_grad: float32 [131072, 768], P('blk')
All inputs are finite; a program needn't handle non-finite values.
Results may differ from a plain program's by a relative error of at most 0.0003.
Values sent between devices are 32-bit elements; how exact they have to be, the bound alone decides.
No kernel may reach another device: no remote copies, remote signals or barrier semaphores. Data moves between devices by JAX's collectives and lax.ppermute only.
A program may use at most 64 MiB of HBM per device.

v0:
```python
import math

import jax
import jax.numpy as jnp
from jax import lax
from jax.sharding import PartitionSpec as P

CYCLE = 3


softness_factor = 2.0
logit_bias = -4.0


def with_halo(cells, sides, width):
    for axis, dim in sides:
        count = lax.axis_size(axis)
        head = lax.slice_in_dim(cells, 0, width, axis=dim)
        tail = lax.slice_in_dim(cells, cells.shape[dim] - width, cells.shape[dim], axis=dim)
        cells = jnp.concatenate(
            [
                lax.ppermute(tail, axis, [(i, (i + 1) % count) for i in range(count)]),
                cells,
                lax.ppermute(head, axis, [((i + 1) % count, i) for i in range(count)]),
            ],
            axis=dim,
        )
    return cells


def from_behind(value, axis, by):
    count = lax.axis_size(axis)
    return lax.ppermute(value, axis, [(i, (i + by) % count) for i in range(count)])


def block_weights(images, block, positive):
    logit_scale = softness_factor / math.sqrt(images.shape[1])
    dots = lax.dot_general(images, block, (((1,), (1,)), ((), ())), precision=lax.Precision.HIGHEST)
    logits = logit_scale * dots + logit_bias
    if positive:
        rows = jnp.arange(images.shape[0])
        labels = jnp.where(rows[:, None] == rows[None, :], 1.0, -1.0).astype(jnp.float32)
    else:
        labels = jnp.full(logits.shape, -1.0, jnp.float32)
    signed = labels * logits
    loss_rows = -jnp.sum(jax.nn.log_sigmoid(signed), axis=1)
    coefs = -labels * jax.nn.sigmoid(-signed)
    return (loss_rows, coefs)


def block_terms(images, block, positive):
    loss_rows, coefs = block_weights(images, block, positive)
    image_part = jnp.dot(coefs, block, precision=lax.Precision.HIGHEST)
    text_part = lax.dot_general(
        coefs, images, (((0,), (0,)), ((), ())), precision=lax.Precision.HIGHEST
    )
    return (loss_rows, image_part, text_part)


def per_device(images, texts):
    pairs = images.shape[0]
    window_width = images.shape[1]
    logit_scale = softness_factor / math.sqrt(window_width)
    window_cols = (2 * CYCLE + 1) * pairs
    losses, image_sum, home_sum = block_terms(images, texts, True)
    padded_blocks = with_halo(texts, (("blk", 0),), pairs)
    plus_text = padded_blocks[:pairs]
    minus_text = padded_blocks[2 * pairs :]
    plus_acc = None
    minus_acc = None
    for step in range(1, CYCLE + 1):
        if step > 1:
            plus_text, plus_acc = from_behind((plus_text, plus_acc), "blk", 1)
            minus_text, minus_acc = from_behind((minus_text, minus_acc), "blk", -1)
        plus_loss, plus_image, plus_part = block_terms(images, plus_text, False)
        minus_loss, minus_image, minus_part = block_terms(images, minus_text, False)
        losses = losses + plus_loss + minus_loss
        image_sum = image_sum + plus_image + minus_image
        plus_acc = plus_part if plus_acc is None else plus_acc + plus_part
        minus_acc = minus_part if minus_acc is None else minus_acc + minus_part
    plus_home = plus_acc
    minus_home = minus_acc
    for step in range(CYCLE):
        plus_home = from_behind(plus_home, "blk", -1)
        minus_home = from_behind(minus_home, "blk", 1)
    pair_loss = losses / window_cols
    image_grad = image_sum * logit_scale
    text_grad = (home_sum + plus_home + minus_home) * logit_scale
    return (pair_loss, image_grad, text_grad)


def solution(mesh):
    return jax.shard_map(
        per_device,
        mesh=mesh,
        in_specs=(P("blk", None), P("blk", None)),
        out_specs=(P("blk"), P("blk", None), P("blk", None)),
        check_vma=False,
    )
```

profile of v0, /device:TPU:0, one launch (start us, length us, event | category | flops | bytes accessed | tf_op | source)
XLA Modules:
  0.0 135.2 jit_solution(11056081963153695275)
XLA Ops:
  0.6 2.1 %collective-permute-start = (f32[256,768]{1,0:T(8,128)}, f32[256,768]{1,0:T(8,128)S(1)}, u32[]{:S(2)}, u32[]{:S(2)}) collective-permute-start(f32[256,768]{1,0:T(8,128)} %param.3), channel_id=1, source_target_pairs={{0,1},{1,2},{2,3},{3,4},{4,5},{5,6},{6,7},{7,8},{8,9},{9,10},{10,1... | collective-permute-start | bytes 2359304 | tf_op jit(solution)/shard_map/ppermute | solution.py:22
  2.7 10.1 %collective-permute-start.1 = (f32[256,768]{1,0:T(8,128)}, f32[256,768]{1,0:T(8,128)S(1)}, u32[]{:S(2)}, u32[]{:S(2)}) collective-permute-start(f32[256,768]{1,0:T(8,128)} %param.3), channel_id=1, source_target_pairs={{1,0},{2,1},{3,2},{4,3},{5,4},{6,5},{7,6},{8,7},{9,8},{10,9},{11,1... | collective-permute-start | bytes 2359304 | tf_op jit(solution)/shard_map/ppermute | solution.py:24
  12.8 2.2 %fusion.18 = (f32[256]{0:T(256)S(1)}, f32[256,256]{0,1:T(8,128)S(1)}) fusion(f32[256,768]{1,0:T(8,128)S(1)} %copy-done, f32[256,768]{1,0:T(8,128)} %param.3), kind=kOutput, calls=%fused_computation.40 | convolution fusion | flops 604831488 | bytes 1836032 | tf_op jit(solution)/shard_map/dot_general | solution.py:38
  15.0 5.8 %collective-permute-done = f32[256,768]{1,0:T(8,128)S(1)} collective-permute-done((f32[256,768]{1,0:T(8,128)}, f32[256,768]{1,0:T(8,128)S(1)}, u32[]{:S(2)}, u32[]{:S(2)}) %collective-permute-start) | collective-permute-done | bytes 786464 | tf_op jit(solution)/shard_map/ppermute | solution.py:22
  20.8 1.9 %collective-permute-start.2 = (f32[256,768]{1,0:T(8,128)S(1)}, f32[256,768]{1,0:T(8,128)S(1)}, u32[]{:S(2)}, u32[]{:S(2)}) collective-permute-start(f32[256,768]{1,0:T(8,128)S(1)} %collective-permute-done), channel_id=1, source_target_pairs={{0,1},{1,2},{2,3},{3,4},{4,5},{5,6},{6,7},{7,8},{8,9},{9,10},{10,1... | collective-permute-start | bytes 2359304 | tf_op jit(solution)/shard_map/ppermute | solution.py:33
  22.7 1.0 fusion.19
  24.5 1.9 %collective-permute-start.6 = (f32[256,768]{1,0:T(8,128)S(1)}, f32[256,768]{1,0:T(8,128)S(1)}, u32[]{:S(2)}, u32[]{:S(2)}) collective-permute-start(f32[256,768]{1,0:T(8,128)S(1)} %fusion.25), channel_id=1, source_target_pairs={{0,1},{1,2},{2,3},{3,4},{4,5},{5,6},{6,7},{7,8},{8,9},{9,10},{10,1... | collective-permute-start | bytes 2359304 | tf_op jit(solution)/shard_map/ppermute | solution.py:33
  26.5 9.1 %collective-permute-start.3 = (f32[256,768]{1,0:T(8,128)S(1)}, f32[256,768]{1,0:T(8,128)S(1)}, u32[]{:S(2)}, u32[]{:S(2)}) collective-permute-start(f32[256,768]{1,0:T(8,128)S(1)} %collective-permute-done.1), channel_id=1, source_target_pairs={{0,511},{1,0},{2,1},{3,2},{4,3},{5,4},{6,5},{7,6},{8,7},{9,8},{10,... | collective-permute-start | bytes 2359304 | tf_op jit(solution)/shard_map/ppermute | solution.py:33
  35.6 1.0 fusion.20
  37.4 2.4 %collective-permute-start.11 = (f32[256,768]{1,0:T(8,128)S(1)}, f32[256,768]{1,0:T(8,128)S(1)}, u32[]{:S(2)}, u32[]{:S(2)}) collective-permute-start(f32[256,768]{1,0:T(8,128)S(1)} %fusion.26), channel_id=1, source_target_pairs={{0,511},{1,0},{2,1},{3,2},{4,3},{5,4},{6,5},{7,6},{8,7},{9,8},{10,... | collective-permute-start | bytes 2359304 | tf_op jit(solution)/shard_map/ppermute | solution.py:33
  39.8 1.9 %collective-permute-start.4 = (f32[256,768]{1,0:T(8,128)S(1)}, f32[256,768]{1,0:T(8,128)S(1)}, u32[]{:S(2)}, u32[]{:S(2)}) collective-permute-start(f32[256,768]{1,0:T(8,128)S(1)} %collective-permute-done.2), channel_id=1, source_target_pairs={{0,1},{1,2},{2,3},{3,4},{4,5},{5,6},{6,7},{7,8},{8,9},{9,10},{10,1... | collective-permute-start | bytes 2359304 | tf_op jit(solution)/shard_map/ppermute | solution.py:33
  41.8 1.0 fusion.21
  42.7 5.2 %collective-permute-done.6 = f32[256,768]{1,0:T(8,128)S(1)} collective-permute-done((f32[256,768]{1,0:T(8,128)S(1)}, f32[256,768]{1,0:T(8,128)S(1)}, u32[]{:S(2)}, u32[]{:S(2)}) %collective-permute-start.6) | collective-permute-done | bytes 786464 | tf_op jit(solution)/shard_map/ppermute | solution.py:33
  48.8 1.9 %collective-permute-start.7 = (f32[256,768]{1,0:T(8,128)S(1)}, f32[256,768]{1,0:T(8,128)S(1)}, u32[]{:S(2)}, u32[]{:S(2)}) collective-permute-start(f32[256,768]{1,0:T(8,128)S(1)} %convolution_add_fusion.1), channel_id=1, source_target_pairs={{0,1},{1,2},{2,3},{3,4},{4,5},{5,6},{6,7},{7,8},{8,9},{9,10},{10,1... | collective-permute-start | bytes 2359304 | tf_op jit(solution)/shard_map/ppermute | solution.py:33
  50.7 9.1 %collective-permute-start.5 = (f32[256,768]{1,0:T(8,128)S(1)}, f32[256,768]{1,0:T(8,128)S(1)}, u32[]{:S(2)}, u32[]{:S(2)}) collective-permute-start(f32[256,768]{1,0:T(8,128)S(1)} %collective-permute-done.3), channel_id=1, source_target_pairs={{0,511},{1,0},{2,1},{3,2},{4,3},{5,4},{6,5},{7,6},{8,7},{9,8},{10,... | collective-permute-start | bytes 2359304 | tf_op jit(solution)/shard_map/ppermute | solution.py:33
  61.7 1.9 %collective-permute-start.12 = (f32[256,768]{1,0:T(8,128)S(1)}, f32[256,768]{1,0:T(8,128)S(1)}, u32[]{:S(2)}, u32[]{:S(2)}) collective-permute-start(f32[256,768]{1,0:T(8,128)S(1)} %convolution_add_fusion), channel_id=1, source_target_pairs={{0,511},{1,0},{2,1},{3,2},{4,3},{5,4},{6,5},{7,6},{8,7},{9,8},{10,... | collective-permute-start | bytes 2359304 | tf_op jit(solution)/shard_map/ppermute | solution.py:33
  65.5 2.1 %collective-permute-done.7 = f32[256,768]{1,0:T(8,128)S(1)} collective-permute-done((f32[256,768]{1,0:T(8,128)S(1)}, f32[256,768]{1,0:T(8,128)S(1)}, u32[]{:S(2)}, u32[]{:S(2)}) %collective-permute-start.7) | collective-permute-done | bytes 786464 | tf_op jit(solution)/shard_map/ppermute | solution.py:33
  67.6 2.1 %collective-permute-start.8 = (f32[256,768]{1,0:T(8,128)S(1)}, f32[256,768]{1,0:T(8,128)S(1)}, u32[]{:S(2)}, u32[]{:S(2)}) collective-permute-start(f32[256,768]{1,0:T(8,128)S(1)} %add.153), channel_id=1, source_target_pairs={{0,511},{1,0},{2,1},{3,2},{4,3},{5,4},{6,5},{7,6},{8,7},{9,8},{10,... | collective-permute-start | bytes 2359304 | tf_op jit(solution)/shard_map/ppermute | solution.py:33
  71.6 6.1 %collective-permute-done.12 = f32[256,768]{1,0:T(8,128)S(1)} collective-permute-done((f32[256,768]{1,0:T(8,128)S(1)}, f32[256,768]{1,0:T(8,128)S(1)}, u32[]{:S(2)}, u32[]{:S(2)}) %collective-permute-start.12) | collective-permute-done | bytes 786464 | tf_op jit(solution)/shard_map/ppermute | solution.py:33
  77.8 1.9 %collective-permute-start.13 = (f32[256,768]{1,0:T(8,128)S(1)}, f32[256,768]{1,0:T(8,128)S(1)}, u32[]{:S(2)}, u32[]{:S(2)}) collective-permute-start(f32[256,768]{1,0:T(8,128)S(1)} %add.156), channel_id=1, source_target_pairs={{0,1},{1,2},{2,3},{3,4},{4,5},{5,6},{6,7},{7,8},{8,9},{9,10},{10,1... | collective-permute-start | bytes 2359304 | tf_op jit(solution)/shard_map/ppermute | solution.py:33
  82.4 3.8 %collective-permute-done.8 = f32[256,768]{1,0:T(8,128)S(1)} collective-permute-done((f32[256,768]{1,0:T(8,128)S(1)}, f32[256,768]{1,0:T(8,128)S(1)}, u32[]{:S(2)}, u32[]{:S(2)}) %collective-permute-start.8) | collective-permute-done | bytes 786464 | tf_op jit(solution)/shard_map/ppermute | solution.py:33
  86.2 9.2 %collective-permute-start.9 = (f32[256,768]{1,0:T(8,128)S(1)}, f32[256,768]{1,0:T(8,128)S(1)}, u32[]{:S(2)}, u32[]{:S(2)}) collective-permute-start(f32[256,768]{1,0:T(8,128)S(1)} %collective-permute-done.8), channel_id=1, source_target_pairs={{0,511},{1,0},{2,1},{3,2},{4,3},{5,4},{6,5},{7,6},{8,7},{9,8},{10,... | collective-permute-start | bytes 2359304 | tf_op jit(solution)/shard_map/ppermute | solution.py:33
  95.4 1.3 collective-permute-done.13
  96.7 1.9 %collective-permute-start.14 = (f32[256,768]{1,0:T(8,128)S(1)}, f32[256,768]{1,0:T(8,128)S(1)}, u32[]{:S(2)}, u32[]{:S(2)}) collective-permute-start(f32[256,768]{1,0:T(8,128)S(1)} %collective-permute-done.13), channel_id=1, source_target_pairs={{0,1},{1,2},{2,3},{3,4},{4,5},{5,6},{6,7},{7,8},{8,9},{9,10},{10,1... | collective-permute-start | bytes 2359304 | tf_op jit(solution)/shard_map/ppermute | solution.py:33
  101.3 3.6 %collective-permute-done.9 = f32[256,768]{1,0:T(8,128)S(1)} collective-permute-done((f32[256,768]{1,0:T(8,128)S(1)}, f32[256,768]{1,0:T(8,128)S(1)}, u32[]{:S(2)}, u32[]{:S(2)}) %collective-permute-start.9) | collective-permute-done | bytes 786464 | tf_op jit(solution)/shard_map/ppermute | solution.py:33
  104.9 9.2 %collective-permute-start.10 = (f32[256,768]{1,0:T(8,128)S(1)}, f32[256,768]{1,0:T(8,128)S(1)}, u32[]{:S(2)}, u32[]{:S(2)}) collective-permute-start(f32[256,768]{1,0:T(8,128)S(1)} %collective-permute-done.9), channel_id=1, source_target_pairs={{0,511},{1,0},{2,1},{3,2},{4,3},{5,4},{6,5},{7,6},{8,7},{9,8},{10,... | collective-permute-start | bytes 2359304 | tf_op jit(solution)/shard_map/ppermute | solution.py:33
  114.1 1.3 collective-permute-done.14
  115.5 1.9 %collective-permute-start.15 = (f32[256,768]{1,0:T(8,128)S(1)}, f32[256,768]{1,0:T(8,128)S(1)}, u32[]{:S(2)}, u32[]{:S(2)}) collective-permute-start(f32[256,768]{1,0:T(8,128)S(1)} %collective-permute-done.14), channel_id=1, source_target_pairs={{0,1},{1,2},{2,3},{3,4},{4,5},{5,6},{6,7},{7,8},{8,9},{9,10},{10,1... | collective-permute-start | bytes 2359304 | tf_op jit(solution)/shard_map/ppermute | solution.py:33
  118.8 1.8 %fusion.1 = f32[256,768]{1,0:T(8,128)} fusion(f32[256,768]{1,0:T(8,128)S(1)} %fusion.30, f32[256,768]{1,0:T(8,128)S(1)} %fusion.2, f32[256,768]{1,0:T(8,128)S(1)} %collective-permute-done.4, f32[256,256]{0,1:T(8,128)S(1)} %get-tuple-element.6), kind=kOutput, calls=%fused_computation.4 | convolution fusion | flops 604700672 | bytes 3407872 | tf_op jit(solution)/shard_map/dot_general | solution.py:53
  120.6 3.0 %collective-permute-done.10 = f32[256,768]{1,0:T(8,128)S(1)} collective-permute-done((f32[256,768]{1,0:T(8,128)S(1)}, f32[256,768]{1,0:T(8,128)S(1)}, u32[]{:S(2)}, u32[]{:S(2)}) %collective-permute-start.10) | collective-permute-done | bytes 786464 | tf_op jit(solution)/shard_map/ppermute | solution.py:33
  123.6 10.6 %collective-permute-done.15 = f32[256,768]{1,0:T(8,128)S(1)} collective-permute-done((f32[256,768]{1,0:T(8,128)S(1)}, f32[256,768]{1,0:T(8,128)S(1)}, u32[]{:S(2)}, u32[]{:S(2)}) %collective-permute-start.15) | collective-permute-done | bytes 786464 | tf_op jit(solution)/shard_map/ppermute | solution.py:33
  134.2 1.0 add_multiply_fusion
  (29 shorter events, 15.0 us)
Async XLA Ops:
  0.6 12.2 %copy-start = (f32[256,768]{1,0:T(8,128)S(1)}, f32[256,768]{1,0:T(8,128)}, u32[]{:S(2)}) copy-start(f32[256,768]{1,0:T(8,128)} %param.2) | copy-start | bytes 2359300
  0.6 20.1 %collective-permute-start = (f32[256,768]{1,0:T(8,128)}, f32[256,768]{1,0:T(8,128)S(1)}, u32[]{:S(2)}, u32[]{:S(2)}) collective-permute-start(f32[256,768]{1,0:T(8,128)} %param.3), channel_id=1, source_target_pairs={{0,1},{1,2},{2,3},{3,4},{4,5},{5,6},{6,7},{7,8},{8,9},{9,10},{10,1... | collective-permute-start | bytes 2359304 | tf_op jit(solution)/shard_map/ppermute | solution.py:22
  2.7 23.8 %collective-permute-start.1 = (f32[256,768]{1,0:T(8,128)}, f32[256,768]{1,0:T(8,128)S(1)}, u32[]{:S(2)}, u32[]{:S(2)}) collective-permute-start(f32[256,768]{1,0:T(8,128)} %param.3), channel_id=1, source_target_pairs={{1,0},{2,1},{3,2},{4,3},{5,4},{6,5},{7,6},{8,7},{9,8},{10,9},{11,1... | collective-permute-start | bytes 2359304 | tf_op jit(solution)/shard_map/ppermute | solution.py:24
  20.8 19.1 %collective-permute-start.2 = (f32[256,768]{1,0:T(8,128)S(1)}, f32[256,768]{1,0:T(8,128)S(1)}, u32[]{:S(2)}, u32[]{:S(2)}) collective-permute-start(f32[256,768]{1,0:T(8,128)S(1)} %collective-permute-done), channel_id=1, source_target_pairs={{0,1},{1,2},{2,3},{3,4},{4,5},{5,6},{6,7},{7,8},{8,9},{9,10},{10,1... | collective-permute-start | bytes 2359304 | tf_op jit(solution)/shard_map/ppermute | solution.py:33
  24.5 23.4 %collective-permute-start.6 = (f32[256,768]{1,0:T(8,128)S(1)}, f32[256,768]{1,0:T(8,128)S(1)}, u32[]{:S(2)}, u32[]{:S(2)}) collective-permute-start(f32[256,768]{1,0:T(8,128)S(1)} %fusion.25), channel_id=1, source_target_pairs={{0,1},{1,2},{2,3},{3,4},{4,5},{5,6},{6,7},{7,8},{8,9},{9,10},{10,1... | collective-permute-start | bytes 2359304 | tf_op jit(solution)/shard_map/ppermute | solution.py:33
  26.5 24.3 %collective-permute-start.3 = (f32[256,768]{1,0:T(8,128)S(1)}, f32[256,768]{1,0:T(8,128)S(1)}, u32[]{:S(2)}, u32[]{:S(2)}) collective-permute-start(f32[256,768]{1,0:T(8,128)S(1)} %collective-permute-done.1), channel_id=1, source_target_pairs={{0,511},{1,0},{2,1},{3,2},{4,3},{5,4},{6,5},{7,6},{8,7},{9,8},{10,... | collective-permute-start | bytes 2359304 | tf_op jit(solution)/shard_map/ppermute | solution.py:33
  37.4 23.4 %collective-permute-start.11 = (f32[256,768]{1,0:T(8,128)S(1)}, f32[256,768]{1,0:T(8,128)S(1)}, u32[]{:S(2)}, u32[]{:S(2)}) collective-permute-start(f32[256,768]{1,0:T(8,128)S(1)} %fusion.26), channel_id=1, source_target_pairs={{0,511},{1,0},{2,1},{3,2},{4,3},{5,4},{6,5},{7,6},{8,7},{9,8},{10,... | collective-permute-start | bytes 2359304 | tf_op jit(solution)/shard_map/ppermute | solution.py:33
  39.8 23.8 %collective-permute-start.4 = (f32[256,768]{1,0:T(8,128)S(1)}, f32[256,768]{1,0:T(8,128)S(1)}, u32[]{:S(2)}, u32[]{:S(2)}) collective-permute-start(f32[256,768]{1,0:T(8,128)S(1)} %collective-permute-done.2), channel_id=1, source_target_pairs={{0,1},{1,2},{2,3},{3,4},{4,5},{5,6},{6,7},{7,8},{8,9},{9,10},{10,1... | collective-permute-start | bytes 2359304 | tf_op jit(solution)/shard_map/ppermute | solution.py:33
  48.8 18.7 %collective-permute-start.7 = (f32[256,768]{1,0:T(8,128)S(1)}, f32[256,768]{1,0:T(8,128)S(1)}, u32[]{:S(2)}, u32[]{:S(2)}) collective-permute-start(f32[256,768]{1,0:T(8,128)S(1)} %convolution_add_fusion.1), channel_id=1, source_target_pairs={{0,1},{1,2},{2,3},{3,4},{4,5},{5,6},{6,7},{7,8},{8,9},{9,10},{10,1... | collective-permute-start | bytes 2359304 | tf_op jit(solution)/shard_map/ppermute | solution.py:33
  50.7 19.0 %collective-permute-start.5 = (f32[256,768]{1,0:T(8,128)S(1)}, f32[256,768]{1,0:T(8,128)S(1)}, u32[]{:S(2)}, u32[]{:S(2)}) collective-permute-start(f32[256,768]{1,0:T(8,128)S(1)} %collective-permute-done.3), channel_id=1, source_target_pairs={{0,511},{1,0},{2,1},{3,2},{4,3},{5,4},{6,5},{7,6},{8,7},{9,8},{10,... | collective-permute-start | bytes 2359304 | tf_op jit(solution)/shard_map/ppermute | solution.py:33
  61.7 16.0 %collective-permute-start.12 = (f32[256,768]{1,0:T(8,128)S(1)}, f32[256,768]{1,0:T(8,128)S(1)}, u32[]{:S(2)}, u32[]{:S(2)}) collective-permute-start(f32[256,768]{1,0:T(8,128)S(1)} %convolution_add_fusion), channel_id=1, source_target_pairs={{0,511},{1,0},{2,1},{3,2},{4,3},{5,4},{6,5},{7,6},{8,7},{9,8},{10,... | collective-permute-start | bytes 2359304 | tf_op jit(solution)/shard_map/ppermute | solution.py:33
  67.6 18.5 %collective-permute-start.8 = (f32[256,768]{1,0:T(8,128)S(1)}, f32[256,768]{1,0:T(8,128)S(1)}, u32[]{:S(2)}, u32[]{:S(2)}) collective-permute-start(f32[256,768]{1,0:T(8,128)S(1)} %add.153), channel_id=1, source_target_pairs={{0,511},{1,0},{2,1},{3,2},{4,3},{5,4},{6,5},{7,6},{8,7},{9,8},{10,... | collective-permute-start | bytes 2359304 | tf_op jit(solution)/shard_map/ppermute | solution.py:33
  71.6 8.1 %copy-start.1 = (f32[256,768]{1,0:T(8,128)S(1)}, f32[256,768]{1,0:T(8,128)}, u32[]{:S(2)}) copy-start(f32[256,768]{1,0:T(8,128)} %param.3) | copy-start | bytes 2359300
  77.8 18.9 %collective-permute-start.13 = (f32[256,768]{1,0:T(8,128)S(1)}, f32[256,768]{1,0:T(8,128)S(1)}, u32[]{:S(2)}, u32[]{:S(2)}) collective-permute-start(f32[256,768]{1,0:T(8,128)S(1)} %add.156), channel_id=1, source_target_pairs={{0,1},{1,2},{2,3},{3,4},{4,5},{5,6},{6,7},{7,8},{8,9},{9,10},{10,1... | collective-permute-start | bytes 2359304 | tf_op jit(solution)/shard_map/ppermute | solution.py:33
  86.2 18.7 %collective-permute-start.9 = (f32[256,768]{1,0:T(8,128)S(1)}, f32[256,768]{1,0:T(8,128)S(1)}, u32[]{:S(2)}, u32[]{:S(2)}) collective-permute-start(f32[256,768]{1,0:T(8,128)S(1)} %collective-permute-done.8), channel_id=1, source_target_pairs={{0,511},{1,0},{2,1},{3,2},{4,3},{5,4},{6,5},{7,6},{8,7},{9,8},{10,... | collective-permute-start | bytes 2359304 | tf_op jit(solution)/shard_map/ppermute | solution.py:33
  96.7 18.7 %collective-permute-start.14 = (f32[256,768]{1,0:T(8,128)S(1)}, f32[256,768]{1,0:T(8,128)S(1)}, u32[]{:S(2)}, u32[]{:S(2)}) collective-permute-start(f32[256,768]{1,0:T(8,128)S(1)} %collective-permute-done.13), channel_id=1, source_target_pairs={{0,1},{1,2},{2,3},{3,4},{4,5},{5,6},{6,7},{7,8},{8,9},{9,10},{10,1... | collective-permute-start | bytes 2359304 | tf_op jit(solution)/shard_map/ppermute | solution.py:33
  104.9 18.7 %collective-permute-start.10 = (f32[256,768]{1,0:T(8,128)S(1)}, f32[256,768]{1,0:T(8,128)S(1)}, u32[]{:S(2)}, u32[]{:S(2)}) collective-permute-start(f32[256,768]{1,0:T(8,128)S(1)} %collective-permute-done.9), channel_id=1, source_target_pairs={{0,511},{1,0},{2,1},{3,2},{4,3},{5,4},{6,5},{7,6},{8,7},{9,8},{10,... | collective-permute-start | bytes 2359304 | tf_op jit(solution)/shard_map/ppermute | solution.py:33
  115.5 18.7 %collective-permute-start.15 = (f32[256,768]{1,0:T(8,128)S(1)}, f32[256,768]{1,0:T(8,128)S(1)}, u32[]{:S(2)}, u32[]{:S(2)}) collective-permute-start(f32[256,768]{1,0:T(8,128)S(1)} %collective-permute-done.14), channel_id=1, source_target_pairs={{0,1},{1,2},{2,3},{3,4},{4,5},{5,6},{6,7},{7,8},{8,9},{9,10},{10,1... | collective-permute-start | bytes 2359304 | tf_op jit(solution)/shard_map/ppermute | solution.py:33
where the time goes:
time: 136 us; the launch traced here: 135 us
  starting transfers between devices  68.6 us (50%)
  waiting for transfers between devices  42.8 us (31%)
  matrix products  21 us (15%)
  other arithmetic  1.76 us (1%)
    ppermute x14, starting transfers between devices, from_behind(): lax.ppermute(value, axis, [(i, (i + by) % count) for i in range(count)])  56.4 us
    ppermute x14, waiting for transfers between devices, from_behind(): lax.ppermute(value, axis, [(i, (i + by) % count) for i in range(count)])  37 us
    ppermute x1, starting transfers between devices, with_halo(): lax.ppermute(head, axis, [((i + 1) % count, i) for i in range(count)])  10.1 us
    dot_general x7, matrix products, block_weights(): lax.dot_general(images, block, (((1,), (1,)), ((), ())), precision=lax.Pr...  8.02 us
    dot_general x7, matrix products, block_terms(): image_part = jnp.dot(coefs, block, precision=lax.Precision.HIGHEST)  6.93 us
    dot_general x7, matrix products, block_terms(): lax.dot_general(coefs, images, (((0,), (0,)), ((), ())), precision=lax.Pr...  6.09 us
    ppermute x1, waiting for transfers between devices, with_halo(): lax.ppermute(tail, axis, [(i, (i + 1) % count) for i in range(count)])  5.76 us
  transfers between devices with their start and end apart: 16, of which 10 were waited for; matrix products, arithmetic and copies ran while one was open for 16% of the time, Pallas kernels for 0%

commit v1 on v0

v1 whole, which is shorter than its diff:
```python
import functools
import math

import jax
import jax.numpy as jnp
from jax import lax
from jax.experimental import pallas as pl
from jax.experimental.pallas import tpu as pltpu
from jax.sharding import PartitionSpec as P

CYCLE = 3
softness_factor = 2.0
logit_bias = -4.0
EXTRA = 8
VMEM_LIMIT = 24 * 1024 * 1024


def permuted(value, target):
    count = lax.axis_size("blk")
    return lax.ppermute(value, "blk", [(i, target(i) % count) for i in range(count)])


def sibling(value):
    return permuted(value, lambda i: i ^ 1)


def outward(value):
    return permuted(value, lambda i: i - 2 if i % 2 else i + 2)


def inward(value):
    return permuted(value, lambda i: i + 2 if i % 2 else i - 2)


def across(value):
    return permuted(value, lambda i: i + 1 if i % 2 else i - 1)


def halves(x):
    high = x.astype(jnp.bfloat16)
    return high, (x - high.astype(jnp.float32)).astype(jnp.bfloat16)


def product(a, b, contract_b):
    dims = (((1,), (contract_b,)), ((), ()))
    dot = functools.partial(lax.dot_general, dimension_numbers=dims, preferred_element_type=jnp.float32)
    return dot(a[0], b[0]) + (dot(a[0], b[1]) + dot(a[1], b[0]))


def terms(own, block, positive=False, loss=False):
    scale = softness_factor / math.sqrt(own[0].shape[1])
    x = scale * product(own, block, 1) + logit_bias
    if positive:
        shape = x.shape
        diagonal = lax.broadcasted_iota(jnp.int32, shape, 0) == lax.broadcasted_iota(jnp.int32, shape, 1)
        x = jnp.where(diagonal, -x, x)
    e = jnp.exp(-jnp.abs(x))
    r = 1.0 / (1.0 + e)
    coefs = jnp.where(x >= 0, r, e * r)
    if positive:
        coefs = jnp.where(diagonal, -coefs, coefs)
    if not loss:
        return coefs, None
    series = e * (1.0 - e * (0.5 - e * (1.0 / 3.0 - e * (0.25 - e * 0.2))))
    each = jnp.maximum(x, 0.0) + jnp.where(e < 0.0625, series, jnp.log(1.0 + e))
    return coefs, each[:, :128] + each[:, 128:]


def as_row(loss):
    return jnp.sum(loss.T, axis=0, keepdims=True)


def first_kernel(loss, own_ref, own_sib_ref, partner_ref, partner_sib_ref, block_ref, mine_ref, theirs_ref):
    rows = own_ref.shape[0]
    own, own_sib = halves(own_ref[...]), halves(own_sib_ref[...])
    total, lost = 0.0, 0.0
    for ref, positive in ((partner_ref, True), (partner_sib_ref, False), (block_ref, False)):
        block = halves(ref[...])
        coefs, each = terms(own, block, positive, loss)
        total = total + product(halves(coefs), block, 0)
        if loss:
            lost = lost + each
    mine_ref[:rows, :] = total
    coefs, each = terms(own_sib, block, False, loss)
    theirs_ref[:rows, :] = product(halves(coefs), block, 0)
    if loss:
        mine_ref[rows : rows + 1, : rows] = as_row(lost)
        theirs_ref[rows : rows + 1, : rows] = as_row(each)


def second_kernel(loss, own_ref, own_sib_ref, block_ref, mine_in, theirs_in, mine_ref, theirs_ref):
    rows = own_ref.shape[0]
    block = halves(block_ref[...])
    for ref, given, out in ((own_sib_ref, theirs_in, theirs_ref), (own_ref, mine_in, mine_ref)):
        coefs, each = terms(halves(ref[...]), block, False, loss)
        out[:rows, :] = given[:rows, :] + product(halves(coefs), block, 0)
        if loss:
            out[rows : rows + 1, : rows] = given[rows : rows + 1, : rows] + as_row(each)


def last_kernel(loss, own_ref, block_ref, mine_in, from_sib, grad_ref, *loss_ref):
    rows, width = own_ref.shape
    scale = softness_factor / math.sqrt(width)
    block = halves(block_ref[...])
    coefs, each = terms(halves(own_ref[...]), block, False, loss)
    grad_ref[...] = scale * (mine_in[:rows, :] + from_sib[:rows, :] + product(halves(coefs), block, 0))
    if loss:
        total = mine_in[rows : rows + 1, : rows] + from_sib[rows : rows + 1, : rows] + as_row(each)
        loss_ref[0][...] = total * (1.0 / ((2 * CYCLE + 1) * rows))


def call(kernel, loss, outs, *args):
    return pl.pallas_call(
        functools.partial(kernel, loss),
        out_shape=[jax.ShapeDtypeStruct(s, jnp.float32) for s in outs],
        compiler_params=pltpu.CompilerParams(vmem_limit_bytes=VMEM_LIMIT),
        cost_estimate=pl.CostEstimate(flops=1000, bytes_accessed=1000, transcendentals=0),
    )(*args)


def per_device(images, texts):
    rows, width = images.shape
    part = ((rows + EXTRA, width), (rows + EXTRA, width))
    part_text = ((rows, width), (rows, width))

    t_in = inward(texts)
    t_out = outward(texts)
    t_sib, i_sib = sibling(texts), sibling(images)
    i_in = inward(images)
    i_out = outward(images)
    t_far = across(t_in)
    i_far = across(i_in)

    i_mine, i_theirs = call(first_kernel, True, part, images, i_sib, texts, t_sib, t_in)
    i_mine, i_theirs = call(second_kernel, True, part, images, i_sib, t_out, i_mine, i_theirs)
    i_theirs = sibling(i_theirs)
    t_mine, t_theirs = call(first_kernel, False, part_text, texts, t_sib, images, i_sib, i_in)
    t_mine, t_theirs = call(second_kernel, False, part_text, texts, t_sib, i_out, t_mine, t_theirs)
    t_theirs = sibling(t_theirs)
    image_grad, pair_loss = call(last_kernel, True, ((rows, width), (1, rows)), images, t_far, i_mine, i_theirs)
    (text_grad,) = call(last_kernel, False, ((rows, width),), texts, i_far, t_mine, t_theirs)
    return (pair_loss.reshape(rows), image_grad, text_grad)


def solution(mesh):
    return jax.shard_map(
        per_device,
        mesh=mesh,
        in_specs=(P("blk", None), P("blk", None)),
        out_specs=(P("blk"), P("blk", None), P("blk", None)),
        check_vma=False,
    )
```

time: 136 us -> 87 us (0.64)
  the two profiles are of different devices: /device:TPU:0 before, /device:TPU:1 now
where the time goes in v1:
time: 87 us; the launch traced here: 86.6 us
  starting transfers between devices  54.6 us (63%)
  Pallas kernels  19.6 us (23%)
  waiting for transfers between devices  9.31 us (11%)
  local copies, waits for them, and re-layouts  2.3 us (3%)
    ppermute x10, starting transfers between devices, permuted(): lax.ppermute(value, 'blk', [(i, target(i) % count) for i in range(count)])  54.6 us
    pallas_call x6, Pallas kernels, call(): pl.pallas_call(functools.partial(kernel, loss), out_shape=[jax.ShapeDtype...  19.6 us
    ppermute x10, waiting for transfers between devices, permuted(): lax.ppermute(value, 'blk', [(i, target(i) % count) for i in range(count)])  9.31 us
    unnamed x8, local copies, waits for them, and re-layouts  2.3 us
  transfers between devices with their start and end apart: 10, of which 1 were waited for; matrix products, arithmetic and copies ran while one was open for 0% of the time, Pallas kernels for 20%

profile of v1, /device:TPU:1, one launch (start us, length us, event | category | flops | bytes accessed | tf_op | source)
XLA Modules:
  0.0 86.6 jit_solution(11418638714516360932)
XLA Ops:
  0.6 8.8 %collective-permute-start.2 = (f32[256,768]{1,0:T(8,128)}, f32[256,768]{1,0:T(8,128)S(1)}, u32[]{:S(2)}, u32[]{:S(2)}) collective-permute-start(f32[256,768]{1,0:T(8,128)} %partner_ref.3), channel_id=1, source_target_pairs={{0,1},{1,0},{2,3},{3,2},{4,5},{5,4},{6,7},{7,6},{8,9},{9,8},{10,11... | collective-permute-start | bytes 2359304 | tf_op jit(solution)/shard_map/ppermute | solution.py:20
  9.4 1.9 %collective-permute-start.4 = (f32[256,768]{1,0:T(8,128)}, f32[256,768]{1,0:T(8,128)S(1)}, u32[]{:S(2)}, u32[]{:S(2)}) collective-permute-start(f32[256,768]{1,0:T(8,128)} %own_ref.11), channel_id=1, source_target_pairs={{0,1},{1,0},{2,3},{3,2},{4,5},{5,4},{6,7},{7,6},{8,9},{9,8},{10,11... | collective-permute-start | bytes 2359304 | tf_op jit(solution)/shard_map/ppermute | solution.py:20
  11.4 1.9 %collective-permute-start = (f32[256,768]{1,0:T(8,128)}, f32[256,768]{1,0:T(8,128)S(1)}, u32[]{:S(2)}, u32[]{:S(2)}) collective-permute-start(f32[256,768]{1,0:T(8,128)} %own_ref.11), channel_id=1, source_target_pairs={{0,510},{1,3},{2,0},{3,5},{4,2},{5,7},{6,4},{7,9},{8,6},{9,11},{10... | collective-permute-start | bytes 2359304 | tf_op jit(solution)/shard_map/ppermute | solution.py:20
  13.3 10.4 %collective-permute-start.3 = (f32[256,768]{1,0:T(8,128)}, f32[256,768]{1,0:T(8,128)S(1)}, u32[]{:S(2)}, u32[]{:S(2)}) collective-permute-start(f32[256,768]{1,0:T(8,128)} %own_ref.11), channel_id=1, source_target_pairs={{0,2},{1,511},{2,4},{3,1},{4,6},{5,3},{6,8},{7,5},{8,10},{9,7},{10... | collective-permute-start | bytes 2359304 | tf_op jit(solution)/shard_map/ppermute | solution.py:20
  23.7 1.9 %collective-permute-start.6 = (f32[256,768]{1,0:T(8,128)}, f32[256,768]{1,0:T(8,128)S(1)}, u32[]{:S(2)}, u32[]{:S(2)}) collective-permute-start(f32[256,768]{1,0:T(8,128)} %partner_ref.3), channel_id=1, source_target_pairs={{0,510},{1,3},{2,0},{3,5},{4,2},{5,7},{6,4},{7,9},{8,6},{9,11},{10... | collective-permute-start | bytes 2359304 | tf_op jit(solution)/shard_map/ppermute | solution.py:20
  25.6 0.0 collective-permute-done.2.own_sib_ref.partner_sib_ref
  25.6 8.8 %collective-permute-start.8 = (f32[256,768]{1,0:T(8,128)}, f32[256,768]{1,0:T(8,128)S(1)}, u32[]{:S(2)}, u32[]{:S(2)}) collective-permute-start(f32[256,768]{1,0:T(8,128)} %partner_ref.3), channel_id=1, source_target_pairs={{0,2},{1,511},{2,4},{3,1},{4,6},{5,3},{6,8},{7,5},{8,10},{9,7},{10... | collective-permute-start | bytes 2359304 | tf_op jit(solution)/shard_map/ppermute | solution.py:20
  34.4 0.0 collective-permute-done.4.partner_sib_ref.own_sib_ref
  34.4 0.0 collective-permute-done.block_ref
  34.5 0.0 copy-start
  34.5 1.1 %copy-done = f32[256,768]{1,0:T(8,128)S(1)} copy-done((f32[256,768]{1,0:T(8,128)S(1)}, f32[256,768]{1,0:T(8,128)}, u32[]{:S(2)}) %copy-start) | copy-done | bytes 786456
  35.6 1.1 %copy-done.2 = f32[256,768]{1,0:T(8,128)S(1)} copy-done((f32[256,768]{1,0:T(8,128)S(1)}, f32[256,768]{1,0:T(8,128)}, u32[]{:S(2)}) %copy-start.2) | copy-done | bytes 786456
  36.8 4.5 %shard_map.49 = (f32[264,768]{1,0:T(8,128)S(1)}, f32[264,768]{1,0:T(8,128)S(1)}) custom-call(f32[256,768]{1,0:T(8,128)S(1)} %copy-done, f32[256,768]{1,0:T(8,128)S(1)} %collective-permute-done.2.own_sib_ref.partner_sib_ref, f32[256,768]{1,0:T(8,128)S(1)} %copy-done.2, f32[256,768]{1,0:T(8,128)S(1)} %collective-permute-done.4.partner_sib_ref.own_sib_ref, ...), custom_call_target="tpu_custom_call" | custom-call | flops 1000 | bytes 1000 | tf_op jit(solution)/shard_map/pallas_call | solution.py:113
  41.3 0.0 collective-permute-done.3.block_ref
  41.3 3.1 %shard_map.50 = (f32[264,768]{1,0:T(8,128)S(1)}, f32[264,768]{1,0:T(8,128)S(1)}) custom-call(f32[256,768]{1,0:T(8,128)S(1)} %copy-done, f32[256,768]{1,0:T(8,128)S(1)} %collective-permute-done.2.own_sib_ref.partner_sib_ref, f32[256,768]{1,0:T(8,128)S(1)} %collective-permute-done.3.block_ref, f32[264,768]{1,0:T(8,128)S(1)} %get-tuple-element.13.mine_in, ...), custom_call_target="tpu_custom_call" | custom-call | flops 1000 | bytes 1000 | tf_op jit(solution)/shard_map/pallas_call | solution.py:113
  44.4 10.4 %collective-permute-start.5 = (f32[264,768]{1,0:T(8,128)S(1)}, f32[264,768]{1,0:T(8,128)S(1)}, u32[]{:S(2)}, u32[]{:S(2)}) collective-permute-start(f32[264,768]{1,0:T(8,128)S(1)} %get-tuple-element.16), channel_id=1, source_target_pairs={{0,1},{1,0},{2,3},{3,2},{4,5},{5,4},{6,7},{7,6},{8,9},{9,8},{10,11... | collective-permute-start | bytes 2433032 | tf_op jit(solution)/shard_map/ppermute | solution.py:20
  54.8 0.0 collective-permute-done.6.block_ref
  54.8 1.9 %collective-permute-start.7 = (f32[256,768]{1,0:T(8,128)S(1)}, f32[256,768]{1,0:T(8,128)S(1)}, u32[]{:S(2)}, u32[]{:S(2)}) collective-permute-start(f32[256,768]{1,0:T(8,128)S(1)} %collective-permute-done.6.block_ref), channel_id=1, source_target_pairs={{0,511},{1,2},{2,1},{3,4},{4,3},{5,6},{6,5},{7,8},{8,7},{9,10},{10... | collective-permute-start | bytes 2359304 | tf_op jit(solution)/shard_map/ppermute | solution.py:20
  56.8 0.0 copy-done.3
  56.8 4.2 %shard_map.52 = (f32[256,768]{1,0:T(8,128)S(1)}, f32[256,768]{1,0:T(8,128)S(1)}) custom-call(f32[256,768]{1,0:T(8,128)S(1)} %copy-done.3, f32[256,768]{1,0:T(8,128)S(1)} %collective-permute-done.4.partner_sib_ref.own_sib_ref, f32[256,768]{1,0:T(8,128)S(1)} %copy-done, f32[256,768]{1,0:T(8,128)S(1)} %collective-permute-done.2.own_sib_ref.partner_sib_ref, ...), custom_call_target="tpu_custom_call" | custom-call | flops 1000 | bytes 1000 | tf_op jit(solution)/shard_map/pallas_call | solution.py:113
  61.0 0.0 collective-permute-done.8.block_ref
  61.0 2.8 %shard_map.53 = (f32[256,768]{1,0:T(8,128)S(1)}, f32[256,768]{1,0:T(8,128)S(1)}) custom-call(f32[256,768]{1,0:T(8,128)S(1)} %copy-done.3, f32[256,768]{1,0:T(8,128)S(1)} %collective-permute-done.4.partner_sib_ref.own_sib_ref, f32[256,768]{1,0:T(8,128)S(1)} %collective-permute-done.8.block_ref, f32[256,768]{1,0:T(8,128)S(1)} %get-tuple-element.19.mine_in, ...), custom_call_target="tpu_custom_call" | custom-call | flops 1000 | bytes 1000 | tf_op jit(solution)/shard_map/pallas_call | solution.py:113
  63.8 6.6 %collective-permute-start.9 = (f32[256,768]{1,0:T(8,128)S(1)}, f32[256,768]{1,0:T(8,128)S(1)}, u32[]{:S(2)}, u32[]{:S(2)}) collective-permute-start(f32[256,768]{1,0:T(8,128)S(1)} %get-tuple-element.22), channel_id=1, source_target_pairs={{0,1},{1,0},{2,3},{3,2},{4,5},{5,4},{6,7},{7,6},{8,9},{9,8},{10,11... | collective-permute-start | bytes 2359304 | tf_op jit(solution)/shard_map/ppermute | solution.py:20
  70.5 1.9 %collective-permute-start.1 = (f32[256,768]{1,0:T(8,128)S(1)}, f32[256,768]{1,0:T(8,128)S(1)}, u32[]{:S(2)}, u32[]{:S(2)}) collective-permute-start(f32[256,768]{1,0:T(8,128)S(1)} %collective-permute-done.block_ref), channel_id=1, source_target_pairs={{0,511},{1,2},{2,1},{3,4},{4,3},{5,6},{6,5},{7,8},{8,7},{9,10},{10... | collective-permute-start | bytes 2359304 | tf_op jit(solution)/shard_map/ppermute | solution.py:20
  72.4 0.0 collective-permute-done.7.block_ref
  72.4 0.0 collective-permute-done.9.from_sib
  72.4 0.0 copy-start.1
  72.4 2.4 %shard_map.54 = f32[256,768]{1,0:T(8,128)} custom-call(f32[256,768]{1,0:T(8,128)S(1)} %copy-done.3, f32[256,768]{1,0:T(8,128)S(1)} %collective-permute-done.7.block_ref, f32[256,768]{1,0:T(8,128)S(1)} %get-tuple-element.21.mine_in, f32[256,768]{1,0:T(8,128)S(1)} %collective-permute-done.9.from_sib), custom_call_target="tpu_custom_call" | custom-call | flops 1000 | bytes 1000 | tf_op jit(solution)/shard_map/pallas_call | solution.py:113
  74.8 9.2 %collective-permute-done.1.block_ref = f32[256,768]{1,0:T(8,128)S(1)} collective-permute-done((f32[256,768]{1,0:T(8,128)S(1)}, f32[256,768]{1,0:T(8,128)S(1)}, u32[]{:S(2)}, u32[]{:S(2)}) %collective-permute-start.1) | collective-permute-done | bytes 786464 | tf_op jit(solution)/shard_map/ppermute | solution.py:20
  84.1 0.0 collective-permute-done.5.from_sib
  84.1 0.0 copy-done.1
  84.1 2.5 %shard_map.51 = (f32[256,768]{1,0:T(8,128)}, f32[1,256]{1,0:T(1,128)}) custom-call(f32[256,768]{1,0:T(8,128)S(1)} %copy-done.1, f32[256,768]{1,0:T(8,128)S(1)} %collective-permute-done.1.block_ref, f32[264,768]{1,0:T(8,128)S(1)} %get-tuple-element.15.mine_in, f32[264,768]{1,0:T(8,128)S(1)} %collective-permute-done.5.from_sib), custom_call_target="tpu_custom_call" | custom-call | flops 1000 | bytes 1000 | tf_op jit(solution)/shard_map/pallas_call | solution.py:113
  (2 shorter events, 0.0 us)
Async XLA Ops:
  0.6 25.0 %collective-permute-start.2 = (f32[256,768]{1,0:T(8,128)}, f32[256,768]{1,0:T(8,128)S(1)}, u32[]{:S(2)}, u32[]{:S(2)}) collective-permute-start(f32[256,768]{1,0:T(8,128)} %partner_ref.3), channel_id=1, source_target_pairs={{0,1},{1,0},{2,3},{3,2},{4,5},{5,4},{6,7},{7,6},{8,9},{9,8},{10,11... | collective-permute-start | bytes 2359304 | tf_op jit(solution)/shard_map/ppermute | solution.py:20
  9.4 25.0 %collective-permute-start.4 = (f32[256,768]{1,0:T(8,128)}, f32[256,768]{1,0:T(8,128)S(1)}, u32[]{:S(2)}, u32[]{:S(2)}) collective-permute-start(f32[256,768]{1,0:T(8,128)} %own_ref.11), channel_id=1, source_target_pairs={{0,1},{1,0},{2,3},{3,2},{4,5},{5,4},{6,7},{7,6},{8,9},{9,8},{10,11... | collective-permute-start | bytes 2359304 | tf_op jit(solution)/shard_map/ppermute | solution.py:20
  11.4 23.1 %collective-permute-start = (f32[256,768]{1,0:T(8,128)}, f32[256,768]{1,0:T(8,128)S(1)}, u32[]{:S(2)}, u32[]{:S(2)}) collective-permute-start(f32[256,768]{1,0:T(8,128)} %own_ref.11), channel_id=1, source_target_pairs={{0,510},{1,3},{2,0},{3,5},{4,2},{5,7},{6,4},{7,9},{8,6},{9,11},{10... | collective-permute-start | bytes 2359304 | tf_op jit(solution)/shard_map/ppermute | solution.py:20
  13.3 28.1 %collective-permute-start.3 = (f32[256,768]{1,0:T(8,128)}, f32[256,768]{1,0:T(8,128)S(1)}, u32[]{:S(2)}, u32[]{:S(2)}) collective-permute-start(f32[256,768]{1,0:T(8,128)} %own_ref.11), channel_id=1, source_target_pairs={{0,2},{1,511},{2,4},{3,1},{4,6},{5,3},{6,8},{7,5},{8,10},{9,7},{10... | collective-permute-start | bytes 2359304 | tf_op jit(solution)/shard_map/ppermute | solution.py:20
  23.7 31.1 %collective-permute-start.6 = (f32[256,768]{1,0:T(8,128)}, f32[256,768]{1,0:T(8,128)S(1)}, u32[]{:S(2)}, u32[]{:S(2)}) collective-permute-start(f32[256,768]{1,0:T(8,128)} %partner_ref.3), channel_id=1, source_target_pairs={{0,510},{1,3},{2,0},{3,5},{4,2},{5,7},{6,4},{7,9},{8,6},{9,11},{10... | collective-permute-start | bytes 2359304 | tf_op jit(solution)/shard_map/ppermute | solution.py:20
  25.6 35.4 %collective-permute-start.8 = (f32[256,768]{1,0:T(8,128)}, f32[256,768]{1,0:T(8,128)S(1)}, u32[]{:S(2)}, u32[]{:S(2)}) collective-permute-start(f32[256,768]{1,0:T(8,128)} %partner_ref.3), channel_id=1, source_target_pairs={{0,2},{1,511},{2,4},{3,1},{4,6},{5,3},{6,8},{7,5},{8,10},{9,7},{10... | collective-permute-start | bytes 2359304 | tf_op jit(solution)/shard_map/ppermute | solution.py:20
  34.5 1.2 %copy-start = (f32[256,768]{1,0:T(8,128)S(1)}, f32[256,768]{1,0:T(8,128)}, u32[]{:S(2)}) copy-start(f32[256,768]{1,0:T(8,128)} %partner_ref.3) | copy-start | bytes 2359300
  35.6 1.1 %copy-start.2 = (f32[256,768]{1,0:T(8,128)S(1)}, f32[256,768]{1,0:T(8,128)}, u32[]{:S(2)}) copy-start(f32[256,768]{1,0:T(8,128)} %own_ref.11) | copy-start | bytes 2359300
  41.3 15.4 %copy-start.3 = (f32[256,768]{1,0:T(8,128)S(1)}, f32[256,768]{1,0:T(8,128)}, u32[]{:S(2)}) copy-start(f32[256,768]{1,0:T(8,128)} %own_ref.11) | copy-start | bytes 2359300
  44.4 39.7 %collective-permute-start.5 = (f32[264,768]{1,0:T(8,128)S(1)}, f32[264,768]{1,0:T(8,128)S(1)}, u32[]{:S(2)}, u32[]{:S(2)}) collective-permute-start(f32[264,768]{1,0:T(8,128)S(1)} %get-tuple-element.16), channel_id=1, source_target_pairs={{0,1},{1,0},{2,3},{3,2},{4,5},{5,4},{6,7},{7,6},{8,9},{9,8},{10,11... | collective-permute-start | bytes 2433032 | tf_op jit(solution)/shard_map/ppermute | solution.py:20
  54.8 17.5 %collective-permute-start.7 = (f32[256,768]{1,0:T(8,128)S(1)}, f32[256,768]{1,0:T(8,128)S(1)}, u32[]{:S(2)}, u32[]{:S(2)}) collective-permute-start(f32[256,768]{1,0:T(8,128)S(1)} %collective-permute-done.6.block_ref), channel_id=1, source_target_pairs={{0,511},{1,2},{2,1},{3,4},{4,3},{5,6},{6,5},{7,8},{8,7},{9,10},{10... | collective-permute-start | bytes 2359304 | tf_op jit(solution)/shard_map/ppermute | solution.py:20
  63.8 8.6 %collective-permute-start.9 = (f32[256,768]{1,0:T(8,128)S(1)}, f32[256,768]{1,0:T(8,128)S(1)}, u32[]{:S(2)}, u32[]{:S(2)}) collective-permute-start(f32[256,768]{1,0:T(8,128)S(1)} %get-tuple-element.22), channel_id=1, source_target_pairs={{0,1},{1,0},{2,3},{3,2},{4,5},{5,4},{6,7},{7,6},{8,9},{9,8},{10,11... | collective-permute-start | bytes 2359304 | tf_op jit(solution)/shard_map/ppermute | solution.py:20
  70.5 13.6 %collective-permute-start.1 = (f32[256,768]{1,0:T(8,128)S(1)}, f32[256,768]{1,0:T(8,128)S(1)}, u32[]{:S(2)}, u32[]{:S(2)}) collective-permute-start(f32[256,768]{1,0:T(8,128)S(1)} %collective-permute-done.block_ref), channel_id=1, source_target_pairs={{0,511},{1,2},{2,1},{3,4},{4,3},{5,6},{6,5},{7,8},{8,7},{9,10},{10... | collective-permute-start | bytes 2359304 | tf_op jit(solution)/shard_map/ppermute | solution.py:20
  72.4 11.7 %copy-start.1 = (f32[256,768]{1,0:T(8,128)S(1)}, f32[256,768]{1,0:T(8,128)}, u32[]{:S(2)}) copy-start(f32[256,768]{1,0:T(8,128)} %partner_ref.3) | copy-start | bytes 2359300

commit v2 on v1

v2 whole, which is shorter than its diff:
```python
import functools
import math

import jax
import jax.numpy as jnp
from jax import lax
from jax.experimental import pallas as pl
from jax.experimental.pallas import tpu as pltpu
from jax.sharding import PartitionSpec as P

CYCLE = 3
softness_factor = 2.0
logit_bias = -4.0
EXTRA = 8
FLOPS_C = 2_000_000_000
FLOPS_D = 2_000_000_000
VMEM_LIMIT = 24 * 1024 * 1024


def permuted(value, target):
    count = lax.axis_size("blk")
    return lax.ppermute(value, "blk", [(i, target(i) % count) for i in range(count)])


def sibling(value):
    return permuted(value, lambda i: i ^ 1)


def outward(value):
    return permuted(value, lambda i: i - 2 if i % 2 else i + 2)


def inward(value):
    return permuted(value, lambda i: i + 2 if i % 2 else i - 2)


def across(value):
    return permuted(value, lambda i: i + 1 if i % 2 else i - 1)


def after(value, *others):
    return lax.optimization_barrier((value,) + others)[0]


def halves(x):
    high = x.astype(jnp.bfloat16)
    return high, (x - high.astype(jnp.float32)).astype(jnp.bfloat16)


def dot(a, b, contract_b):
    dims = (((1,), (contract_b,)), ((), ()))
    return lax.dot_general(a, b, dims, preferred_element_type=jnp.float32)


def dots_of(own, block):
    return dot(own[0], block[0], 1) + dot(own[0], block[1], 1) + dot(own[1], block[0], 1)


def weighted(total, coefs, block):
    high, low = halves(coefs)
    first = dot(high, block[0], 0)
    total = first if total is None else total + first
    return total + dot(high, block[1], 0) + dot(low, block[0], 0)


def terms(own, block, positive=False, loss=False):
    scale = softness_factor / math.sqrt(own[0].shape[1])
    x = scale * dots_of(own, block) + logit_bias
    if positive:
        diagonal = lax.broadcasted_iota(jnp.int32, x.shape, 0) == lax.broadcasted_iota(jnp.int32, x.shape, 1)
        x = jnp.where(diagonal, -x, x)
    e = jnp.exp(-jnp.abs(x))
    r = 1.0 / (1.0 + e)
    coefs = jnp.where(x >= 0, r, e * r)
    if positive:
        coefs = jnp.where(diagonal, -coefs, coefs)
    if not loss:
        return coefs, None
    series = e * (1.0 - e * (0.5 - e * (1.0 / 3.0 - e * (0.25 - e * 0.2))))
    each = jnp.maximum(x, 0.0) + jnp.where(e < 0.0625, series, jnp.log(1.0 + e))
    return coefs, each[:, :128] + each[:, 128:]


def as_row(loss):
    return jnp.sum(loss.T, axis=0, keepdims=True)


def own_kernel(
    i_hbm, t_hbm, i_mine_ref, l_mine_ref, i_high_ref, i_low_ref, t_mine_ref, t_high_ref, t_low_ref, i_ref, t_ref, sems
):
    copies = [
        pltpu.make_async_copy(source, target, sems.at[k])
        for k, (source, target) in enumerate(((i_hbm, i_ref), (t_hbm, t_ref)))
    ]
    for copy in copies:
        copy.start()
    for copy in copies:
        copy.wait()
    own, texts = halves(i_ref[...]), halves(t_ref[...])
    i_high_ref[...], i_low_ref[...] = own
    t_high_ref[...], t_low_ref[...] = texts
    coefs, lost = terms(own, texts, True, True)
    i_mine_ref[...] = weighted(None, coefs, texts)
    l_mine_ref[...] = jnp.broadcast_to(as_row(lost), l_mine_ref.shape)
    coefs, _ = terms(texts, own, True)
    t_mine_ref[...] = weighted(None, coefs, own)


def texts_kernel(high_ref, low_ref, in_ref, out_ref, given_ref, l_given, mine_ref, l_mine_ref):
    own = high_ref[...], low_ref[...]
    blocks = [halves(in_ref[...]), halves(out_ref[...])]
    found = [terms(own, block, False, True) for block in blocks]
    mine = given_ref[...]
    for (coefs, _), block in zip(found, blocks):
        mine = weighted(mine, coefs, block)
    mine_ref[...] = mine
    l_mine_ref[...] = l_given[...] + as_row(found[0][1] + found[1][1])


def pair_kernel(
    i_sib_ref, t_sib_ref, in_ref, out_ref, i_high_ref, i_low_ref, t_high_ref, t_low_ref, i_given, l_given, t_given,
    i_mine_ref, theirs_ref, l_mine_ref, t_mine_ref, high_ref, low_ref,
):
    rows = i_sib_ref.shape[0]
    images, texts = halves(i_sib_ref[...]), halves(t_sib_ref[...])
    own_texts = t_high_ref[...], t_low_ref[...]
    high_ref[:rows, :], low_ref[:rows, :] = own_texts
    high_ref[rows:, :], low_ref[rows:, :] = texts
    coefs, lost = terms((i_high_ref[...], i_low_ref[...]), texts, False, True)
    i_mine_ref[...] = weighted(i_given[...], coefs, texts)
    l_mine_ref[...] = l_given[...] + as_row(lost)
    coefs, _ = terms(own_texts, images)
    t_mine_ref[...] = weighted(t_given[...], coefs, images)
    theirs, lost = None, 0.0
    for ref in (in_ref, out_ref):
        block = halves(ref[...])
        coefs, each = terms(images, block, False, True)
        theirs = weighted(theirs, coefs, block)
        lost = lost + each
    theirs_ref[:rows, :] = theirs
    theirs_ref[rows:, :rows] = jnp.broadcast_to(as_row(lost), (EXTRA, rows))


def images_kernel(high_ref, low_ref, in_ref, out_ref, given_ref, mine_ref, theirs_ref):
    rows = in_ref.shape[0]
    both = high_ref[...], low_ref[...]
    total = None
    blocks = [halves(in_ref[...]), halves(out_ref[...])]
    coefs = [terms(both, block)[0] for block in blocks]
    for coef, block in zip(coefs, blocks):
        total = weighted(total, coef, block)
    mine_ref[...] = given_ref[...] + total[:rows]
    theirs_ref[...] = total[rows:]


def far_kernel(loss, high_ref, low_ref, block_ref, given_ref, *rest):
    rows = block_ref.shape[0]
    block = halves(block_ref[...])
    coefs, each = terms((high_ref[:rows, :], low_ref[:rows, :]), block, False, loss)
    mine_ref = rest[1] if loss else rest[0]
    mine_ref[...] = weighted(given_ref[...], coefs, block)
    if loss:
        rest[2][...] = rest[0][...] + as_row(each)


def final_kernel(i_mine, i_theirs, l_mine, t_mine, t_theirs, image_ref, text_ref, loss_ref):
    rows, width = t_mine.shape
    scale = softness_factor / math.sqrt(width)
    image_ref[...] = scale * (i_mine[...] + i_theirs[:rows, :])
    text_ref[...] = scale * (t_mine[...] + t_theirs[...])
    loss_ref[...] = (l_mine[:1, :] + i_theirs[rows : rows + 1, :rows]) * (1.0 / ((2 * CYCLE + 1) * rows))


def call(kernel, outs, *args, flops=1000, **specs):
    return pl.pallas_call(
        kernel,
        out_shape=[jax.ShapeDtypeStruct(shape, dtype) for shape, dtype in outs],
        compiler_params=pltpu.CompilerParams(vmem_limit_bytes=VMEM_LIMIT),
        cost_estimate=pl.CostEstimate(flops=flops, bytes_accessed=1000, transcendentals=0),
        **specs,
    )(*args)


def per_device(images, texts):
    rows, width = images.shape
    f32, bf16 = jnp.float32, jnp.bfloat16
    grad, longer = ((rows, width), f32), ((rows + EXTRA, width), f32)
    low, low2, loss = ((rows, width), bf16), ((2 * rows, width), bf16), ((EXTRA, rows), f32)

    t_in, t_out = inward(texts), outward(texts)
    t_sib, i_sib = sibling(texts), sibling(images)
    i_mine, l_mine, i_high, i_low, t_mine, t_high, t_low = call(
        own_kernel,
        (grad, loss, low, low, grad, low, low),
        images,
        texts,
        in_specs=[pl.BlockSpec(memory_space=pl.ANY)] * 2,
        scratch_shapes=[pltpu.VMEM(images.shape, f32)] * 2 + [pltpu.SemaphoreType.DMA((2,))],
    )
    i_in, i_out = inward(after(images, t_mine)), outward(images)
    t_far = across(t_in)
    i_mine, l_mine = call(texts_kernel, (grad, loss), i_high, i_low, t_in, t_out, i_mine, l_mine)
    i_far = across(after(i_in, l_mine))
    i_mine, i_theirs, l_mine, t_mine, t_high, t_low = call(
        pair_kernel,
        (grad, longer, loss, grad, low2, low2),
        i_sib, t_sib, t_in, t_out, i_high, i_low, t_high, t_low, i_mine, l_mine, t_mine,
    )
    i_theirs = sibling(i_theirs)
    t_mine, t_theirs = call(images_kernel, (grad, grad), t_high, t_low, i_in, i_out, t_mine)
    t_theirs = sibling(t_theirs)
    i_mine, l_mine = call(
        functools.partial(far_kernel, True), (grad, loss), i_high, i_low, t_far, after(i_mine, t_mine), l_mine, flops=FLOPS_C
    )
    (t_mine,) = call(
        functools.partial(far_kernel, False), (grad,), t_high, t_low, i_far, after(t_mine, l_mine), flops=FLOPS_D
    )
    image_grad, text_grad, pair_loss = call(
        final_kernel, (grad, grad, ((1, rows), f32)), i_mine, i_theirs, l_mine, t_mine, t_theirs
    )
    return (pair_loss.reshape(rows), image_grad, text_grad)


def solution(mesh):
    return jax.shard_map(
        per_device,
        mesh=mesh,
        in_specs=(P("blk", None), P("blk", None)),
        out_specs=(P("blk"), P("blk", None), P("blk", None)),
        check_vma=False,
    )
```

time: 87 us -> 73.4 us (0.84)
  waiting for transfers between devices: 9.31 us -> 2.26 us
  starting transfers between devices: 54.6 us -> 52.2 us
  local copies, waits for them, and re-layouts: 2.3 us -> 0 us
  Pallas kernels: 19.6 us -> 17.7 us
    ppermute x10, waiting for transfers between devices: 9.31 us -> 2.26 us  [permuted(): lax.ppermute(value, 'blk', [(i, target(i) % count) for i in range(count)])]
    ppermute x10, starting transfers between devices: 54.6 us -> 52.2 us  [permuted(): lax.ppermute(value, 'blk', [(i, target(i) % count) for i in range(count)])]
    unnamed x8 -> x0, local copies, waits for them, and re-layouts: 2.3 us -> none
    pallas_call x6 -> x7, Pallas kernels: 19.6 us -> 17.7 us  [call(): pl.pallas_call(kernel, out_shape=[jax.ShapeDtypeStruct(shape, dtype) for...]
  transfers between devices with their start and end apart: 10 -> 10, of which waited for: 1 -> 1; matrix products, arithmetic and copies ran while one was open for 0% -> 0% of each run, Pallas kernels for 20% -> 22%
where the time goes in v2:
time: 73.4 us; the launch traced here: 73 us
  starting transfers between devices  52.2 us (71%)
  Pallas kernels  17.7 us (24%)
  waiting for transfers between devices  2.26 us (3%)
  between operations  0.81 us (1%)
    ppermute x10, starting transfers between devices, permuted(): lax.ppermute(value, 'blk', [(i, target(i) % count) for i in range(count)])  52.2 us
    pallas_call x7, Pallas kernels, call(): pl.pallas_call(kernel, out_shape=[jax.ShapeDtypeStruct(shape, dtype) for...  17.7 us
    ppermute x10, waiting for transfers between devices, permuted(): lax.ppermute(value, 'blk', [(i, target(i) % count) for i in range(count)])  2.26 us
  transfers between devices with their start and end apart: 10, of which 1 were waited for; matrix products, arithmetic and copies ran while one was open for 0% of the time, Pallas kernels for 22%

profile of v2, /device:TPU:1, one launch (start us, length us, event | category | flops | bytes accessed | tf_op | source)
XLA Modules:
  0.0 73.0 jit_solution(16618228518925039057)
XLA Ops:
  0.6 4.8 %collective-permute-start = (f32[256,768]{1,0:T(8,128)}, f32[256,768]{1,0:T(8,128)S(1)}, u32[]{:S(2)}, u32[]{:S(2)}) collective-permute-start(f32[256,768]{1,0:T(8,128)} %t_hbm.1), channel_id=1, source_target_pairs={{0,510},{1,3},{2,0},{3,5},{4,2},{5,7},{6,4},{7,9},{8,6},{9,11},{10... | collective-permute-start | bytes 2359304 | tf_op jit(solution)/shard_map/ppermute | solution.py:22
  5.5 13.7 %collective-permute-start.4 = (f32[256,768]{1,0:T(8,128)}, f32[256,768]{1,0:T(8,128)S(1)}, u32[]{:S(2)}, u32[]{:S(2)}) collective-permute-start(f32[256,768]{1,0:T(8,128)} %t_hbm.1), channel_id=1, source_target_pairs={{0,2},{1,511},{2,4},{3,1},{4,6},{5,3},{6,8},{7,5},{8,10},{9,7},{10... | collective-permute-start | bytes 2359304 | tf_op jit(solution)/shard_map/ppermute | solution.py:22
  19.2 4.3 %shard_map.49 = (f32[256,768]{1,0:T(8,128)S(1)}, f32[8,256]{1,0:T(8,128)S(1)}, bf16[256,768]{1,0:T(8,128)(2,1)S(1)}, bf16[256,768]{1,0:T(8,128)(2,1)S(1)}, f32[2...) custom-call(f32[256,768]{1,0:T(8,128)} %i_hbm.1, f32[256,768]{1,0:T(8,128)} %t_hbm.1), custom_call_target="tpu_custom_call" | custom-call | flops 1000 | bytes 1000 | tf_op jit(solution)/shard_map/pallas_call | solution.py:175
  23.5 1.9 %collective-permute-start.5 = (f32[256,768]{1,0:T(8,128)}, f32[256,768]{1,0:T(8,128)S(1)}, u32[]{:S(2)}, u32[]{:S(2)}) collective-permute-start(f32[256,768]{1,0:T(8,128)} %i_hbm.1), channel_id=1, source_target_pairs={{0,510},{1,3},{2,0},{3,5},{4,2},{5,7},{6,4},{7,9},{8,6},{9,11},{10... | collective-permute-start | bytes 2359304 | tf_op jit(solution)/shard_map/ppermute | solution.py:22
  25.4 10.3 %collective-permute-start.2 = (f32[256,768]{1,0:T(8,128)}, f32[256,768]{1,0:T(8,128)S(1)}, u32[]{:S(2)}, u32[]{:S(2)}) collective-permute-start(f32[256,768]{1,0:T(8,128)} %i_hbm.1), channel_id=1, source_target_pairs={{0,1},{1,0},{2,3},{3,2},{4,5},{5,4},{6,7},{7,6},{8,9},{9,8},{10,11... | collective-permute-start | bytes 2359304 | tf_op jit(solution)/shard_map/ppermute | solution.py:22
  35.7 1.9 %collective-permute-start.3 = (f32[256,768]{1,0:T(8,128)}, f32[256,768]{1,0:T(8,128)S(1)}, u32[]{:S(2)}, u32[]{:S(2)}) collective-permute-start(f32[256,768]{1,0:T(8,128)} %t_hbm.1), channel_id=1, source_target_pairs={{0,1},{1,0},{2,3},{3,2},{4,5},{5,4},{6,7},{7,6},{8,9},{9,8},{10,11... | collective-permute-start | bytes 2359304 | tf_op jit(solution)/shard_map/ppermute | solution.py:22
  37.7 0.0 collective-permute-done.in_ref
  37.7 1.9 %collective-permute-start.6 = (f32[256,768]{1,0:T(8,128)}, f32[256,768]{1,0:T(8,128)S(1)}, u32[]{:S(2)}, u32[]{:S(2)}) collective-permute-start(f32[256,768]{1,0:T(8,128)} %i_hbm.1), channel_id=1, source_target_pairs={{0,2},{1,511},{2,4},{3,1},{4,6},{5,3},{6,8},{7,5},{8,10},{9,7},{10... | collective-permute-start | bytes 2359304 | tf_op jit(solution)/shard_map/ppermute | solution.py:22
  39.6 0.0 collective-permute-done.4.out_ref
  39.6 1.9 %collective-permute-start.1 = (f32[256,768]{1,0:T(8,128)S(1)}, f32[256,768]{1,0:T(8,128)S(1)}, u32[]{:S(2)}, u32[]{:S(2)}) collective-permute-start(f32[256,768]{1,0:T(8,128)S(1)} %collective-permute-done.in_ref), channel_id=1, source_target_pairs={{0,511},{1,2},{2,1},{3,4},{4,3},{5,6},{6,5},{7,8},{8,7},{9,10},{10... | collective-permute-start | bytes 2359304 | tf_op jit(solution)/shard_map/ppermute | solution.py:22
  41.5 1.7 %shard_map.50 = (f32[256,768]{1,0:T(8,128)S(1)}, f32[8,256]{1,0:T(8,128)S(1)}) custom-call(bf16[256,768]{1,0:T(8,128)(2,1)S(1)} %get-tuple-element.29.high_ref.i_high_ref, bf16[256,768]{1,0:T(8,128)(2,1)S(1)} %get-tuple-element.30.low_ref.i_low_ref, f32[256,768]{1,0:T(8,128)S(1)} %collective-permute-done.in_ref, ...), custom_call_target="tpu_custom_call" | custom-call | flops 1000 | bytes 1000 | tf_op jit(solution)/shard_map/pallas_call | solution.py:175
  43.2 2.2 %collective-permute-done.5.in_ref = f32[256,768]{1,0:T(8,128)S(1)} collective-permute-done((f32[256,768]{1,0:T(8,128)}, f32[256,768]{1,0:T(8,128)S(1)}, u32[]{:S(2)}, u32[]{:S(2)}) %collective-permute-start.5) | collective-permute-done | bytes 786464 | tf_op jit(solution)/shard_map/ppermute | solution.py:22
  45.5 1.9 %collective-permute-start.8 = (f32[256,768]{1,0:T(8,128)S(1)}, f32[256,768]{1,0:T(8,128)S(1)}, u32[]{:S(2)}, u32[]{:S(2)}) collective-permute-start(f32[256,768]{1,0:T(8,128)S(1)} %collective-permute-done.5.in_ref), channel_id=1, source_target_pairs={{0,511},{1,2},{2,1},{3,4},{4,3},{5,6},{6,5},{7,8},{8,7},{9,10},{10... | collective-permute-start | bytes 2359304 | tf_op jit(solution)/shard_map/ppermute | solution.py:22
  47.4 0.0 collective-permute-done.2.i_sib_ref
  47.4 0.0 collective-permute-done.3.t_sib_ref
  47.4 4.5 %shard_map.51 = (f32[256,768]{1,0:T(8,128)S(1)}, f32[264,768]{1,0:T(8,128)S(1)}, f32[8,256]{1,0:T(8,128)S(1)}, f32[256,768]{1,0:T(8,128)S(1)}, bf16[512,768]{1,0...) custom-call(f32[256,768]{1,0:T(8,128)S(1)} %collective-permute-done.2.i_sib_ref, ...), custom_call_target="tpu_custom_call" | custom-call | flops 1000 | bytes 1000 | tf_op jit(solution)/shard_map/pallas_call | solution.py:175
  51.9 8.4 %collective-permute-start.7 = (f32[264,768]{1,0:T(8,128)S(1)}, f32[264,768]{1,0:T(8,128)S(1)}, u32[]{:S(2)}, u32[]{:S(2)}) collective-permute-start(f32[264,768]{1,0:T(8,128)S(1)} %get-tuple-element.47), channel_id=1, source_target_pairs={{0,1},{1,0},{2,3},{3,2},{4,5},{5,4},{6,7},{7,6},{8,9},{9,8},{10,11... | collective-permute-start | bytes 2433032 | tf_op jit(solution)/shard_map/ppermute | solution.py:22
  60.3 0.0 collective-permute-done.6.out_ref
  60.4 2.8 %shard_map.52 = (f32[256,768]{1,0:T(8,128)S(1)}, f32[256,768]{1,0:T(8,128)S(1)}) custom-call(bf16[512,768]{1,0:T(8,128)(2,1)S(1)} %get-tuple-element.39.high_ref, bf16[512,768]{1,0:T(8,128)(2,1)S(1)} %get-tuple-element.40.low_ref, f32[256,768]{1,0:T(8,128)S(1)} %collective-permute-done.5.in_ref, f32[256,768]{1,0:T(8,128)S(1)} %collective-permute-done.6.out_ref, ...), custom_call_target="tpu_custom_call" | custom-call | flops 1000 | bytes 1000 | tf_op jit(solution)/shard_map/pallas_call | solution.py:175
  63.1 5.3 %collective-permute-start.9 = (f32[256,768]{1,0:T(8,128)S(1)}, f32[256,768]{1,0:T(8,128)S(1)}, u32[]{:S(2)}, u32[]{:S(2)}) collective-permute-start(f32[256,768]{1,0:T(8,128)S(1)} %get-tuple-element.51), channel_id=1, source_target_pairs={{0,1},{1,0},{2,3},{3,2},{4,5},{5,4},{6,7},{7,6},{8,9},{9,8},{10,11... | collective-permute-start | bytes 2359304 | tf_op jit(solution)/shard_map/ppermute | solution.py:22
  68.5 0.0 collective-permute-done.1.block_ref
  68.5 1.6 %shard_map.53 = (f32[256,768]{1,0:T(8,128)S(1)}, f32[8,256]{1,0:T(8,128)S(1)}) custom-call(bf16[256,768]{1,0:T(8,128)(2,1)S(1)} %get-tuple-element.29.high_ref.i_high_ref, bf16[256,768]{1,0:T(8,128)(2,1)S(1)} %get-tuple-element.30.low_ref.i_low_ref, f32[256,768]{1,0:T(8,128)S(1)} %collective-permute-done.1.block_ref, ...), custom_call_target="tpu_custom_call" | custom-call | flops 2000000000 | bytes 1000 | tf_op jit(solution)/shard_map/pallas_call | solution.py:175
  70.1 0.0 collective-permute-done.8.block_ref
  70.1 1.5 %shard_map.54.t_mine = f32[256,768]{1,0:T(8,128)S(1)} custom-call(bf16[512,768]{1,0:T(8,128)(2,1)S(1)} %get-tuple-element.39.high_ref, bf16[512,768]{1,0:T(8,128)(2,1)S(1)} %get-tuple-element.40.low_ref, f32[256,768]{1,0:T(8,128)S(1)} %collective-permute-done.8.block_ref, f32[256,768]{1,0:T(8,128)S(1)} %get-tuple-element.50.given_ref), custom_call_target="tpu_custom_call" | custom-call | flops 2000000000 | bytes 1000 | tf_op jit(solution)/shard_map/pallas_call | solution.py:175
  71.6 0.0 collective-permute-done.9.t_theirs
  71.6 0.0 collective-permute-done.7.i_theirs
  71.6 1.3 %shard_map.55 = (f32[256,768]{1,0:T(8,128)}, f32[256,768]{1,0:T(8,128)}, f32[1,256]{1,0:T(1,128)}) custom-call(f32[256,768]{1,0:T(8,128)S(1)} %get-tuple-element.46.i_mine, f32[264,768]{1,0:T(8,128)S(1)} %collective-permute-done.7.i_theirs, f32[8,256]{1,0:T(8,128)S(1)} %get-tuple-element.48.l_mine, f32[256,768]{1,0:T(8,128)S(1)} %shard_map.54.t_mine, ...), custom_call_target="tpu_custom_call" | custom-call | flops 1000 | bytes 1000 | tf_op jit(solution)/shard_map/pallas_call | solution.py:175
Async XLA Ops:
  0.6 37.0 %collective-permute-start = (f32[256,768]{1,0:T(8,128)}, f32[256,768]{1,0:T(8,128)S(1)}, u32[]{:S(2)}, u32[]{:S(2)}) collective-permute-start(f32[256,768]{1,0:T(8,128)} %t_hbm.1), channel_id=1, source_target_pairs={{0,510},{1,3},{2,0},{3,5},{4,2},{5,7},{6,4},{7,9},{8,6},{9,11},{10... | collective-permute-start | bytes 2359304 | tf_op jit(solution)/shard_map/ppermute | solution.py:22
  5.5 34.1 %collective-permute-start.4 = (f32[256,768]{1,0:T(8,128)}, f32[256,768]{1,0:T(8,128)S(1)}, u32[]{:S(2)}, u32[]{:S(2)}) collective-permute-start(f32[256,768]{1,0:T(8,128)} %t_hbm.1), channel_id=1, source_target_pairs={{0,2},{1,511},{2,4},{3,1},{4,6},{5,3},{6,8},{7,5},{8,10},{9,7},{10... | collective-permute-start | bytes 2359304 | tf_op jit(solution)/shard_map/ppermute | solution.py:22
  23.5 22.0 %collective-permute-start.5 = (f32[256,768]{1,0:T(8,128)}, f32[256,768]{1,0:T(8,128)S(1)}, u32[]{:S(2)}, u32[]{:S(2)}) collective-permute-start(f32[256,768]{1,0:T(8,128)} %i_hbm.1), channel_id=1, source_target_pairs={{0,510},{1,3},{2,0},{3,5},{4,2},{5,7},{6,4},{7,9},{8,6},{9,11},{10... | collective-permute-start | bytes 2359304 | tf_op jit(solution)/shard_map/ppermute | solution.py:22
  25.4 21.9 %collective-permute-start.2 = (f32[256,768]{1,0:T(8,128)}, f32[256,768]{1,0:T(8,128)S(1)}, u32[]{:S(2)}, u32[]{:S(2)}) collective-permute-start(f32[256,768]{1,0:T(8,128)} %i_hbm.1), channel_id=1, source_target_pairs={{0,1},{1,0},{2,3},{3,2},{4,5},{5,4},{6,7},{7,6},{8,9},{9,8},{10,11... | collective-permute-start | bytes 2359304 | tf_op jit(solution)/shard_map/ppermute | solution.py:22
  35.7 11.7 %collective-permute-start.3 = (f32[256,768]{1,0:T(8,128)}, f32[256,768]{1,0:T(8,128)S(1)}, u32[]{:S(2)}, u32[]{:S(2)}) collective-permute-start(f32[256,768]{1,0:T(8,128)} %t_hbm.1), channel_id=1, source_target_pairs={{0,1},{1,0},{2,3},{3,2},{4,5},{5,4},{6,7},{7,6},{8,9},{9,8},{10,11... | collective-permute-start | bytes 2359304 | tf_op jit(solution)/shard_map/ppermute | solution.py:22
  37.7 22.7 %collective-permute-start.6 = (f32[256,768]{1,0:T(8,128)}, f32[256,768]{1,0:T(8,128)S(1)}, u32[]{:S(2)}, u32[]{:S(2)}) collective-permute-start(f32[256,768]{1,0:T(8,128)} %i_hbm.1), channel_id=1, source_target_pairs={{0,2},{1,511},{2,4},{3,1},{4,6},{5,3},{6,8},{7,5},{8,10},{9,7},{10... | collective-permute-start | bytes 2359304 | tf_op jit(solution)/shard_map/ppermute | solution.py:22
  39.6 28.9 %collective-permute-start.1 = (f32[256,768]{1,0:T(8,128)S(1)}, f32[256,768]{1,0:T(8,128)S(1)}, u32[]{:S(2)}, u32[]{:S(2)}) collective-permute-start(f32[256,768]{1,0:T(8,128)S(1)} %collective-permute-done.in_ref), channel_id=1, source_target_pairs={{0,511},{1,2},{2,1},{3,4},{4,3},{5,6},{6,5},{7,8},{8,7},{9,10},{10... | collective-permute-start | bytes 2359304 | tf_op jit(solution)/shard_map/ppermute | solution.py:22
  45.5 24.6 %collective-permute-start.8 = (f32[256,768]{1,0:T(8,128)S(1)}, f32[256,768]{1,0:T(8,128)S(1)}, u32[]{:S(2)}, u32[]{:S(2)}) collective-permute-start(f32[256,768]{1,0:T(8,128)S(1)} %collective-permute-done.5.in_ref), channel_id=1, source_target_pairs={{0,511},{1,2},{2,1},{3,4},{4,3},{5,6},{6,5},{7,8},{8,7},{9,10},{10... | collective-permute-start | bytes 2359304 | tf_op jit(solution)/shard_map/ppermute | solution.py:22
  51.9 19.7 %collective-permute-start.7 = (f32[264,768]{1,0:T(8,128)S(1)}, f32[264,768]{1,0:T(8,128)S(1)}, u32[]{:S(2)}, u32[]{:S(2)}) collective-permute-start(f32[264,768]{1,0:T(8,128)S(1)} %get-tuple-element.47), channel_id=1, source_target_pairs={{0,1},{1,0},{2,3},{3,2},{4,5},{5,4},{6,7},{7,6},{8,9},{9,8},{10,11... | collective-permute-start | bytes 2433032 | tf_op jit(solution)/shard_map/ppermute | solution.py:22
  63.1 8.5 %collective-permute-start.9 = (f32[256,768]{1,0:T(8,128)S(1)}, f32[256,768]{1,0:T(8,128)S(1)}, u32[]{:S(2)}, u32[]{:S(2)}) collective-permute-start(f32[256,768]{1,0:T(8,128)S(1)} %get-tuple-element.51), channel_id=1, source_target_pairs={{0,1},{1,0},{2,3},{3,2},{4,5},{5,4},{6,7},{7,6},{8,9},{9,8},{10,11... | collective-permute-start | bytes 2359304 | tf_op jit(solution)/shard_map/ppermute | solution.py:22

commit v3 on v2

--- a/solution.py
+++ b/solution.py
@@ -86,7 +86,7 @@
 
 
 def own_kernel(
-    i_hbm, t_hbm, i_mine_ref, l_mine_ref, i_high_ref, i_low_ref, t_mine_ref, t_high_ref, t_low_ref, i_ref, t_ref, sems
+    i_hbm, t_hbm, first_ref, second_ref, i_mine_ref, l_mine_ref, i_high_ref, i_low_ref, t_mine_ref, t_high_ref, t_low_ref, i_ref, t_ref, sems
 ):
     copies = [
         pltpu.make_async_copy(source, target, sems.at[k])
@@ -96,6 +96,8 @@
         copy.start()
     for copy in copies:
         copy.wait()
+    middle = first_ref.shape[0]
+    first_ref[...], second_ref[...] = t_ref[:middle, :], t_ref[middle:, :]
     own, texts = halves(i_ref[...]), halves(t_ref[...])
     i_high_ref[...], i_low_ref[...] = own
     t_high_ref[...], t_low_ref[...] = texts
@@ -106,39 +108,41 @@
     t_mine_ref[...] = weighted(None, coefs, own)
 
 
-def texts_kernel(high_ref, low_ref, in_ref, out_ref, given_ref, l_given, mine_ref, l_mine_ref):
-    own = high_ref[...], low_ref[...]
+def texts_kernel(
+    i_high_ref, i_low_ref, t_high_ref, t_low_ref, i_sib_ref, in_ref, out_ref, i_given, l_given, t_given,
+    i_mine_ref, l_mine_ref, t_mine_ref, high_ref, low_ref,
+):
+    own, texts, images = (i_high_ref[...], i_low_ref[...]), (t_high_ref[...], t_low_ref[...]), halves(i_sib_ref[...])
+    high_ref[...], low_ref[...] = images
     blocks = [halves(in_ref[...]), halves(out_ref[...])]
     found = [terms(own, block, False, True) for block in blocks]
-    mine = given_ref[...]
+    coefs, _ = terms(texts, images)
+    t_mine_ref[...] = weighted(t_given[...], coefs, images)
+    mine = i_given[...]
     for (coefs, _), block in zip(found, blocks):
         mine = weighted(mine, coefs, block)
-    mine_ref[...] = mine
+    i_mine_ref[...] = mine
     l_mine_ref[...] = l_given[...] + as_row(found[0][1] + found[1][1])
 
 
 def pair_kernel(
-    i_sib_ref, t_sib_ref, in_ref, out_ref, i_high_ref, i_low_ref, t_high_ref, t_low_ref, i_given, l_given, t_given,
-    i_mine_ref, theirs_ref, l_mine_ref, t_mine_ref, high_ref, low_ref,
+    i_sib_high, i_sib_low, t_sib_first, t_sib_second, in_ref, out_ref, i_high_ref, i_low_ref, t_high_ref, t_low_ref, i_given, l_given,
+    i_mine_ref, theirs_ref, l_mine_ref, high_ref, low_ref,
 ):
-    rows = i_sib_ref.shape[0]
-    images, texts = halves(i_sib_ref[...]), halves(t_sib_ref[...])
-    own_texts = t_high_ref[...], t_low_ref[...]
-    high_ref[:rows, :], low_ref[:rows, :] = own_texts
+    rows = in_ref.shape[0]
+    images, texts = (i_sib_high[...], i_sib_low[...]), halves(jnp.concatenate([t_sib_first[...], t_sib_second[...]]))
+    high_ref[:rows, :], low_ref[:rows, :] = t_high_ref[...], t_low_ref[...]
     high_ref[rows:, :], low_ref[rows:, :] = texts
+    blocks = [halves(in_ref[...]), halves(out_ref[...])]
     coefs, lost = terms((i_high_ref[...], i_low_ref[...]), texts, False, True)
+    found = [terms(images, block, False, True) for block in blocks]
     i_mine_ref[...] = weighted(i_given[...], coefs, texts)
     l_mine_ref[...] = l_given[...] + as_row(lost)
-    coefs, _ = terms(own_texts, images)
-    t_mine_ref[...] = weighted(t_given[...], coefs, images)
-    theirs, lost = None, 0.0
-    for ref in (in_ref, out_ref):
-        block = halves(ref[...])
-        coefs, each = terms(images, block, False, True)
+    theirs = None
+    for (coefs, _), block in zip(found, blocks):
         theirs = weighted(theirs, coefs, block)
-        lost = lost + each
     theirs_ref[:rows, :] = theirs
-    theirs_ref[rows:, :rows] = jnp.broadcast_to(as_row(lost), (EXTRA, rows))
+    theirs_ref[rows:, :rows] = jnp.broadcast_to(as_row(found[0][1] + found[1][1]), (EXTRA, rows))
 
 
 def images_kernel(high_ref, low_ref, in_ref, out_ref, given_ref, mine_ref, theirs_ref):
@@ -185,13 +189,14 @@
     rows, width = images.shape
     f32, bf16 = jnp.float32, jnp.bfloat16
     grad, longer = ((rows, width), f32), ((rows + EXTRA, width), f32)
+    half = ((rows // 2, width), f32)
     low, low2, loss = ((rows, width), bf16), ((2 * rows, width), bf16), ((EXTRA, rows), f32)
 
     t_in, t_out = inward(texts), outward(texts)
-    t_sib, i_sib = sibling(texts), sibling(images)
-    i_mine, l_mine, i_high, i_low, t_mine, t_high, t_low = call(
+    i_sib = sibling(images)
+    *t_parts, i_mine, l_mine, i_high, i_low, t_mine, t_high, t_low = call(
         own_kernel,
-        (grad, loss, low, low, grad, low, low),
+        (half, half, grad, loss, low, low, grad, low, low),
         images,
         texts,
         in_specs=[pl.BlockSpec(memory_space=pl.ANY)] * 2,
@@ -199,12 +204,17 @@
     )
     i_in, i_out = inward(after(images, t_mine)), outward(images)
     t_far = across(t_in)
-    i_mine, l_mine = call(texts_kernel, (grad, loss), i_high, i_low, t_in, t_out, i_mine, l_mine)
+    i_mine, l_mine, t_mine, i_sib_high, i_sib_low = call(
+        texts_kernel,
+        (grad, loss, grad, low, low),
+        i_high, i_low, t_high, t_low, i_sib, t_in, t_out, i_mine, l_mine, t_mine,
+    )
     i_far = across(after(i_in, l_mine))
-    i_mine, i_theirs, l_mine, t_mine, t_high, t_low = call(
+    t_sib = [sibling(after(part, l_mine)) for part in t_parts]
+    i_mine, i_theirs, l_mine, t_high, t_low = call(
         pair_kernel,
-        (grad, longer, loss, grad, low2, low2),
-        i_sib, t_sib, t_in, t_out, i_high, i_low, t_high, t_low, i_mine, l_mine, t_mine,
+        (grad, longer, loss, low2, low2),
+        i_sib_high, i_sib_low, *t_sib, t_in, t_out, i_high, i_low, t_high, t_low, i_mine, l_mine,
     )
     i_theirs = sibling(i_theirs)
     t_mine, t_theirs = call(images_kernel, (grad, grad), t_high, t_low, i_in, i_out, t_mine)

time: 73.4 us -> 70.6 us (0.962)
  waiting for transfers between devices: 2.26 us -> 0.06 us
  Pallas kernels: 17.7 us -> 16.3 us
  local copies, waits for them, and re-layouts: 0 us -> 1.13 us
    ppermute x10 -> x11, waiting for transfers between devices: 2.26 us -> 0.06 us  [permuted(): lax.ppermute(value, 'blk', [(i, target(i) % count) for i in range(count)])]
    pallas_call x7, Pallas kernels: 17.7 us -> 16.3 us  [call(): pl.pallas_call(kernel, out_shape=[jax.ShapeDtypeStruct(shape, dtype) for...]
    unnamed x0 -> x2, local copies, waits for them, and re-layouts: none -> 1.13 us
    ppermute x10 -> x11, starting transfers between devices: 52.2 us -> 51.8 us  [permuted(): lax.ppermute(value, 'blk', [(i, target(i) % count) for i in range(count)])]
  transfers between devices with their start and end apart: 10 -> 11, of which waited for: 1 -> 0; matrix products, arithmetic and copies ran while one was open for 0% -> 0% of each run, Pallas kernels for 22% -> 21%
where the time goes in v3:
time: 70.6 us; the launch traced here: 70.1 us
  starting transfers between devices  51.8 us (73%)
  Pallas kernels  16.3 us (23%)
  local copies, waits for them, and re-layouts  1.13 us (2%)
  between operations  0.84 us (1%)
    ppermute x11, starting transfers between devices, permuted(): lax.ppermute(value, 'blk', [(i, target(i) % count) for i in range(count)])  51.8 us
    pallas_call x7, Pallas kernels, call(): pl.pallas_call(kernel, out_shape=[jax.ShapeDtypeStruct(shape, dtype) for...  16.3 us
  transfers between devices with their start and end apart: 11, of which 0 were waited for; matrix products, arithmetic and copies ran while one was open for 0% of the time, Pallas kernels for 21%

profile of v3, /device:TPU:1, one launch (start us, length us, event | category | flops | bytes accessed | tf_op | source)
XLA Modules:
  0.0 70.1 jit_solution(5376686593263150268)
XLA Ops:
  0.6 4.8 %collective-permute-start = (f32[256,768]{1,0:T(8,128)}, f32[256,768]{1,0:T(8,128)S(1)}, u32[]{:S(2)}, u32[]{:S(2)}) collective-permute-start(f32[256,768]{1,0:T(8,128)} %t_hbm.1), channel_id=1, source_target_pairs={{0,510},{1,3},{2,0},{3,5},{4,2},{5,7},{6,4},{7,9},{8,6},{9,11},{10... | collective-permute-start | bytes 2359304 | tf_op jit(solution)/shard_map/ppermute | solution.py:22
  5.5 13.7 %collective-permute-start.3 = (f32[256,768]{1,0:T(8,128)}, f32[256,768]{1,0:T(8,128)S(1)}, u32[]{:S(2)}, u32[]{:S(2)}) collective-permute-start(f32[256,768]{1,0:T(8,128)} %t_hbm.1), channel_id=1, source_target_pairs={{0,2},{1,511},{2,4},{3,1},{4,6},{5,3},{6,8},{7,5},{8,10},{9,7},{10... | collective-permute-start | bytes 2359304 | tf_op jit(solution)/shard_map/ppermute | solution.py:22
  19.2 2.9 %collective-permute-start.2 = (f32[256,768]{1,0:T(8,128)}, f32[256,768]{1,0:T(8,128)S(1)}, u32[]{:S(2)}, u32[]{:S(2)}) collective-permute-start(f32[256,768]{1,0:T(8,128)} %i_hbm.1), channel_id=1, source_target_pairs={{0,1},{1,0},{2,3},{3,2},{4,5},{5,4},{6,7},{7,6},{8,9},{9,8},{10,11... | collective-permute-start | bytes 2359304 | tf_op jit(solution)/shard_map/ppermute | solution.py:22
  22.0 0.0 copy-start
  22.0 1.1 %copy-done = f32[256,768]{1,0:T(8,128)S(1)} copy-done((f32[256,768]{1,0:T(8,128)S(1)}, f32[256,768]{1,0:T(8,128)}, u32[]{:S(2)}) %copy-start) | copy-done | bytes 786456
  23.2 4.1 %shard_map.49 = (f32[128,768]{1,0:T(8,128)S(1)}, f32[128,768]{1,0:T(8,128)S(1)}, f32[256,768]{1,0:T(8,128)S(1)}, f32[8,256]{1,0:T(8,128)S(1)}, bf16[256,768]{1,0...) custom-call(f32[256,768]{1,0:T(8,128)} %i_hbm.1, ...), custom_call_target="tpu_custom_call" | custom-call | flops 1000 | bytes 1000 | tf_op jit(solution)/shard_map/pallas_call | solution.py:179
  27.3 1.9 %collective-permute-start.6 = (f32[256,768]{1,0:T(8,128)}, f32[256,768]{1,0:T(8,128)S(1)}, u32[]{:S(2)}, u32[]{:S(2)}) collective-permute-start(f32[256,768]{1,0:T(8,128)} %i_hbm.1), channel_id=1, source_target_pairs={{0,510},{1,3},{2,0},{3,5},{4,2},{5,7},{6,4},{7,9},{8,6},{9,11},{10... | collective-permute-start | bytes 2359304 | tf_op jit(solution)/shard_map/ppermute | solution.py:22
  29.2 9.1 %collective-permute-start.7 = (f32[256,768]{1,0:T(8,128)}, f32[256,768]{1,0:T(8,128)S(1)}, u32[]{:S(2)}, u32[]{:S(2)}) collective-permute-start(f32[256,768]{1,0:T(8,128)} %i_hbm.1), channel_id=1, source_target_pairs={{0,2},{1,511},{2,4},{3,1},{4,6},{5,3},{6,8},{7,5},{8,10},{9,7},{10... | collective-permute-start | bytes 2359304 | tf_op jit(solution)/shard_map/ppermute | solution.py:22
  38.3 0.0 collective-permute-done.in_ref
  38.3 0.0 collective-permute-done.3.out_ref
  38.3 0.0 collective-permute-done.2.i_sib_ref
  38.4 2.5 %shard_map.50 = (f32[256,768]{1,0:T(8,128)S(1)}, f32[8,256]{1,0:T(8,128)S(1)}, f32[256,768]{1,0:T(8,128)S(1)}, bf16[256,768]{1,0:T(8,128)(2,1)S(1)}, bf16[256,768]{1,0:T(8,128)(2,1)S(1)}) custom-call(bf16[256,768]{1,0:T(8,128)(2,1)S(1)} %get-tuple-element.35.i_high_ref.high_ref, bf16[256,768]{1,0:T(8,128)(2,1)S(1)} %get-tuple-element.36.i_low_ref.low_ref, ...), custom_call_target="tpu_custom_call" | custom-call | flops 1000 | bytes 1000 | tf_op jit(solution)/shard_map/pallas_call | solution.py:179
  40.9 2.2 %collective-permute-start.5 = (f32[128,768]{1,0:T(8,128)S(1)}, f32[128,768]{1,0:T(8,128)S(1)}, u32[]{:S(2)}, u32[]{:S(2)}) collective-permute-start(f32[128,768]{1,0:T(8,128)S(1)} %get-tuple-element.48), channel_id=1, source_target_pairs={{0,1},{1,0},{2,3},{3,2},{4,5},{5,4},{6,7},{7,6},{8,9},{9,8},{10,11... | collective-permute-start | bytes 1179656 | tf_op jit(solution)/shard_map/ppermute | solution.py:22
  43.1 2.1 %collective-permute-start.4 = (f32[128,768]{1,0:T(8,128)S(1)}, f32[128,768]{1,0:T(8,128)S(1)}, u32[]{:S(2)}, u32[]{:S(2)}) collective-permute-start(f32[128,768]{1,0:T(8,128)S(1)} %get-tuple-element.46), channel_id=1, source_target_pairs={{0,1},{1,0},{2,3},{3,2},{4,5},{5,4},{6,7},{7,6},{8,9},{9,8},{10,11... | collective-permute-start | bytes 1179656 | tf_op jit(solution)/shard_map/ppermute | solution.py:22
  45.2 1.9 %collective-permute-start.1 = (f32[256,768]{1,0:T(8,128)S(1)}, f32[256,768]{1,0:T(8,128)S(1)}, u32[]{:S(2)}, u32[]{:S(2)}) collective-permute-start(f32[256,768]{1,0:T(8,128)S(1)} %collective-permute-done.in_ref), channel_id=1, source_target_pairs={{0,511},{1,2},{2,1},{3,4},{4,3},{5,6},{6,5},{7,8},{8,7},{9,10},{10... | collective-permute-start | bytes 2359304 | tf_op jit(solution)/shard_map/ppermute | solution.py:22
  47.2 0.0 collective-permute-done.6.in_ref
  47.2 3.6 %collective-permute-start.9 = (f32[256,768]{1,0:T(8,128)S(1)}, f32[256,768]{1,0:T(8,128)S(1)}, u32[]{:S(2)}, u32[]{:S(2)}) collective-permute-start(f32[256,768]{1,0:T(8,128)S(1)} %collective-permute-done.6.in_ref), channel_id=1, source_target_pairs={{0,511},{1,2},{2,1},{3,4},{4,3},{5,6},{6,5},{7,8},{8,7},{9,10},{10... | collective-permute-start | bytes 2359304 | tf_op jit(solution)/shard_map/ppermute | solution.py:22
  50.8 0.0 collective-permute-done.5.t_sib_second
  50.8 0.0 collective-permute-done.4.t_sib_first
  50.8 2.4 %shard_map.51 = (f32[256,768]{1,0:T(8,128)S(1)}, f32[264,768]{1,0:T(8,128)S(1)}, f32[8,256]{1,0:T(8,128)S(1)}, bf16[512,768]{1,0:T(8,128)(2,1)S(1)}, bf16[512,768]{1,0:T(8,128)(2,1)S(1)}) custom-call(bf16[256,768]{1,0:T(8,128)(2,1)S(1)} %get-tuple-element.42.i_sib_high, bf16[256,768]{1,0:T(8,128)(2,1)S(1)} %get-tuple-element.43.i_sib_low, ...), custom_call_target="tpu_custom_call" | custom-call | flops 1000 | bytes 1000 | tf_op jit(solution)/shard_map/pallas_call | solution.py:179
  53.3 7.6 %collective-permute-start.8 = (f32[264,768]{1,0:T(8,128)S(1)}, f32[264,768]{1,0:T(8,128)S(1)}, u32[]{:S(2)}, u32[]{:S(2)}) collective-permute-start(f32[264,768]{1,0:T(8,128)S(1)} %get-tuple-element.59), channel_id=1, source_target_pairs={{0,1},{1,0},{2,3},{3,2},{4,5},{5,4},{6,7},{7,6},{8,9},{9,8},{10,11... | collective-permute-start | bytes 2433032 | tf_op jit(solution)/shard_map/ppermute | solution.py:22
  60.9 0.0 collective-permute-done.7.out_ref
  60.9 2.8 %shard_map.52 = (f32[256,768]{1,0:T(8,128)S(1)}, f32[256,768]{1,0:T(8,128)S(1)}) custom-call(bf16[512,768]{1,0:T(8,128)(2,1)S(1)} %get-tuple-element.51.high_ref, bf16[512,768]{1,0:T(8,128)(2,1)S(1)} %get-tuple-element.52.low_ref, f32[256,768]{1,0:T(8,128)S(1)} %collective-permute-done.6.in_ref, f32[256,768]{1,0:T(8,128)S(1)} %collective-permute-done.7.out_ref, ...), custom_call_target="tpu_custom_call" | custom-call | flops 1000 | bytes 1000 | tf_op jit(solution)/shard_map/pallas_call | solution.py:179
  63.7 1.9 %collective-permute-start.10 = (f32[256,768]{1,0:T(8,128)S(1)}, f32[256,768]{1,0:T(8,128)S(1)}, u32[]{:S(2)}, u32[]{:S(2)}) collective-permute-start(f32[256,768]{1,0:T(8,128)S(1)} %get-tuple-element.63), channel_id=1, source_target_pairs={{0,1},{1,0},{2,3},{3,2},{4,5},{5,4},{6,7},{7,6},{8,9},{9,8},{10,11... | collective-permute-start | bytes 2359304 | tf_op jit(solution)/shard_map/ppermute | solution.py:22
  65.6 0.0 collective-permute-done.1.block_ref
  65.6 1.6 %shard_map.53 = (f32[256,768]{1,0:T(8,128)S(1)}, f32[8,256]{1,0:T(8,128)S(1)}) custom-call(bf16[256,768]{1,0:T(8,128)(2,1)S(1)} %get-tuple-element.35.i_high_ref.high_ref, bf16[256,768]{1,0:T(8,128)(2,1)S(1)} %get-tuple-element.36.i_low_ref.low_ref, f32[256,768]{1,0:T(8,128)S(1)} %collective-permute-done.1.block_ref, ...), custom_call_target="tpu_custom_call" | custom-call | flops 2000000000 | bytes 1000 | tf_op jit(solution)/shard_map/pallas_call | solution.py:179
  67.2 0.0 collective-permute-done.9.block_ref
  67.3 1.5 %shard_map.54.t_mine = f32[256,768]{1,0:T(8,128)S(1)} custom-call(bf16[512,768]{1,0:T(8,128)(2,1)S(1)} %get-tuple-element.51.high_ref, bf16[512,768]{1,0:T(8,128)(2,1)S(1)} %get-tuple-element.52.low_ref, f32[256,768]{1,0:T(8,128)S(1)} %collective-permute-done.9.block_ref, f32[256,768]{1,0:T(8,128)S(1)} %get-tuple-element.62.given_ref), custom_call_target="tpu_custom_call" | custom-call | flops 2000000000 | bytes 1000 | tf_op jit(solution)/shard_map/pallas_call | solution.py:179
  68.8 0.0 collective-permute-done.10.t_theirs
  68.8 0.0 collective-permute-done.8.i_theirs
  68.8 1.3 %shard_map.55 = (f32[256,768]{1,0:T(8,128)}, f32[256,768]{1,0:T(8,128)}, f32[1,256]{1,0:T(1,128)}) custom-call(f32[256,768]{1,0:T(8,128)S(1)} %get-tuple-element.58.i_mine, f32[264,768]{1,0:T(8,128)S(1)} %collective-permute-done.8.i_theirs, f32[8,256]{1,0:T(8,128)S(1)} %get-tuple-element.60.l_mine, f32[256,768]{1,0:T(8,128)S(1)} %shard_map.54.t_mine, ...), custom_call_target="tpu_custom_call" | custom-call | flops 1000 | bytes 1000 | tf_op jit(solution)/shard_map/pallas_call | solution.py:179
Async XLA Ops:
  0.6 37.7 %collective-permute-start = (f32[256,768]{1,0:T(8,128)}, f32[256,768]{1,0:T(8,128)S(1)}, u32[]{:S(2)}, u32[]{:S(2)}) collective-permute-start(f32[256,768]{1,0:T(8,128)} %t_hbm.1), channel_id=1, source_target_pairs={{0,510},{1,3},{2,0},{3,5},{4,2},{5,7},{6,4},{7,9},{8,6},{9,11},{10... | collective-permute-start | bytes 2359304 | tf_op jit(solution)/shard_map/ppermute | solution.py:22
  5.5 32.9 %collective-permute-start.3 = (f32[256,768]{1,0:T(8,128)}, f32[256,768]{1,0:T(8,128)S(1)}, u32[]{:S(2)}, u32[]{:S(2)}) collective-permute-start(f32[256,768]{1,0:T(8,128)} %t_hbm.1), channel_id=1, source_target_pairs={{0,2},{1,511},{2,4},{3,1},{4,6},{5,3},{6,8},{7,5},{8,10},{9,7},{10... | collective-permute-start | bytes 2359304 | tf_op jit(solution)/shard_map/ppermute | solution.py:22
  19.2 19.2 %collective-permute-start.2 = (f32[256,768]{1,0:T(8,128)}, f32[256,768]{1,0:T(8,128)S(1)}, u32[]{:S(2)}, u32[]{:S(2)}) collective-permute-start(f32[256,768]{1,0:T(8,128)} %i_hbm.1), channel_id=1, source_target_pairs={{0,1},{1,0},{2,3},{3,2},{4,5},{5,4},{6,7},{7,6},{8,9},{9,8},{10,11... | collective-permute-start | bytes 2359304 | tf_op jit(solution)/shard_map/ppermute | solution.py:22
  22.0 1.1 %copy-start = (f32[256,768]{1,0:T(8,128)S(1)}, f32[256,768]{1,0:T(8,128)}, u32[]{:S(2)}) copy-start(f32[256,768]{1,0:T(8,128)} %t_hbm.1) | copy-start | bytes 2359300
  27.3 19.8 %collective-permute-start.6 = (f32[256,768]{1,0:T(8,128)}, f32[256,768]{1,0:T(8,128)S(1)}, u32[]{:S(2)}, u32[]{:S(2)}) collective-permute-start(f32[256,768]{1,0:T(8,128)} %i_hbm.1), channel_id=1, source_target_pairs={{0,510},{1,3},{2,0},{3,5},{4,2},{5,7},{6,4},{7,9},{8,6},{9,11},{10... | collective-permute-start | bytes 2359304 | tf_op jit(solution)/shard_map/ppermute | solution.py:22
  29.2 31.7 %collective-permute-start.7 = (f32[256,768]{1,0:T(8,128)}, f32[256,768]{1,0:T(8,128)S(1)}, u32[]{:S(2)}, u32[]{:S(2)}) collective-permute-start(f32[256,768]{1,0:T(8,128)} %i_hbm.1), channel_id=1, source_target_pairs={{0,2},{1,511},{2,4},{3,1},{4,6},{5,3},{6,8},{7,5},{8,10},{9,7},{10... | collective-permute-start | bytes 2359304 | tf_op jit(solution)/shard_map/ppermute | solution.py:22
  40.9 9.9 %collective-permute-start.5 = (f32[128,768]{1,0:T(8,128)S(1)}, f32[128,768]{1,0:T(8,128)S(1)}, u32[]{:S(2)}, u32[]{:S(2)}) collective-permute-start(f32[128,768]{1,0:T(8,128)S(1)} %get-tuple-element.48), channel_id=1, source_target_pairs={{0,1},{1,0},{2,3},{3,2},{4,5},{5,4},{6,7},{7,6},{8,9},{9,8},{10,11... | collective-permute-start | bytes 1179656 | tf_op jit(solution)/shard_map/ppermute | solution.py:22
  43.1 7.7 %collective-permute-start.4 = (f32[128,768]{1,0:T(8,128)S(1)}, f32[128,768]{1,0:T(8,128)S(1)}, u32[]{:S(2)}, u32[]{:S(2)}) collective-permute-start(f32[128,768]{1,0:T(8,128)S(1)} %get-tuple-element.46), channel_id=1, source_target_pairs={{0,1},{1,0},{2,3},{3,2},{4,5},{5,4},{6,7},{7,6},{8,9},{9,8},{10,11... | collective-permute-start | bytes 1179656 | tf_op jit(solution)/shard_map/ppermute | solution.py:22
  45.2 20.4 %collective-permute-start.1 = (f32[256,768]{1,0:T(8,128)S(1)}, f32[256,768]{1,0:T(8,128)S(1)}, u32[]{:S(2)}, u32[]{:S(2)}) collective-permute-start(f32[256,768]{1,0:T(8,128)S(1)} %collective-permute-done.in_ref), channel_id=1, source_target_pairs={{0,511},{1,2},{2,1},{3,4},{4,3},{5,6},{6,5},{7,8},{8,7},{9,10},{10... | collective-permute-start | bytes 2359304 | tf_op jit(solution)/shard_map/ppermute | solution.py:22
  47.2 20.1 %collective-permute-start.9 = (f32[256,768]{1,0:T(8,128)S(1)}, f32[256,768]{1,0:T(8,128)S(1)}, u32[]{:S(2)}, u32[]{:S(2)}) collective-permute-start(f32[256,768]{1,0:T(8,128)S(1)} %collective-permute-done.6.in_ref), channel_id=1, source_target_pairs={{0,511},{1,2},{2,1},{3,4},{4,3},{5,6},{6,5},{7,8},{8,7},{9,10},{10... | collective-permute-start | bytes 2359304 | tf_op jit(solution)/shard_map/ppermute | solution.py:22
  53.3 15.5 %collective-permute-start.8 = (f32[264,768]{1,0:T(8,128)S(1)}, f32[264,768]{1,0:T(8,128)S(1)}, u32[]{:S(2)}, u32[]{:S(2)}) collective-permute-start(f32[264,768]{1,0:T(8,128)S(1)} %get-tuple-element.59), channel_id=1, source_target_pairs={{0,1},{1,0},{2,3},{3,2},{4,5},{5,4},{6,7},{7,6},{8,9},{9,8},{10,11... | collective-permute-start | bytes 2433032 | tf_op jit(solution)/shard_map/ppermute | solution.py:22
  63.7 5.1 %collective-permute-start.10 = (f32[256,768]{1,0:T(8,128)S(1)}, f32[256,768]{1,0:T(8,128)S(1)}, u32[]{:S(2)}, u32[]{:S(2)}) collective-permute-start(f32[256,768]{1,0:T(8,128)S(1)} %get-tuple-element.63), channel_id=1, source_target_pairs={{0,1},{1,0},{2,3},{3,2},{4,5},{5,4},{6,7},{7,6},{8,9},{9,8},{10,11... | collective-permute-start | bytes 2359304 | tf_op jit(solution)/shard_map/ppermute | solution.py:22

commit v4 on v3

--- a/solution.py
+++ b/solution.py
@@ -12,8 +12,8 @@
 softness_factor = 2.0
 logit_bias = -4.0
 EXTRA = 8
-FLOPS_C = 2_000_000_000
-FLOPS_D = 2_000_000_000
+FLOPS_C = 1_000_000_000
+FLOPS_D = 10_000_000_000
 VMEM_LIMIT = 24 * 1024 * 1024
 
 
@@ -145,7 +145,7 @@
     theirs_ref[rows:, :rows] = jnp.broadcast_to(as_row(found[0][1] + found[1][1]), (EXTRA, rows))
 
 
-def images_kernel(high_ref, low_ref, in_ref, out_ref, given_ref, mine_ref, theirs_ref):
+def images_kernel(high_ref, low_ref, in_ref, out_ref, given_ref, i_theirs_ref, mine_ref, theirs_ref):
     rows = in_ref.shape[0]
     both = high_ref[...], low_ref[...]
     total = None
@@ -154,25 +154,35 @@
     for coef, block in zip(coefs, blocks):
         total = weighted(total, coef, block)
     mine_ref[...] = given_ref[...] + total[:rows]
-    theirs_ref[...] = total[rows:]
-
-
-def far_kernel(loss, high_ref, low_ref, block_ref, given_ref, *rest):
+    theirs_ref[:rows, :] = total[rows:]
+    theirs_ref[rows:, :] = i_theirs_ref[...]
+
+
+def far_texts_kernel(high_ref, low_ref, block_ref, given_ref, l_given, mine_ref, l_mine_ref):
+    block = halves(block_ref[...])
+    coefs, each = terms((high_ref[...], low_ref[...]), block, False, True)
+    mine_ref[...] = weighted(given_ref[...], coefs, block)
+    l_mine_ref[...] = l_given[...] + as_row(each)
+
+
+def far_images_kernel(high_ref, low_ref, block_ref, c_high_ref, c_low_ref, b_high_ref, b_low_ref):
     rows = block_ref.shape[0]
     block = halves(block_ref[...])
-    coefs, each = terms((high_ref[:rows, :], low_ref[:rows, :]), block, False, loss)
-    mine_ref = rest[1] if loss else rest[0]
-    mine_ref[...] = weighted(given_ref[...], coefs, block)
-    if loss:
-        rest[2][...] = rest[0][...] + as_row(each)
-
-
-def final_kernel(i_mine, i_theirs, l_mine, t_mine, t_theirs, image_ref, text_ref, loss_ref):
+    b_high_ref[...], b_low_ref[...] = block
+    coefs, _ = terms((high_ref[:rows, :], low_ref[:rows, :]), block)
+    c_high_ref[...], c_low_ref[...] = halves(coefs)
+
+
+def last_kernel(
+    c_high_ref, c_low_ref, b_high_ref, b_low_ref, i_mine, t_mine, l_mine, theirs, image_ref, text_ref, loss_ref
+):
     rows, width = t_mine.shape
     scale = softness_factor / math.sqrt(width)
-    image_ref[...] = scale * (i_mine[...] + i_theirs[:rows, :])
-    text_ref[...] = scale * (t_mine[...] + t_theirs[...])
-    loss_ref[...] = (l_mine[:1, :] + i_theirs[rows : rows + 1, :rows]) * (1.0 / ((2 * CYCLE + 1) * rows))
+    image_ref[...] = scale * (i_mine[...] + theirs[rows : 2 * rows, :])
+    loss_ref[...] = (l_mine[:1, :] + theirs[2 * rows : 2 * rows + 1, :rows]) * (1.0 / ((2 * CYCLE + 1) * rows))
+    high, low, b_high = c_high_ref[...], c_low_ref[...], b_high_ref[...]
+    total = dot(high, b_high, 0) + dot(high, b_low_ref[...], 0) + dot(low, b_high, 0)
+    text_ref[...] = scale * (total + (t_mine[...] + theirs[:rows, :]))
 
 
 def call(kernel, outs, *args, flops=1000, **specs):
@@ -216,17 +226,17 @@
         (grad, longer, loss, low2, low2),
         i_sib_high, i_sib_low, *t_sib, t_in, t_out, i_high, i_low, t_high, t_low, i_mine, l_mine,
     )
-    i_theirs = sibling(i_theirs)
-    t_mine, t_theirs = call(images_kernel, (grad, grad), t_high, t_low, i_in, i_out, t_mine)
-    t_theirs = sibling(t_theirs)
+    t_mine, theirs = call(
+        images_kernel, (grad, ((2 * rows + EXTRA, width), f32)), t_high, t_low, i_in, i_out, t_mine, i_theirs
+    )
     i_mine, l_mine = call(
-        functools.partial(far_kernel, True), (grad, loss), i_high, i_low, t_far, after(i_mine, t_mine), l_mine, flops=FLOPS_C
-    )
-    (t_mine,) = call(
-        functools.partial(far_kernel, False), (grad,), t_high, t_low, i_far, after(t_mine, l_mine), flops=FLOPS_D
-    )
+        far_texts_kernel, (grad, loss), i_high, i_low, t_far, after(i_mine, t_mine), l_mine, flops=FLOPS_C
+    )
+    theirs = sibling(theirs)
+    square = ((rows, rows), bf16)
+    found = call(far_images_kernel, (square, square, low, low), t_high, after(t_low, l_mine), i_far, flops=FLOPS_D)
     image_grad, text_grad, pair_loss = call(
-        final_kernel, (grad, grad, ((1, rows), f32)), i_mine, i_theirs, l_mine, t_mine, t_theirs
+        last_kernel, (grad, grad, ((1, rows), f32)), *found, i_mine, t_mine, l_mine, theirs
     )
     return (pair_loss.reshape(rows), image_grad, text_grad)
 

time: 70.6 us -> 70.1 us (level)
  waiting for transfers between devices: 0.06 us -> 3.24 us
  starting transfers between devices: 51.8 us -> 48.7 us
    ppermute x11 -> x10, waiting for transfers between devices: 0.06 us -> 3.24 us  [permuted(): lax.ppermute(value, 'blk', [(i, target(i) % count) for i in range(count)])]
    ppermute x11 -> x10, starting transfers between devices: 51.8 us -> 48.7 us  [permuted(): lax.ppermute(value, 'blk', [(i, target(i) % count) for i in range(count)])]
  transfers between devices with their start and end apart: 11 -> 10, of which waited for: 0 -> 2; matrix products, arithmetic and copies ran while one was open for 0% -> 0% of each run, Pallas kernels for 21% -> 20%
where the time goes in v4:
time: 70.1 us; the launch traced here: 69.6 us
  starting transfers between devices  48.7 us (69%)
  Pallas kernels  15.7 us (22%)
  waiting for transfers between devices  3.24 us (5%)
  local copies, waits for them, and re-layouts  1.13 us (2%)
  between operations  0.82 us (1%)
    ppermute x10, starting transfers between devices, permuted(): lax.ppermute(value, 'blk', [(i, target(i) % count) for i in range(count)])  48.7 us
    pallas_call x7, Pallas kernels, call(): pl.pallas_call(kernel, out_shape=[jax.ShapeDtypeStruct(shape, dtype) for...  15.7 us
    ppermute x10, waiting for transfers between devices, permuted(): lax.ppermute(value, 'blk', [(i, target(i) % count) for i in range(count)])  3.24 us
  transfers between devices with their start and end apart: 10, of which 2 were waited for; matrix products, arithmetic and copies ran while one was open for 0% of the time, Pallas kernels for 20%

profile of v4, /device:TPU:1, one launch (start us, length us, event | category | flops | bytes accessed | tf_op | source)
XLA Modules:
  0.0 69.6 jit_solution(16043716570597890920)
XLA Ops:
  0.6 4.8 %collective-permute-start.1 = (f32[256,768]{1,0:T(8,128)}, f32[256,768]{1,0:T(8,128)S(1)}, u32[]{:S(2)}, u32[]{:S(2)}) collective-permute-start(f32[256,768]{1,0:T(8,128)} %t_hbm.1), channel_id=1, source_target_pairs={{0,510},{1,3},{2,0},{3,5},{4,2},{5,7},{6,4},{7,9},{8,6},{9,11},{10... | collective-permute-start | bytes 2359304 | tf_op jit(solution)/shard_map/ppermute | solution.py:22
  5.5 13.7 %collective-permute-start.2 = (f32[256,768]{1,0:T(8,128)}, f32[256,768]{1,0:T(8,128)S(1)}, u32[]{:S(2)}, u32[]{:S(2)}) collective-permute-start(f32[256,768]{1,0:T(8,128)} %t_hbm.1), channel_id=1, source_target_pairs={{0,2},{1,511},{2,4},{3,1},{4,6},{5,3},{6,8},{7,5},{8,10},{9,7},{10... | collective-permute-start | bytes 2359304 | tf_op jit(solution)/shard_map/ppermute | solution.py:22
  19.2 2.9 %collective-permute-start = (f32[256,768]{1,0:T(8,128)}, f32[256,768]{1,0:T(8,128)S(1)}, u32[]{:S(2)}, u32[]{:S(2)}) collective-permute-start(f32[256,768]{1,0:T(8,128)} %i_hbm.1), channel_id=1, source_target_pairs={{0,1},{1,0},{2,3},{3,2},{4,5},{5,4},{6,7},{7,6},{8,9},{9,8},{10,11... | collective-permute-start | bytes 2359304 | tf_op jit(solution)/shard_map/ppermute | solution.py:22
  22.0 0.0 copy-start
  22.0 1.1 %copy-done = f32[256,768]{1,0:T(8,128)S(1)} copy-done((f32[256,768]{1,0:T(8,128)S(1)}, f32[256,768]{1,0:T(8,128)}, u32[]{:S(2)}) %copy-start) | copy-done | bytes 786456
  23.2 4.1 %shard_map.49 = (f32[128,768]{1,0:T(8,128)S(1)}, f32[128,768]{1,0:T(8,128)S(1)}, f32[256,768]{1,0:T(8,128)S(1)}, f32[8,256]{1,0:T(8,128)S(1)}, bf16[256,768]{1,0...) custom-call(f32[256,768]{1,0:T(8,128)} %i_hbm.1, ...), custom_call_target="tpu_custom_call" | custom-call | flops 1000 | bytes 1000 | tf_op jit(solution)/shard_map/pallas_call | solution.py:189
  27.3 1.9 %collective-permute-start.6 = (f32[256,768]{1,0:T(8,128)}, f32[256,768]{1,0:T(8,128)S(1)}, u32[]{:S(2)}, u32[]{:S(2)}) collective-permute-start(f32[256,768]{1,0:T(8,128)} %i_hbm.1), channel_id=1, source_target_pairs={{0,510},{1,3},{2,0},{3,5},{4,2},{5,7},{6,4},{7,9},{8,6},{9,11},{10... | collective-permute-start | bytes 2359304 | tf_op jit(solution)/shard_map/ppermute | solution.py:22
  29.2 9.1 %collective-permute-start.7 = (f32[256,768]{1,0:T(8,128)}, f32[256,768]{1,0:T(8,128)S(1)}, u32[]{:S(2)}, u32[]{:S(2)}) collective-permute-start(f32[256,768]{1,0:T(8,128)} %i_hbm.1), channel_id=1, source_target_pairs={{0,2},{1,511},{2,4},{3,1},{4,6},{5,3},{6,8},{7,5},{8,10},{9,7},{10... | collective-permute-start | bytes 2359304 | tf_op jit(solution)/shard_map/ppermute | solution.py:22
  38.3 0.0 collective-permute-done.1.in_ref
  38.3 0.0 collective-permute-done.2.out_ref
  38.3 0.0 collective-permute-done.i_sib_ref
  38.4 2.5 %shard_map.50 = (f32[256,768]{1,0:T(8,128)S(1)}, f32[8,256]{1,0:T(8,128)S(1)}, f32[256,768]{1,0:T(8,128)S(1)}, bf16[256,768]{1,0:T(8,128)(2,1)S(1)}, bf16[256,768]{1,0:T(8,128)(2,1)S(1)}) custom-call(bf16[256,768]{1,0:T(8,128)(2,1)S(1)} %get-tuple-element.39.i_high_ref.high_ref, bf16[256,768]{1,0:T(8,128)(2,1)S(1)} %get-tuple-element.40.i_low_ref.low_ref, ...), custom_call_target="tpu_custom_call" | custom-call | flops 1000 | bytes 1000 | tf_op jit(solution)/shard_map/pallas_call | solution.py:189
  40.9 2.2 %collective-permute-start.4 = (f32[128,768]{1,0:T(8,128)S(1)}, f32[128,768]{1,0:T(8,128)S(1)}, u32[]{:S(2)}, u32[]{:S(2)}) collective-permute-start(f32[128,768]{1,0:T(8,128)S(1)} %get-tuple-element.52), channel_id=1, source_target_pairs={{0,1},{1,0},{2,3},{3,2},{4,5},{5,4},{6,7},{7,6},{8,9},{9,8},{10,11... | collective-permute-start | bytes 1179656 | tf_op jit(solution)/shard_map/ppermute | solution.py:22
  43.1 2.1 %collective-permute-start.3 = (f32[128,768]{1,0:T(8,128)S(1)}, f32[128,768]{1,0:T(8,128)S(1)}, u32[]{:S(2)}, u32[]{:S(2)}) collective-permute-start(f32[128,768]{1,0:T(8,128)S(1)} %get-tuple-element.50), channel_id=1, source_target_pairs={{0,1},{1,0},{2,3},{3,2},{4,5},{5,4},{6,7},{7,6},{8,9},{9,8},{10,11... | collective-permute-start | bytes 1179656 | tf_op jit(solution)/shard_map/ppermute | solution.py:22
  45.2 1.9 %collective-permute-start.5 = (f32[256,768]{1,0:T(8,128)S(1)}, f32[256,768]{1,0:T(8,128)S(1)}, u32[]{:S(2)}, u32[]{:S(2)}) collective-permute-start(f32[256,768]{1,0:T(8,128)S(1)} %collective-permute-done.1.in_ref), channel_id=1, source_target_pairs={{0,511},{1,2},{2,1},{3,4},{4,3},{5,6},{6,5},{7,8},{8,7},{9,10},{10... | collective-permute-start | bytes 2359304 | tf_op jit(solution)/shard_map/ppermute | solution.py:22
  47.2 0.0 collective-permute-done.6.in_ref
  47.2 3.6 %collective-permute-start.8 = (f32[256,768]{1,0:T(8,128)S(1)}, f32[256,768]{1,0:T(8,128)S(1)}, u32[]{:S(2)}, u32[]{:S(2)}) collective-permute-start(f32[256,768]{1,0:T(8,128)S(1)} %collective-permute-done.6.in_ref), channel_id=1, source_target_pairs={{0,511},{1,2},{2,1},{3,4},{4,3},{5,6},{6,5},{7,8},{8,7},{9,10},{10... | collective-permute-start | bytes 2359304 | tf_op jit(solution)/shard_map/ppermute | solution.py:22
  50.8 0.0 collective-permute-done.4.t_sib_second
  50.8 0.0 collective-permute-done.3.t_sib_first
  50.8 2.4 %shard_map.51 = (f32[256,768]{1,0:T(8,128)S(1)}, f32[264,768]{1,0:T(8,128)S(1)}, f32[8,256]{1,0:T(8,128)S(1)}, bf16[512,768]{1,0:T(8,128)(2,1)S(1)}, bf16[512,768]{1,0:T(8,128)(2,1)S(1)}) custom-call(bf16[256,768]{1,0:T(8,128)(2,1)S(1)} %get-tuple-element.46.i_sib_high, bf16[256,768]{1,0:T(8,128)(2,1)S(1)} %get-tuple-element.47.i_sib_low, ...), custom_call_target="tpu_custom_call" | custom-call | flops 1000 | bytes 1000 | tf_op jit(solution)/shard_map/pallas_call | solution.py:189
  53.3 1.3 %collective-permute-done.7.out_ref = f32[256,768]{1,0:T(8,128)S(1)} collective-permute-done((f32[256,768]{1,0:T(8,128)}, f32[256,768]{1,0:T(8,128)S(1)}, u32[]{:S(2)}, u32[]{:S(2)}) %collective-permute-start.7) | collective-permute-done | bytes 786464 | tf_op jit(solution)/shard_map/ppermute | solution.py:22
  54.5 2.8 %shard_map.52 = (f32[256,768]{1,0:T(8,128)S(1)}, f32[520,768]{1,0:T(8,128)S(1)}) custom-call(bf16[512,768]{1,0:T(8,128)(2,1)S(1)} %get-tuple-element.54.high_ref, bf16[512,768]{1,0:T(8,128)(2,1)S(1)} %get-tuple-element.64.low_ref, f32[256,768]{1,0:T(8,128)S(1)} %collective-permute-done.6.in_ref, f32[256,768]{1,0:T(8,128)S(1)} %collective-permute-done.7.out_ref, ...), custom_call_target="tpu_custom_call" | custom-call | flops 1000 | bytes 1000 | tf_op jit(solution)/shard_map/pallas_call | solution.py:189
  57.3 6.4 %collective-permute-start.9 = (f32[520,768]{1,0:T(8,128)S(1)}, f32[520,768]{1,0:T(8,128)S(1)}, u32[]{:S(2)}, u32[]{:S(2)}) collective-permute-start(f32[520,768]{1,0:T(8,128)S(1)} %get-tuple-element.71), channel_id=1, source_target_pairs={{0,1},{1,0},{2,3},{3,2},{4,5},{5,4},{6,7},{7,6},{8,9},{9,8},{10,11... | collective-permute-start | bytes 4792328 | tf_op jit(solution)/shard_map/ppermute | solution.py:22
  63.7 0.0 collective-permute-done.5.block_ref
  63.7 1.6 %shard_map.53 = (f32[256,768]{1,0:T(8,128)S(1)}, f32[8,256]{1,0:T(8,128)S(1)}) custom-call(bf16[256,768]{1,0:T(8,128)(2,1)S(1)} %get-tuple-element.39.i_high_ref.high_ref, bf16[256,768]{1,0:T(8,128)(2,1)S(1)} %get-tuple-element.40.i_low_ref.low_ref, f32[256,768]{1,0:T(8,128)S(1)} %collective-permute-done.5.block_ref, ...), custom_call_target="tpu_custom_call" | custom-call | flops 1000000000 | bytes 1000 | tf_op jit(solution)/shard_map/pallas_call | solution.py:189
  65.3 2.0 %collective-permute-done.8.block_ref = f32[256,768]{1,0:T(8,128)S(1)} collective-permute-done((f32[256,768]{1,0:T(8,128)S(1)}, f32[256,768]{1,0:T(8,128)S(1)}, u32[]{:S(2)}, u32[]{:S(2)}) %collective-permute-start.8) | collective-permute-done | bytes 786464 | tf_op jit(solution)/shard_map/ppermute | solution.py:22
  67.3 0.6 shard_map.54
  67.9 0.0 collective-permute-done.9.theirs
  67.9 1.7 %shard_map.55 = (f32[256,768]{1,0:T(8,128)}, f32[256,768]{1,0:T(8,128)}, f32[1,256]{1,0:T(1,128)}) custom-call(bf16[256,256]{1,0:T(8,128)(2,1)S(1)} %get-tuple-element.66.c_high_ref, bf16[256,256]{1,0:T(8,128)(2,1)S(1)} %get-tuple-element.67.c_low_ref, bf16[256,768]{1,0:T(8,128)(2,1)S(1)} %get-tuple-element.68.b_high_ref, ...), custom_call_target="tpu_custom_call" | custom-call | flops 1000 | bytes 1000 | tf_op jit(solution)/shard_map/pallas_call | solution.py:189
Async XLA Ops:
  0.6 37.7 %collective-permute-start.1 = (f32[256,768]{1,0:T(8,128)}, f32[256,768]{1,0:T(8,128)S(1)}, u32[]{:S(2)}, u32[]{:S(2)}) collective-permute-start(f32[256,768]{1,0:T(8,128)} %t_hbm.1), channel_id=1, source_target_pairs={{0,510},{1,3},{2,0},{3,5},{4,2},{5,7},{6,4},{7,9},{8,6},{9,11},{10... | collective-permute-start | bytes 2359304 | tf_op jit(solution)/shard_map/ppermute | solution.py:22
  5.5 32.9 %collective-permute-start.2 = (f32[256,768]{1,0:T(8,128)}, f32[256,768]{1,0:T(8,128)S(1)}, u32[]{:S(2)}, u32[]{:S(2)}) collective-permute-start(f32[256,768]{1,0:T(8,128)} %t_hbm.1), channel_id=1, source_target_pairs={{0,2},{1,511},{2,4},{3,1},{4,6},{5,3},{6,8},{7,5},{8,10},{9,7},{10... | collective-permute-start | bytes 2359304 | tf_op jit(solution)/shard_map/ppermute | solution.py:22
  19.2 19.2 %collective-permute-start = (f32[256,768]{1,0:T(8,128)}, f32[256,768]{1,0:T(8,128)S(1)}, u32[]{:S(2)}, u32[]{:S(2)}) collective-permute-start(f32[256,768]{1,0:T(8,128)} %i_hbm.1), channel_id=1, source_target_pairs={{0,1},{1,0},{2,3},{3,2},{4,5},{5,4},{6,7},{7,6},{8,9},{9,8},{10,11... | collective-permute-start | bytes 2359304 | tf_op jit(solution)/shard_map/ppermute | solution.py:22
  22.0 1.1 %copy-start = (f32[256,768]{1,0:T(8,128)S(1)}, f32[256,768]{1,0:T(8,128)}, u32[]{:S(2)}) copy-start(f32[256,768]{1,0:T(8,128)} %t_hbm.1) | copy-start | bytes 2359300
  27.3 19.8 %collective-permute-start.6 = (f32[256,768]{1,0:T(8,128)}, f32[256,768]{1,0:T(8,128)S(1)}, u32[]{:S(2)}, u32[]{:S(2)}) collective-permute-start(f32[256,768]{1,0:T(8,128)} %i_hbm.1), channel_id=1, source_target_pairs={{0,510},{1,3},{2,0},{3,5},{4,2},{5,7},{6,4},{7,9},{8,6},{9,11},{10... | collective-permute-start | bytes 2359304 | tf_op jit(solution)/shard_map/ppermute | solution.py:22
  29.2 25.3 %collective-permute-start.7 = (f32[256,768]{1,0:T(8,128)}, f32[256,768]{1,0:T(8,128)S(1)}, u32[]{:S(2)}, u32[]{:S(2)}) collective-permute-start(f32[256,768]{1,0:T(8,128)} %i_hbm.1), channel_id=1, source_target_pairs={{0,2},{1,511},{2,4},{3,1},{4,6},{5,3},{6,8},{7,5},{8,10},{9,7},{10... | collective-permute-start | bytes 2359304 | tf_op jit(solution)/shard_map/ppermute | solution.py:22
  40.9 9.9 %collective-permute-start.4 = (f32[128,768]{1,0:T(8,128)S(1)}, f32[128,768]{1,0:T(8,128)S(1)}, u32[]{:S(2)}, u32[]{:S(2)}) collective-permute-start(f32[128,768]{1,0:T(8,128)S(1)} %get-tuple-element.52), channel_id=1, source_target_pairs={{0,1},{1,0},{2,3},{3,2},{4,5},{5,4},{6,7},{7,6},{8,9},{9,8},{10,11... | collective-permute-start | bytes 1179656 | tf_op jit(solution)/shard_map/ppermute | solution.py:22
  43.1 7.7 %collective-permute-start.3 = (f32[128,768]{1,0:T(8,128)S(1)}, f32[128,768]{1,0:T(8,128)S(1)}, u32[]{:S(2)}, u32[]{:S(2)}) collective-permute-start(f32[128,768]{1,0:T(8,128)S(1)} %get-tuple-element.50), channel_id=1, source_target_pairs={{0,1},{1,0},{2,3},{3,2},{4,5},{5,4},{6,7},{7,6},{8,9},{9,8},{10,11... | collective-permute-start | bytes 1179656 | tf_op jit(solution)/shard_map/ppermute | solution.py:22
  45.2 18.5 %collective-permute-start.5 = (f32[256,768]{1,0:T(8,128)S(1)}, f32[256,768]{1,0:T(8,128)S(1)}, u32[]{:S(2)}, u32[]{:S(2)}) collective-permute-start(f32[256,768]{1,0:T(8,128)S(1)} %collective-permute-done.1.in_ref), channel_id=1, source_target_pairs={{0,511},{1,2},{2,1},{3,4},{4,3},{5,6},{6,5},{7,8},{8,7},{9,10},{10... | collective-permute-start | bytes 2359304 | tf_op jit(solution)/shard_map/ppermute | solution.py:22
  47.2 20.1 %collective-permute-start.8 = (f32[256,768]{1,0:T(8,128)S(1)}, f32[256,768]{1,0:T(8,128)S(1)}, u32[]{:S(2)}, u32[]{:S(2)}) collective-permute-start(f32[256,768]{1,0:T(8,128)S(1)} %collective-permute-done.6.in_ref), channel_id=1, source_target_pairs={{0,511},{1,2},{2,1},{3,4},{4,3},{5,6},{6,5},{7,8},{8,7},{9,10},{10... | collective-permute-start | bytes 2359304 | tf_op jit(solution)/shard_map/ppermute | solution.py:22
  57.3 10.6 %collective-permute-start.9 = (f32[520,768]{1,0:T(8,128)S(1)}, f32[520,768]{1,0:T(8,128)S(1)}, u32[]{:S(2)}, u32[]{:S(2)}) collective-permute-start(f32[520,768]{1,0:T(8,128)S(1)} %get-tuple-element.71), channel_id=1, source_target_pairs={{0,1},{1,0},{2,3},{3,2},{4,5},{5,4},{6,7},{7,6},{8,9},{9,8},{10,11... | collective-permute-start | bytes 4792328 | tf_op jit(solution)/shard_map/ppermute | solution.py:22

commit v5 on v4

--- a/solution.py
+++ b/solution.py
@@ -86,7 +86,7 @@
 
 
 def own_kernel(
-    i_hbm, t_hbm, first_ref, second_ref, i_mine_ref, l_mine_ref, i_high_ref, i_low_ref, t_mine_ref, t_high_ref, t_low_ref, i_ref, t_ref, sems
+    i_hbm, t_hbm, first_ref, second_ref, i_mine_ref, l_mine_ref, i_high_ref, i_low_ref, t_high_ref, t_low_ref, i_ref, t_ref, sems
 ):
     copies = [
         pltpu.make_async_copy(source, target, sems.at[k])
@@ -104,12 +104,10 @@
     coefs, lost = terms(own, texts, True, True)
     i_mine_ref[...] = weighted(None, coefs, texts)
     l_mine_ref[...] = jnp.broadcast_to(as_row(lost), l_mine_ref.shape)
-    coefs, _ = terms(texts, own, True)
-    t_mine_ref[...] = weighted(None, coefs, own)
 
 
 def texts_kernel(
-    i_high_ref, i_low_ref, t_high_ref, t_low_ref, i_sib_ref, in_ref, out_ref, i_given, l_given, t_given,
+    i_high_ref, i_low_ref, t_high_ref, t_low_ref, in_ref, out_ref, i_sib_ref, i_given, l_given,
     i_mine_ref, l_mine_ref, t_mine_ref, high_ref, low_ref,
 ):
     own, texts, images = (i_high_ref[...], i_low_ref[...]), (t_high_ref[...], t_low_ref[...]), halves(i_sib_ref[...])
@@ -117,7 +115,7 @@
     blocks = [halves(in_ref[...]), halves(out_ref[...])]
     found = [terms(own, block, False, True) for block in blocks]
     coefs, _ = terms(texts, images)
-    t_mine_ref[...] = weighted(t_given[...], coefs, images)
+    t_mine_ref[...] = weighted(None, coefs, images)
     mine = i_given[...]
     for (coefs, _), block in zip(found, blocks):
         mine = weighted(mine, coefs, block)
@@ -158,11 +156,16 @@
     theirs_ref[rows:, :] = i_theirs_ref[...]
 
 
-def far_texts_kernel(high_ref, low_ref, block_ref, given_ref, l_given, mine_ref, l_mine_ref):
-    block = halves(block_ref[...])
-    coefs, each = terms((high_ref[...], low_ref[...]), block, False, True)
-    mine_ref[...] = weighted(given_ref[...], coefs, block)
+def far_texts_kernel(
+    i_high_ref, i_low_ref, t_high_ref, t_low_ref, block_ref, i_given, l_given, t_given, i_mine_ref, l_mine_ref, t_mine_ref
+):
+    rows = block_ref.shape[0]
+    own, texts, block = (i_high_ref[...], i_low_ref[...]), (t_high_ref[:rows, :], t_low_ref[:rows, :]), halves(block_ref[...])
+    coefs, each = terms(own, block, False, True)
+    i_mine_ref[...] = weighted(i_given[...], coefs, block)
     l_mine_ref[...] = l_given[...] + as_row(each)
+    coefs, _ = terms(texts, own, True)
+    t_mine_ref[...] = weighted(t_given[...], coefs, own)
 
 
 def far_images_kernel(high_ref, low_ref, block_ref, c_high_ref, c_low_ref, b_high_ref, b_low_ref):
@@ -204,20 +207,20 @@
 
     t_in, t_out = inward(texts), outward(texts)
     i_sib = sibling(images)
-    *t_parts, i_mine, l_mine, i_high, i_low, t_mine, t_high, t_low = call(
+    *t_parts, i_mine, l_mine, i_high, i_low, t_high, t_low = call(
         own_kernel,
-        (half, half, grad, loss, low, low, grad, low, low),
+        (half, half, grad, loss, low, low, low, low),
         images,
         texts,
-        in_specs=[pl.BlockSpec(memory_space=pl.ANY)] * 2,
+        in_specs=[pl.BlockSpec(memory_space=pltpu.HBM)] * 2,
         scratch_shapes=[pltpu.VMEM(images.shape, f32)] * 2 + [pltpu.SemaphoreType.DMA((2,))],
     )
-    i_in, i_out = inward(after(images, t_mine)), outward(images)
+    i_in, i_out = inward(after(images, l_mine)), outward(images)
     t_far = across(t_in)
     i_mine, l_mine, t_mine, i_sib_high, i_sib_low = call(
         texts_kernel,
         (grad, loss, grad, low, low),
-        i_high, i_low, t_high, t_low, i_sib, t_in, t_out, i_mine, l_mine, t_mine,
+        i_high, i_low, t_high, t_low, t_in, t_out, i_sib, i_mine, l_mine,
     )
     i_far = across(after(i_in, l_mine))
     t_sib = [sibling(after(part, l_mine)) for part in t_parts]
@@ -229,8 +232,8 @@
     t_mine, theirs = call(
         images_kernel, (grad, ((2 * rows + EXTRA, width), f32)), t_high, t_low, i_in, i_out, t_mine, i_theirs
     )
-    i_mine, l_mine = call(
-        far_texts_kernel, (grad, loss), i_high, i_low, t_far, after(i_mine, t_mine), l_mine, flops=FLOPS_C
+    i_mine, l_mine, t_mine = call(
+        far_texts_kernel, (grad, loss, grad), i_high, i_low, t_high, t_low, t_far, i_mine, l_mine, t_mine, flops=FLOPS_C
     )
     theirs = sibling(theirs)
     square = ((rows, rows), bf16)

time: 70.1 us -> 69.7 us (level)
  waiting for transfers between devices: 3.24 us -> 0.75 us
  starting transfers between devices: 48.7 us -> 50.8 us
    ppermute x10, waiting for transfers between devices: 3.24 us -> 0.75 us  [permuted(): lax.ppermute(value, 'blk', [(i, target(i) % count) for i in range(count)])]
    ppermute x10, starting transfers between devices: 48.7 us -> 50.8 us  [permuted(): lax.ppermute(value, 'blk', [(i, target(i) % count) for i in range(count)])]
where the time goes in v5:
time: 69.7 us; the launch traced here: 69.1 us
  starting transfers between devices  50.8 us (73%)
  Pallas kernels  15.6 us (22%)
  local copies, waits for them, and re-layouts  1.13 us (2%)
  between operations  0.82 us (1%)
  waiting for transfers between devices  0.75 us (1%)
    ppermute x10, starting transfers between devices, permuted(): lax.ppermute(value, 'blk', [(i, target(i) % count) for i in range(count)])  50.8 us
    pallas_call x7, Pallas kernels, call(): pl.pallas_call(kernel, out_shape=[jax.ShapeDtypeStruct(shape, dtype) for...  15.6 us
  transfers between devices with their start and end apart: 10, of which 2 were waited for; matrix products, arithmetic and copies ran while one was open for 0% of the time, Pallas kernels for 20%

profile of v5, /device:TPU:1, one launch (start us, length us, event | category | flops | bytes accessed | tf_op | source)
XLA Modules:
  0.0 69.1 jit_solution(579402053939757009)
XLA Ops:
  0.6 4.8 %collective-permute-start = (f32[256,768]{1,0:T(8,128)}, f32[256,768]{1,0:T(8,128)S(1)}, u32[]{:S(2)}, u32[]{:S(2)}) collective-permute-start(f32[256,768]{1,0:T(8,128)} %t_hbm.1), channel_id=1, source_target_pairs={{0,510},{1,3},{2,0},{3,5},{4,2},{5,7},{6,4},{7,9},{8,6},{9,11},{10... | collective-permute-start | bytes 2359304 | tf_op jit(solution)/shard_map/ppermute | solution.py:22
  5.5 13.7 %collective-permute-start.1 = (f32[256,768]{1,0:T(8,128)}, f32[256,768]{1,0:T(8,128)S(1)}, u32[]{:S(2)}, u32[]{:S(2)}) collective-permute-start(f32[256,768]{1,0:T(8,128)} %t_hbm.1), channel_id=1, source_target_pairs={{0,2},{1,511},{2,4},{3,1},{4,6},{5,3},{6,8},{7,5},{8,10},{9,7},{10... | collective-permute-start | bytes 2359304 | tf_op jit(solution)/shard_map/ppermute | solution.py:22
  19.2 2.9 %collective-permute-start.2 = (f32[256,768]{1,0:T(8,128)}, f32[256,768]{1,0:T(8,128)S(1)}, u32[]{:S(2)}, u32[]{:S(2)}) collective-permute-start(f32[256,768]{1,0:T(8,128)} %i_hbm.1), channel_id=1, source_target_pairs={{0,1},{1,0},{2,3},{3,2},{4,5},{5,4},{6,7},{7,6},{8,9},{9,8},{10,11... | collective-permute-start | bytes 2359304 | tf_op jit(solution)/shard_map/ppermute | solution.py:22
  22.0 0.0 copy-start
  22.0 1.1 %copy-done = f32[256,768]{1,0:T(8,128)S(1)} copy-done((f32[256,768]{1,0:T(8,128)S(1)}, f32[256,768]{1,0:T(8,128)}, u32[]{:S(2)}) %copy-start) | copy-done | bytes 786456
  23.2 2.8 %shard_map.49 = (f32[128,768]{1,0:T(8,128)S(1)}, f32[128,768]{1,0:T(8,128)S(1)}, f32[256,768]{1,0:T(8,128)S(1)}, f32[8,256]{1,0:T(8,128)S(1)}, bf16[256,768]{1,0...) custom-call(f32[256,768]{1,0:T(8,128)} %i_hbm.1, ...), custom_call_target="tpu_custom_call" | custom-call | flops 1000 | bytes 1000 | tf_op jit(solution)/shard_map/pallas_call | solution.py:192
  26.0 1.9 %collective-permute-start.6 = (f32[256,768]{1,0:T(8,128)}, f32[256,768]{1,0:T(8,128)S(1)}, u32[]{:S(2)}, u32[]{:S(2)}) collective-permute-start(f32[256,768]{1,0:T(8,128)} %i_hbm.1), channel_id=1, source_target_pairs={{0,510},{1,3},{2,0},{3,5},{4,2},{5,7},{6,4},{7,9},{8,6},{9,11},{10... | collective-permute-start | bytes 2359304 | tf_op jit(solution)/shard_map/ppermute | solution.py:22
  27.9 9.1 %collective-permute-start.7 = (f32[256,768]{1,0:T(8,128)}, f32[256,768]{1,0:T(8,128)S(1)}, u32[]{:S(2)}, u32[]{:S(2)}) collective-permute-start(f32[256,768]{1,0:T(8,128)} %i_hbm.1), channel_id=1, source_target_pairs={{0,2},{1,511},{2,4},{3,1},{4,6},{5,3},{6,8},{7,5},{8,10},{9,7},{10... | collective-permute-start | bytes 2359304 | tf_op jit(solution)/shard_map/ppermute | solution.py:22
  37.0 0.0 collective-permute-done.in_ref
  37.0 0.0 collective-permute-done.1.out_ref
  37.0 0.0 collective-permute-done.2.i_sib_ref
  37.0 2.5 %shard_map.50 = (f32[256,768]{1,0:T(8,128)S(1)}, f32[8,256]{1,0:T(8,128)S(1)}, f32[256,768]{1,0:T(8,128)S(1)}, bf16[256,768]{1,0:T(8,128)(2,1)S(1)}, bf16[256,768]{1,0:T(8,128)(2,1)S(1)}) custom-call(bf16[256,768]{1,0:T(8,128)(2,1)S(1)} %get-tuple-element.38.i_high_ref, bf16[256,768]{1,0:T(8,128)(2,1)S(1)} %get-tuple-element.39.i_low_ref, ...), custom_call_target="tpu_custom_call" | custom-call | flops 1000 | bytes 1000 | tf_op jit(solution)/shard_map/pallas_call | solution.py:192
  39.5 3.3 %collective-permute-start.3 = (f32[128,768]{1,0:T(8,128)S(1)}, f32[128,768]{1,0:T(8,128)S(1)}, u32[]{:S(2)}, u32[]{:S(2)}) collective-permute-start(f32[128,768]{1,0:T(8,128)S(1)} %get-tuple-element.48), channel_id=1, source_target_pairs={{0,1},{1,0},{2,3},{3,2},{4,5},{5,4},{6,7},{7,6},{8,9},{9,8},{10,11... | collective-permute-start | bytes 1179656 | tf_op jit(solution)/shard_map/ppermute | solution.py:22
  42.9 1.9 %collective-permute-start.4 = (f32[128,768]{1,0:T(8,128)S(1)}, f32[128,768]{1,0:T(8,128)S(1)}, u32[]{:S(2)}, u32[]{:S(2)}) collective-permute-start(f32[128,768]{1,0:T(8,128)S(1)} %get-tuple-element.50), channel_id=1, source_target_pairs={{0,1},{1,0},{2,3},{3,2},{4,5},{5,4},{6,7},{7,6},{8,9},{9,8},{10,11... | collective-permute-start | bytes 1179656 | tf_op jit(solution)/shard_map/ppermute | solution.py:22
  44.8 1.9 %collective-permute-start.5 = (f32[256,768]{1,0:T(8,128)S(1)}, f32[256,768]{1,0:T(8,128)S(1)}, u32[]{:S(2)}, u32[]{:S(2)}) collective-permute-start(f32[256,768]{1,0:T(8,128)S(1)} %collective-permute-done.in_ref), channel_id=1, source_target_pairs={{0,511},{1,2},{2,1},{3,4},{4,3},{5,6},{6,5},{7,8},{8,7},{9,10},{10... | collective-permute-start | bytes 2359304 | tf_op jit(solution)/shard_map/ppermute | solution.py:22
  46.7 0.0 collective-permute-done.6.in_ref
  46.7 3.6 %collective-permute-start.8 = (f32[256,768]{1,0:T(8,128)S(1)}, f32[256,768]{1,0:T(8,128)S(1)}, u32[]{:S(2)}, u32[]{:S(2)}) collective-permute-start(f32[256,768]{1,0:T(8,128)S(1)} %collective-permute-done.6.in_ref), channel_id=1, source_target_pairs={{0,511},{1,2},{2,1},{3,4},{4,3},{5,6},{6,5},{7,8},{8,7},{9,10},{10... | collective-permute-start | bytes 2359304 | tf_op jit(solution)/shard_map/ppermute | solution.py:22
  50.4 0.0 collective-permute-done.3.t_sib_first
  50.4 0.0 collective-permute-done.4.t_sib_second
  50.4 2.4 %shard_map.51 = (f32[256,768]{1,0:T(8,128)S(1)}, f32[264,768]{1,0:T(8,128)S(1)}, f32[8,256]{1,0:T(8,128)S(1)}, bf16[512,768]{1,0:T(8,128)(2,1)S(1)}, bf16[512,768]{1,0:T(8,128)(2,1)S(1)}) custom-call(bf16[256,768]{1,0:T(8,128)(2,1)S(1)} %get-tuple-element.44.i_sib_high, bf16[256,768]{1,0:T(8,128)(2,1)S(1)} %get-tuple-element.45.i_sib_low, ...), custom_call_target="tpu_custom_call" | custom-call | flops 1000 | bytes 1000 | tf_op jit(solution)/shard_map/pallas_call | solution.py:192
  52.8 0.4 collective-permute-done.7.out_ref
  53.2 2.8 %shard_map.52 = (f32[256,768]{1,0:T(8,128)S(1)}, f32[520,768]{1,0:T(8,128)S(1)}) custom-call(bf16[512,768]{1,0:T(8,128)(2,1)S(1)} %get-tuple-element.52.high_ref.t_high_ref, bf16[512,768]{1,0:T(8,128)(2,1)S(1)} %get-tuple-element.61.low_ref.t_low_ref, f32[256,768]{1,0:T(8,128)S(1)} %collective-permute-done.6.in_ref, ...), custom_call_target="tpu_custom_call" | custom-call | flops 1000 | bytes 1000 | tf_op jit(solution)/shard_map/pallas_call | solution.py:192
  56.0 7.6 %collective-permute-start.9 = (f32[520,768]{1,0:T(8,128)S(1)}, f32[520,768]{1,0:T(8,128)S(1)}, u32[]{:S(2)}, u32[]{:S(2)}) collective-permute-start(f32[520,768]{1,0:T(8,128)S(1)} %get-tuple-element.69), channel_id=1, source_target_pairs={{0,1},{1,0},{2,3},{3,2},{4,5},{5,4},{6,7},{7,6},{8,9},{9,8},{10,11... | collective-permute-start | bytes 4792328 | tf_op jit(solution)/shard_map/ppermute | solution.py:22
  63.6 0.0 collective-permute-done.5.block_ref
  63.6 2.9 %shard_map.53 = (f32[256,768]{1,0:T(8,128)S(1)}, f32[8,256]{1,0:T(8,128)S(1)}, f32[256,768]{1,0:T(8,128)S(1)}) custom-call(bf16[256,768]{1,0:T(8,128)(2,1)S(1)} %get-tuple-element.38.i_high_ref, bf16[256,768]{1,0:T(8,128)(2,1)S(1)} %get-tuple-element.39.i_low_ref, bf16[512,768]{1,0:T(8,128)(2,1)S(1)} %get-tuple-element.52.high_ref.t_high_ref, ...), custom_call_target="tpu_custom_call" | custom-call | flops 1000000000 | bytes 1000 | tf_op jit(solution)/shard_map/pallas_call | solution.py:192
  66.5 0.3 collective-permute-done.8.block_ref
  66.8 0.6 shard_map.54
  67.5 0.0 collective-permute-done.9.theirs
  67.5 1.6 %shard_map.55 = (f32[256,768]{1,0:T(8,128)}, f32[256,768]{1,0:T(8,128)}, f32[1,256]{1,0:T(1,128)}) custom-call(bf16[256,256]{1,0:T(8,128)(2,1)S(1)} %get-tuple-element.63.c_high_ref, bf16[256,256]{1,0:T(8,128)(2,1)S(1)} %get-tuple-element.64.c_low_ref, bf16[256,768]{1,0:T(8,128)(2,1)S(1)} %get-tuple-element.65.b_high_ref, ...), custom_call_target="tpu_custom_call" | custom-call | flops 1000 | bytes 1000 | tf_op jit(solution)/shard_map/pallas_call | solution.py:192
Async XLA Ops:
  0.6 36.4 %collective-permute-start = (f32[256,768]{1,0:T(8,128)}, f32[256,768]{1,0:T(8,128)S(1)}, u32[]{:S(2)}, u32[]{:S(2)}) collective-permute-start(f32[256,768]{1,0:T(8,128)} %t_hbm.1), channel_id=1, source_target_pairs={{0,510},{1,3},{2,0},{3,5},{4,2},{5,7},{6,4},{7,9},{8,6},{9,11},{10... | collective-permute-start | bytes 2359304 | tf_op jit(solution)/shard_map/ppermute | solution.py:22
  5.5 31.5 %collective-permute-start.1 = (f32[256,768]{1,0:T(8,128)}, f32[256,768]{1,0:T(8,128)S(1)}, u32[]{:S(2)}, u32[]{:S(2)}) collective-permute-start(f32[256,768]{1,0:T(8,128)} %t_hbm.1), channel_id=1, source_target_pairs={{0,2},{1,511},{2,4},{3,1},{4,6},{5,3},{6,8},{7,5},{8,10},{9,7},{10... | collective-permute-start | bytes 2359304 | tf_op jit(solution)/shard_map/ppermute | solution.py:22
  19.2 17.9 %collective-permute-start.2 = (f32[256,768]{1,0:T(8,128)}, f32[256,768]{1,0:T(8,128)S(1)}, u32[]{:S(2)}, u32[]{:S(2)}) collective-permute-start(f32[256,768]{1,0:T(8,128)} %i_hbm.1), channel_id=1, source_target_pairs={{0,1},{1,0},{2,3},{3,2},{4,5},{5,4},{6,7},{7,6},{8,9},{9,8},{10,11... | collective-permute-start | bytes 2359304 | tf_op jit(solution)/shard_map/ppermute | solution.py:22
  22.0 1.1 %copy-start = (f32[256,768]{1,0:T(8,128)S(1)}, f32[256,768]{1,0:T(8,128)}, u32[]{:S(2)}) copy-start(f32[256,768]{1,0:T(8,128)} %t_hbm.1) | copy-start | bytes 2359300
  26.0 20.8 %collective-permute-start.6 = (f32[256,768]{1,0:T(8,128)}, f32[256,768]{1,0:T(8,128)S(1)}, u32[]{:S(2)}, u32[]{:S(2)}) collective-permute-start(f32[256,768]{1,0:T(8,128)} %i_hbm.1), channel_id=1, source_target_pairs={{0,510},{1,3},{2,0},{3,5},{4,2},{5,7},{6,4},{7,9},{8,6},{9,11},{10... | collective-permute-start | bytes 2359304 | tf_op jit(solution)/shard_map/ppermute | solution.py:22
  27.9 25.3 %collective-permute-start.7 = (f32[256,768]{1,0:T(8,128)}, f32[256,768]{1,0:T(8,128)S(1)}, u32[]{:S(2)}, u32[]{:S(2)}) collective-permute-start(f32[256,768]{1,0:T(8,128)} %i_hbm.1), channel_id=1, source_target_pairs={{0,2},{1,511},{2,4},{3,1},{4,6},{5,3},{6,8},{7,5},{8,10},{9,7},{10... | collective-permute-start | bytes 2359304 | tf_op jit(solution)/shard_map/ppermute | solution.py:22
  39.5 10.9 %collective-permute-start.3 = (f32[128,768]{1,0:T(8,128)S(1)}, f32[128,768]{1,0:T(8,128)S(1)}, u32[]{:S(2)}, u32[]{:S(2)}) collective-permute-start(f32[128,768]{1,0:T(8,128)S(1)} %get-tuple-element.48), channel_id=1, source_target_pairs={{0,1},{1,0},{2,3},{3,2},{4,5},{5,4},{6,7},{7,6},{8,9},{9,8},{10,11... | collective-permute-start | bytes 1179656 | tf_op jit(solution)/shard_map/ppermute | solution.py:22
  42.9 7.5 %collective-permute-start.4 = (f32[128,768]{1,0:T(8,128)S(1)}, f32[128,768]{1,0:T(8,128)S(1)}, u32[]{:S(2)}, u32[]{:S(2)}) collective-permute-start(f32[128,768]{1,0:T(8,128)S(1)} %get-tuple-element.50), channel_id=1, source_target_pairs={{0,1},{1,0},{2,3},{3,2},{4,5},{5,4},{6,7},{7,6},{8,9},{9,8},{10,11... | collective-permute-start | bytes 1179656 | tf_op jit(solution)/shard_map/ppermute | solution.py:22
  44.8 18.8 %collective-permute-start.5 = (f32[256,768]{1,0:T(8,128)S(1)}, f32[256,768]{1,0:T(8,128)S(1)}, u32[]{:S(2)}, u32[]{:S(2)}) collective-permute-start(f32[256,768]{1,0:T(8,128)S(1)} %collective-permute-done.in_ref), channel_id=1, source_target_pairs={{0,511},{1,2},{2,1},{3,4},{4,3},{5,6},{6,5},{7,8},{8,7},{9,10},{10... | collective-permute-start | bytes 2359304 | tf_op jit(solution)/shard_map/ppermute | solution.py:22
  46.7 20.1 %collective-permute-start.8 = (f32[256,768]{1,0:T(8,128)S(1)}, f32[256,768]{1,0:T(8,128)S(1)}, u32[]{:S(2)}, u32[]{:S(2)}) collective-permute-start(f32[256,768]{1,0:T(8,128)S(1)} %collective-permute-done.6.in_ref), channel_id=1, source_target_pairs={{0,511},{1,2},{2,1},{3,4},{4,3},{5,6},{6,5},{7,8},{8,7},{9,10},{10... | collective-permute-start | bytes 2359304 | tf_op jit(solution)/shard_map/ppermute | solution.py:22
  56.0 11.5 %collective-permute-start.9 = (f32[520,768]{1,0:T(8,128)S(1)}, f32[520,768]{1,0:T(8,128)S(1)}, u32[]{:S(2)}, u32[]{:S(2)}) collective-permute-start(f32[520,768]{1,0:T(8,128)S(1)} %get-tuple-element.69), channel_id=1, source_target_pairs={{0,1},{1,0},{2,3},{3,2},{4,5},{5,4},{6,7},{7,6},{8,9},{9,8},{10,11... | collective-permute-start | bytes 4792328 | tf_op jit(solution)/shard_map/ppermute | solution.py:22

commit v6 on v5

--- a/solution.py
+++ b/solution.py
@@ -12,7 +12,7 @@
 softness_factor = 2.0
 logit_bias = -4.0
 EXTRA = 8
-FLOPS_C = 1_000_000_000
+FLOPS_C = 2_000_000_000
 FLOPS_D = 10_000_000_000
 VMEM_LIMIT = 24 * 1024 * 1024
 
@@ -202,14 +202,14 @@
     rows, width = images.shape
     f32, bf16 = jnp.float32, jnp.bfloat16
     grad, longer = ((rows, width), f32), ((rows + EXTRA, width), f32)
-    half = ((rows // 2, width), f32)
+    most, rest = ((rows - rows // 4, width), f32), ((rows // 4, width), f32)
     low, low2, loss = ((rows, width), bf16), ((2 * rows, width), bf16), ((EXTRA, rows), f32)
 
     t_in, t_out = inward(texts), outward(texts)
     i_sib = sibling(images)
     *t_parts, i_mine, l_mine, i_high, i_low, t_high, t_low = call(
         own_kernel,
-        (half, half, grad, loss, low, low, low, low),
+        (most, rest, grad, loss, low, low, low, low),
         images,
         texts,
         in_specs=[pl.BlockSpec(memory_space=pltpu.HBM)] * 2,

time: 69.7 us -> 69.5 us (level)
  transfers between devices with their start and end apart: 10 -> 10, of which waited for: 2 -> 1; matrix products, arithmetic and copies ran while one was open for 0% -> 0% of each run, Pallas kernels for 20% -> 20%
where the time goes in v6:
time: 69.5 us; the launch traced here: 69 us
  starting transfers between devices  50.7 us (73%)
  Pallas kernels  15.7 us (23%)
  local copies, waits for them, and re-layouts  1.13 us (2%)
  between operations  0.82 us (1%)
    ppermute x10, starting transfers between devices, permuted(): lax.ppermute(value, 'blk', [(i, target(i) % count) for i in range(count)])  50.7 us
    pallas_call x7, Pallas kernels, call(): pl.pallas_call(kernel, out_shape=[jax.ShapeDtypeStruct(shape, dtype) for...  15.7 us
  transfers between devices with their start and end apart: 10, of which 1 were waited for; matrix products, arithmetic and copies ran while one was open for 0% of the time, Pallas kernels for 20%

profile of v6, /device:TPU:1, one launch (start us, length us, event | category | flops | bytes accessed | tf_op | source)
XLA Modules:
  0.0 69.0 jit_solution(3236396734892209786)
XLA Ops:
  0.6 4.8 %collective-permute-start = (f32[256,768]{1,0:T(8,128)}, f32[256,768]{1,0:T(8,128)S(1)}, u32[]{:S(2)}, u32[]{:S(2)}) collective-permute-start(f32[256,768]{1,0:T(8,128)} %t_hbm.1), channel_id=1, source_target_pairs={{0,510},{1,3},{2,0},{3,5},{4,2},{5,7},{6,4},{7,9},{8,6},{9,11},{10... | collective-permute-start | bytes 2359304 | tf_op jit(solution)/shard_map/ppermute | solution.py:22
  5.5 13.7 %collective-permute-start.1 = (f32[256,768]{1,0:T(8,128)}, f32[256,768]{1,0:T(8,128)S(1)}, u32[]{:S(2)}, u32[]{:S(2)}) collective-permute-start(f32[256,768]{1,0:T(8,128)} %t_hbm.1), channel_id=1, source_target_pairs={{0,2},{1,511},{2,4},{3,1},{4,6},{5,3},{6,8},{7,5},{8,10},{9,7},{10... | collective-permute-start | bytes 2359304 | tf_op jit(solution)/shard_map/ppermute | solution.py:22
  19.2 2.9 %collective-permute-start.2 = (f32[256,768]{1,0:T(8,128)}, f32[256,768]{1,0:T(8,128)S(1)}, u32[]{:S(2)}, u32[]{:S(2)}) collective-permute-start(f32[256,768]{1,0:T(8,128)} %i_hbm.1), channel_id=1, source_target_pairs={{0,1},{1,0},{2,3},{3,2},{4,5},{5,4},{6,7},{7,6},{8,9},{9,8},{10,11... | collective-permute-start | bytes 2359304 | tf_op jit(solution)/shard_map/ppermute | solution.py:22
  22.0 0.0 copy-start
  22.0 1.1 %copy-done = f32[256,768]{1,0:T(8,128)S(1)} copy-done((f32[256,768]{1,0:T(8,128)S(1)}, f32[256,768]{1,0:T(8,128)}, u32[]{:S(2)}) %copy-start) | copy-done | bytes 786456
  23.2 2.8 %shard_map.49 = (f32[192,768]{1,0:T(8,128)S(1)}, f32[64,768]{1,0:T(8,128)S(1)}, f32[256,768]{1,0:T(8,128)S(1)}, f32[8,256]{1,0:T(8,128)S(1)}, bf16[256,768]{1,0:...) custom-call(f32[256,768]{1,0:T(8,128)} %i_hbm.1, ...), custom_call_target="tpu_custom_call" | custom-call | flops 1000 | bytes 1000 | tf_op jit(solution)/shard_map/pallas_call | solution.py:192
  26.0 1.9 %collective-permute-start.6 = (f32[256,768]{1,0:T(8,128)}, f32[256,768]{1,0:T(8,128)S(1)}, u32[]{:S(2)}, u32[]{:S(2)}) collective-permute-start(f32[256,768]{1,0:T(8,128)} %i_hbm.1), channel_id=1, source_target_pairs={{0,510},{1,3},{2,0},{3,5},{4,2},{5,7},{6,4},{7,9},{8,6},{9,11},{10... | collective-permute-start | bytes 2359304 | tf_op jit(solution)/shard_map/ppermute | solution.py:22
  27.9 9.1 %collective-permute-start.7 = (f32[256,768]{1,0:T(8,128)}, f32[256,768]{1,0:T(8,128)S(1)}, u32[]{:S(2)}, u32[]{:S(2)}) collective-permute-start(f32[256,768]{1,0:T(8,128)} %i_hbm.1), channel_id=1, source_target_pairs={{0,2},{1,511},{2,4},{3,1},{4,6},{5,3},{6,8},{7,5},{8,10},{9,7},{10... | collective-permute-start | bytes 2359304 | tf_op jit(solution)/shard_map/ppermute | solution.py:22
  37.0 0.0 collective-permute-done.in_ref
  37.0 0.0 collective-permute-done.1.out_ref
  37.0 0.0 collective-permute-done.2.i_sib_ref
  37.0 2.5 %shard_map.50 = (f32[256,768]{1,0:T(8,128)S(1)}, f32[8,256]{1,0:T(8,128)S(1)}, f32[256,768]{1,0:T(8,128)S(1)}, bf16[256,768]{1,0:T(8,128)(2,1)S(1)}, bf16[256,768]{1,0:T(8,128)(2,1)S(1)}) custom-call(bf16[256,768]{1,0:T(8,128)(2,1)S(1)} %get-tuple-element.38.i_high_ref, bf16[256,768]{1,0:T(8,128)(2,1)S(1)} %get-tuple-element.39.i_low_ref, ...), custom_call_target="tpu_custom_call" | custom-call | flops 1000 | bytes 1000 | tf_op jit(solution)/shard_map/pallas_call | solution.py:192
  39.5 3.3 %collective-permute-start.3 = (f32[192,768]{1,0:T(8,128)S(1)}, f32[192,768]{1,0:T(8,128)S(1)}, u32[]{:S(2)}, u32[]{:S(2)}) collective-permute-start(f32[192,768]{1,0:T(8,128)S(1)} %get-tuple-element.48), channel_id=1, source_target_pairs={{0,1},{1,0},{2,3},{3,2},{4,5},{5,4},{6,7},{7,6},{8,9},{9,8},{10,11... | collective-permute-start | bytes 1769480 | tf_op jit(solution)/shard_map/ppermute | solution.py:22
  42.9 1.9 %collective-permute-start.5 = (f32[256,768]{1,0:T(8,128)S(1)}, f32[256,768]{1,0:T(8,128)S(1)}, u32[]{:S(2)}, u32[]{:S(2)}) collective-permute-start(f32[256,768]{1,0:T(8,128)S(1)} %collective-permute-done.in_ref), channel_id=1, source_target_pairs={{0,511},{1,2},{2,1},{3,4},{4,3},{5,6},{6,5},{7,8},{8,7},{9,10},{10... | collective-permute-start | bytes 2359304 | tf_op jit(solution)/shard_map/ppermute | solution.py:22
  44.8 8.3 %collective-permute-start.4 = (f32[64,768]{1,0:T(8,128)S(1)}, f32[64,768]{1,0:T(8,128)S(1)}, u32[]{:S(2)}, u32[]{:S(2)}) collective-permute-start(f32[64,768]{1,0:T(8,128)S(1)} %get-tuple-element.50), channel_id=1, source_target_pairs={{0,1},{1,0},{2,3},{3,2},{4,5},{5,4},{6,7},{7,6},{8,9},{9,8},{10,11... | collective-permute-start | bytes 589832 | tf_op jit(solution)/shard_map/ppermute | solution.py:22
  53.1 0.0 collective-permute-done.6.in_ref
  53.2 1.9 %collective-permute-start.8 = (f32[256,768]{1,0:T(8,128)S(1)}, f32[256,768]{1,0:T(8,128)S(1)}, u32[]{:S(2)}, u32[]{:S(2)}) collective-permute-start(f32[256,768]{1,0:T(8,128)S(1)} %collective-permute-done.6.in_ref), channel_id=1, source_target_pairs={{0,511},{1,2},{2,1},{3,4},{4,3},{5,6},{6,5},{7,8},{8,7},{9,10},{10... | collective-permute-start | bytes 2359304 | tf_op jit(solution)/shard_map/ppermute | solution.py:22
  55.1 0.0 collective-permute-done.4.t_sib_second
  55.1 0.0 collective-permute-done.3.t_sib_first
  55.1 2.4 %shard_map.51 = (f32[256,768]{1,0:T(8,128)S(1)}, f32[264,768]{1,0:T(8,128)S(1)}, f32[8,256]{1,0:T(8,128)S(1)}, bf16[512,768]{1,0:T(8,128)(2,1)S(1)}, bf16[512,768]{1,0:T(8,128)(2,1)S(1)}) custom-call(bf16[256,768]{1,0:T(8,128)(2,1)S(1)} %get-tuple-element.44.i_sib_high, bf16[256,768]{1,0:T(8,128)(2,1)S(1)} %get-tuple-element.45.i_sib_low, ...), custom_call_target="tpu_custom_call" | custom-call | flops 1000 | bytes 1000 | tf_op jit(solution)/shard_map/pallas_call | solution.py:192
  57.5 0.0 collective-permute-done.7.out_ref
  57.5 2.8 %shard_map.52 = (f32[256,768]{1,0:T(8,128)S(1)}, f32[520,768]{1,0:T(8,128)S(1)}) custom-call(bf16[512,768]{1,0:T(8,128)(2,1)S(1)} %get-tuple-element.52.high_ref.t_high_ref, bf16[512,768]{1,0:T(8,128)(2,1)S(1)} %get-tuple-element.61.low_ref.t_low_ref, f32[256,768]{1,0:T(8,128)S(1)} %collective-permute-done.6.in_ref, ...), custom_call_target="tpu_custom_call" | custom-call | flops 1000 | bytes 1000 | tf_op jit(solution)/shard_map/pallas_call | solution.py:192
  60.3 2.9 %collective-permute-start.9 = (f32[520,768]{1,0:T(8,128)S(1)}, f32[520,768]{1,0:T(8,128)S(1)}, u32[]{:S(2)}, u32[]{:S(2)}) collective-permute-start(f32[520,768]{1,0:T(8,128)S(1)} %get-tuple-element.69), channel_id=1, source_target_pairs={{0,1},{1,0},{2,3},{3,2},{4,5},{5,4},{6,7},{7,6},{8,9},{9,8},{10,11... | collective-permute-start | bytes 4792328 | tf_op jit(solution)/shard_map/ppermute | solution.py:22
  63.2 0.0 collective-permute-done.5.block_ref
  63.2 2.9 %shard_map.53 = (f32[256,768]{1,0:T(8,128)S(1)}, f32[8,256]{1,0:T(8,128)S(1)}, f32[256,768]{1,0:T(8,128)S(1)}) custom-call(bf16[256,768]{1,0:T(8,128)(2,1)S(1)} %get-tuple-element.38.i_high_ref, bf16[256,768]{1,0:T(8,128)(2,1)S(1)} %get-tuple-element.39.i_low_ref, bf16[512,768]{1,0:T(8,128)(2,1)S(1)} %get-tuple-element.52.high_ref.t_high_ref, ...), custom_call_target="tpu_custom_call" | custom-call | flops 2000000000 | bytes 1000 | tf_op jit(solution)/shard_map/pallas_call | solution.py:192
  66.1 0.7 collective-permute-done.8.block_ref
  66.8 0.6 shard_map.54
  67.4 0.0 collective-permute-done.9.theirs
  67.4 1.6 %shard_map.55 = (f32[256,768]{1,0:T(8,128)}, f32[256,768]{1,0:T(8,128)}, f32[1,256]{1,0:T(1,128)}) custom-call(bf16[256,256]{1,0:T(8,128)(2,1)S(1)} %get-tuple-element.63.c_high_ref, bf16[256,256]{1,0:T(8,128)(2,1)S(1)} %get-tuple-element.64.c_low_ref, bf16[256,768]{1,0:T(8,128)(2,1)S(1)} %get-tuple-element.65.b_high_ref, ...), custom_call_target="tpu_custom_call" | custom-call | flops 1000 | bytes 1000 | tf_op jit(solution)/shard_map/pallas_call | solution.py:192
Async XLA Ops:
  0.6 36.4 %collective-permute-start = (f32[256,768]{1,0:T(8,128)}, f32[256,768]{1,0:T(8,128)S(1)}, u32[]{:S(2)}, u32[]{:S(2)}) collective-permute-start(f32[256,768]{1,0:T(8,128)} %t_hbm.1), channel_id=1, source_target_pairs={{0,510},{1,3},{2,0},{3,5},{4,2},{5,7},{6,4},{7,9},{8,6},{9,11},{10... | collective-permute-start | bytes 2359304 | tf_op jit(solution)/shard_map/ppermute | solution.py:22
  5.5 31.5 %collective-permute-start.1 = (f32[256,768]{1,0:T(8,128)}, f32[256,768]{1,0:T(8,128)S(1)}, u32[]{:S(2)}, u32[]{:S(2)}) collective-permute-start(f32[256,768]{1,0:T(8,128)} %t_hbm.1), channel_id=1, source_target_pairs={{0,2},{1,511},{2,4},{3,1},{4,6},{5,3},{6,8},{7,5},{8,10},{9,7},{10... | collective-permute-start | bytes 2359304 | tf_op jit(solution)/shard_map/ppermute | solution.py:22
  19.2 17.9 %collective-permute-start.2 = (f32[256,768]{1,0:T(8,128)}, f32[256,768]{1,0:T(8,128)S(1)}, u32[]{:S(2)}, u32[]{:S(2)}) collective-permute-start(f32[256,768]{1,0:T(8,128)} %i_hbm.1), channel_id=1, source_target_pairs={{0,1},{1,0},{2,3},{3,2},{4,5},{5,4},{6,7},{7,6},{8,9},{9,8},{10,11... | collective-permute-start | bytes 2359304 | tf_op jit(solution)/shard_map/ppermute | solution.py:22
  22.0 1.1 %copy-start = (f32[256,768]{1,0:T(8,128)S(1)}, f32[256,768]{1,0:T(8,128)}, u32[]{:S(2)}) copy-start(f32[256,768]{1,0:T(8,128)} %t_hbm.1) | copy-start | bytes 2359300
  26.0 27.2 %collective-permute-start.6 = (f32[256,768]{1,0:T(8,128)}, f32[256,768]{1,0:T(8,128)S(1)}, u32[]{:S(2)}, u32[]{:S(2)}) collective-permute-start(f32[256,768]{1,0:T(8,128)} %i_hbm.1), channel_id=1, source_target_pairs={{0,510},{1,3},{2,0},{3,5},{4,2},{5,7},{6,4},{7,9},{8,6},{9,11},{10... | collective-permute-start | bytes 2359304 | tf_op jit(solution)/shard_map/ppermute | solution.py:22
  27.9 29.6 %collective-permute-start.7 = (f32[256,768]{1,0:T(8,128)}, f32[256,768]{1,0:T(8,128)S(1)}, u32[]{:S(2)}, u32[]{:S(2)}) collective-permute-start(f32[256,768]{1,0:T(8,128)} %i_hbm.1), channel_id=1, source_target_pairs={{0,2},{1,511},{2,4},{3,1},{4,6},{5,3},{6,8},{7,5},{8,10},{9,7},{10... | collective-permute-start | bytes 2359304 | tf_op jit(solution)/shard_map/ppermute | solution.py:22
  39.5 15.6 %collective-permute-start.3 = (f32[192,768]{1,0:T(8,128)S(1)}, f32[192,768]{1,0:T(8,128)S(1)}, u32[]{:S(2)}, u32[]{:S(2)}) collective-permute-start(f32[192,768]{1,0:T(8,128)S(1)} %get-tuple-element.48), channel_id=1, source_target_pairs={{0,1},{1,0},{2,3},{3,2},{4,5},{5,4},{6,7},{7,6},{8,9},{9,8},{10,11... | collective-permute-start | bytes 1769480 | tf_op jit(solution)/shard_map/ppermute | solution.py:22
  42.9 20.3 %collective-permute-start.5 = (f32[256,768]{1,0:T(8,128)S(1)}, f32[256,768]{1,0:T(8,128)S(1)}, u32[]{:S(2)}, u32[]{:S(2)}) collective-permute-start(f32[256,768]{1,0:T(8,128)S(1)} %collective-permute-done.in_ref), channel_id=1, source_target_pairs={{0,511},{1,2},{2,1},{3,4},{4,3},{5,6},{6,5},{7,8},{8,7},{9,10},{10... | collective-permute-start | bytes 2359304 | tf_op jit(solution)/shard_map/ppermute | solution.py:22
  44.8 10.3 %collective-permute-start.4 = (f32[64,768]{1,0:T(8,128)S(1)}, f32[64,768]{1,0:T(8,128)S(1)}, u32[]{:S(2)}, u32[]{:S(2)}) collective-permute-start(f32[64,768]{1,0:T(8,128)S(1)} %get-tuple-element.50), channel_id=1, source_target_pairs={{0,1},{1,0},{2,3},{3,2},{4,5},{5,4},{6,7},{7,6},{8,9},{9,8},{10,11... | collective-permute-start | bytes 589832 | tf_op jit(solution)/shard_map/ppermute | solution.py:22
  53.2 13.6 %collective-permute-start.8 = (f32[256,768]{1,0:T(8,128)S(1)}, f32[256,768]{1,0:T(8,128)S(1)}, u32[]{:S(2)}, u32[]{:S(2)}) collective-permute-start(f32[256,768]{1,0:T(8,128)S(1)} %collective-permute-done.6.in_ref), channel_id=1, source_target_pairs={{0,511},{1,2},{2,1},{3,4},{4,3},{5,6},{6,5},{7,8},{8,7},{9,10},{10... | collective-permute-start | bytes 2359304 | tf_op jit(solution)/shard_map/ppermute | solution.py:22
  60.3 7.1 %collective-permute-start.9 = (f32[520,768]{1,0:T(8,128)S(1)}, f32[520,768]{1,0:T(8,128)S(1)}, u32[]{:S(2)}, u32[]{:S(2)}) collective-permute-start(f32[520,768]{1,0:T(8,128)S(1)} %get-tuple-element.69), channel_id=1, source_target_pairs={{0,1},{1,0},{2,3},{3,2},{4,5},{5,4},{6,7},{7,6},{8,9},{9,8},{10,11... | collective-permute-start | bytes 4792328 | tf_op jit(solution)/shard_map/ppermute | solution.py:22

commit v7 on v6

--- a/solution.py
+++ b/solution.py
@@ -206,7 +206,6 @@
     low, low2, loss = ((rows, width), bf16), ((2 * rows, width), bf16), ((EXTRA, rows), f32)
 
     t_in, t_out = inward(texts), outward(texts)
-    i_sib = sibling(images)
     *t_parts, i_mine, l_mine, i_high, i_low, t_high, t_low = call(
         own_kernel,
         (most, rest, grad, loss, low, low, low, low),
@@ -215,6 +214,7 @@
         in_specs=[pl.BlockSpec(memory_space=pltpu.HBM)] * 2,
         scratch_shapes=[pltpu.VMEM(images.shape, f32)] * 2 + [pltpu.SemaphoreType.DMA((2,))],
     )
+    i_sib = sibling(after(images, l_mine))
     i_in, i_out = inward(after(images, l_mine)), outward(images)
     t_far = across(t_in)
     i_mine, l_mine, t_mine, i_sib_high, i_sib_low = call(

time: 69.5 us -> 69.5 us (level)
  no operation moved by 1% of the time
where the time goes in v7:
time: 69.5 us; the launch traced here: 69 us
  starting transfers between devices  50.7 us (73%)
  Pallas kernels  15.6 us (22%)
  local copies, waits for them, and re-layouts  1.14 us (2%)
  between operations  0.82 us (1%)
  waiting for transfers between devices  0.73 us (1%)
    ppermute x10, starting transfers between devices, permuted(): lax.ppermute(value, 'blk', [(i, target(i) % count) for i in range(count)])  50.7 us
    pallas_call x7, Pallas kernels, call(): pl.pallas_call(kernel, out_shape=[jax.ShapeDtypeStruct(shape, dtype) for...  15.6 us
  transfers between devices with their start and end apart: 10, of which 1 were waited for; matrix products, arithmetic and copies ran while one was open for 0% of the time, Pallas kernels for 20%

profile of v7, /device:TPU:1, one launch (start us, length us, event | category | flops | bytes accessed | tf_op | source)
XLA Modules:
  0.0 69.0 jit_solution(5691979119740795278)
XLA Ops:
  0.6 4.8 %collective-permute-start = (f32[256,768]{1,0:T(8,128)}, f32[256,768]{1,0:T(8,128)S(1)}, u32[]{:S(2)}, u32[]{:S(2)}) collective-permute-start(f32[256,768]{1,0:T(8,128)} %t_hbm.1), channel_id=1, source_target_pairs={{0,510},{1,3},{2,0},{3,5},{4,2},{5,7},{6,4},{7,9},{8,6},{9,11},{10... | collective-permute-start | bytes 2359304 | tf_op jit(solution)/shard_map/ppermute | solution.py:22
  5.5 13.7 %collective-permute-start.1 = (f32[256,768]{1,0:T(8,128)}, f32[256,768]{1,0:T(8,128)S(1)}, u32[]{:S(2)}, u32[]{:S(2)}) collective-permute-start(f32[256,768]{1,0:T(8,128)} %t_hbm.1), channel_id=1, source_target_pairs={{0,2},{1,511},{2,4},{3,1},{4,6},{5,3},{6,8},{7,5},{8,10},{9,7},{10... | collective-permute-start | bytes 2359304 | tf_op jit(solution)/shard_map/ppermute | solution.py:22
  19.2 0.0 copy-start
  19.2 1.1 %copy-done = f32[256,768]{1,0:T(8,128)S(1)} copy-done((f32[256,768]{1,0:T(8,128)S(1)}, f32[256,768]{1,0:T(8,128)}, u32[]{:S(2)}) %copy-start) | copy-done | bytes 786456
  20.3 2.8 %shard_map.49 = (f32[192,768]{1,0:T(8,128)S(1)}, f32[64,768]{1,0:T(8,128)S(1)}, f32[256,768]{1,0:T(8,128)S(1)}, f32[8,256]{1,0:T(8,128)S(1)}, bf16[256,768]{1,0:...) custom-call(f32[256,768]{1,0:T(8,128)} %i_hbm.1, ...), custom_call_target="tpu_custom_call" | custom-call | flops 1000 | bytes 1000 | tf_op jit(solution)/shard_map/pallas_call | solution.py:192
  23.1 2.9 %collective-permute-start.2 = (f32[256,768]{1,0:T(8,128)}, f32[256,768]{1,0:T(8,128)S(1)}, u32[]{:S(2)}, u32[]{:S(2)}) collective-permute-start(f32[256,768]{1,0:T(8,128)} %i_hbm.1), channel_id=1, source_target_pairs={{0,1},{1,0},{2,3},{3,2},{4,5},{5,4},{6,7},{7,6},{8,9},{9,8},{10,11... | collective-permute-start | bytes 2359304 | tf_op jit(solution)/shard_map/ppermute | solution.py:22
  26.0 1.9 %collective-permute-start.6 = (f32[256,768]{1,0:T(8,128)}, f32[256,768]{1,0:T(8,128)S(1)}, u32[]{:S(2)}, u32[]{:S(2)}) collective-permute-start(f32[256,768]{1,0:T(8,128)} %i_hbm.1), channel_id=1, source_target_pairs={{0,510},{1,3},{2,0},{3,5},{4,2},{5,7},{6,4},{7,9},{8,6},{9,11},{10... | collective-permute-start | bytes 2359304 | tf_op jit(solution)/shard_map/ppermute | solution.py:22
  27.9 9.1 %collective-permute-start.7 = (f32[256,768]{1,0:T(8,128)}, f32[256,768]{1,0:T(8,128)S(1)}, u32[]{:S(2)}, u32[]{:S(2)}) collective-permute-start(f32[256,768]{1,0:T(8,128)} %i_hbm.1), channel_id=1, source_target_pairs={{0,2},{1,511},{2,4},{3,1},{4,6},{5,3},{6,8},{7,5},{8,10},{9,7},{10... | collective-permute-start | bytes 2359304 | tf_op jit(solution)/shard_map/ppermute | solution.py:22
  37.0 0.0 collective-permute-done.in_ref
  37.0 0.0 collective-permute-done.1.out_ref
  37.0 0.0 collective-permute-done.2.i_sib_ref
  37.0 2.5 %shard_map.50 = (f32[256,768]{1,0:T(8,128)S(1)}, f32[8,256]{1,0:T(8,128)S(1)}, f32[256,768]{1,0:T(8,128)S(1)}, bf16[256,768]{1,0:T(8,128)(2,1)S(1)}, bf16[256,768]{1,0:T(8,128)(2,1)S(1)}) custom-call(bf16[256,768]{1,0:T(8,128)(2,1)S(1)} %get-tuple-element.38.i_high_ref, bf16[256,768]{1,0:T(8,128)(2,1)S(1)} %get-tuple-element.39.i_low_ref, ...), custom_call_target="tpu_custom_call" | custom-call | flops 1000 | bytes 1000 | tf_op jit(solution)/shard_map/pallas_call | solution.py:192
  39.5 3.3 %collective-permute-start.3 = (f32[192,768]{1,0:T(8,128)S(1)}, f32[192,768]{1,0:T(8,128)S(1)}, u32[]{:S(2)}, u32[]{:S(2)}) collective-permute-start(f32[192,768]{1,0:T(8,128)S(1)} %get-tuple-element.49), channel_id=1, source_target_pairs={{0,1},{1,0},{2,3},{3,2},{4,5},{5,4},{6,7},{7,6},{8,9},{9,8},{10,11... | collective-permute-start | bytes 1769480 | tf_op jit(solution)/shard_map/ppermute | solution.py:22
  42.8 1.9 %collective-permute-start.5 = (f32[256,768]{1,0:T(8,128)S(1)}, f32[256,768]{1,0:T(8,128)S(1)}, u32[]{:S(2)}, u32[]{:S(2)}) collective-permute-start(f32[256,768]{1,0:T(8,128)S(1)} %collective-permute-done.in_ref), channel_id=1, source_target_pairs={{0,511},{1,2},{2,1},{3,4},{4,3},{5,6},{6,5},{7,8},{8,7},{9,10},{10... | collective-permute-start | bytes 2359304 | tf_op jit(solution)/shard_map/ppermute | solution.py:22
  44.8 8.3 %collective-permute-start.4 = (f32[64,768]{1,0:T(8,128)S(1)}, f32[64,768]{1,0:T(8,128)S(1)}, u32[]{:S(2)}, u32[]{:S(2)}) collective-permute-start(f32[64,768]{1,0:T(8,128)S(1)} %get-tuple-element.51), channel_id=1, source_target_pairs={{0,1},{1,0},{2,3},{3,2},{4,5},{5,4},{6,7},{7,6},{8,9},{9,8},{10,11... | collective-permute-start | bytes 589832 | tf_op jit(solution)/shard_map/ppermute | solution.py:22
  53.1 0.0 collective-permute-done.6.in_ref
  53.1 1.9 %collective-permute-start.8 = (f32[256,768]{1,0:T(8,128)S(1)}, f32[256,768]{1,0:T(8,128)S(1)}, u32[]{:S(2)}, u32[]{:S(2)}) collective-permute-start(f32[256,768]{1,0:T(8,128)S(1)} %collective-permute-done.6.in_ref), channel_id=1, source_target_pairs={{0,511},{1,2},{2,1},{3,4},{4,3},{5,6},{6,5},{7,8},{8,7},{9,10},{10... | collective-permute-start | bytes 2359304 | tf_op jit(solution)/shard_map/ppermute | solution.py:22
  55.0 0.0 collective-permute-done.4.t_sib_second
  55.0 0.0 collective-permute-done.3.t_sib_first
  55.1 2.4 %shard_map.51 = (f32[256,768]{1,0:T(8,128)S(1)}, f32[264,768]{1,0:T(8,128)S(1)}, f32[8,256]{1,0:T(8,128)S(1)}, bf16[512,768]{1,0:T(8,128)(2,1)S(1)}, bf16[512,768]{1,0:T(8,128)(2,1)S(1)}) custom-call(bf16[256,768]{1,0:T(8,128)(2,1)S(1)} %get-tuple-element.45.i_sib_high, bf16[256,768]{1,0:T(8,128)(2,1)S(1)} %get-tuple-element.46.i_sib_low, ...), custom_call_target="tpu_custom_call" | custom-call | flops 1000 | bytes 1000 | tf_op jit(solution)/shard_map/pallas_call | solution.py:192
  57.5 0.0 collective-permute-done.7.out_ref
  57.5 2.7 %shard_map.52 = (f32[256,768]{1,0:T(8,128)S(1)}, f32[520,768]{1,0:T(8,128)S(1)}) custom-call(bf16[512,768]{1,0:T(8,128)(2,1)S(1)} %get-tuple-element.53.high_ref.t_high_ref, bf16[512,768]{1,0:T(8,128)(2,1)S(1)} %get-tuple-element.61.low_ref.t_low_ref, f32[256,768]{1,0:T(8,128)S(1)} %collective-permute-done.6.in_ref, ...), custom_call_target="tpu_custom_call" | custom-call | flops 1000 | bytes 1000 | tf_op jit(solution)/shard_map/pallas_call | solution.py:192
  60.2 2.8 %collective-permute-start.9 = (f32[520,768]{1,0:T(8,128)S(1)}, f32[520,768]{1,0:T(8,128)S(1)}, u32[]{:S(2)}, u32[]{:S(2)}) collective-permute-start(f32[520,768]{1,0:T(8,128)S(1)} %get-tuple-element.69), channel_id=1, source_target_pairs={{0,1},{1,0},{2,3},{3,2},{4,5},{5,4},{6,7},{7,6},{8,9},{9,8},{10,11... | collective-permute-start | bytes 4792328 | tf_op jit(solution)/shard_map/ppermute | solution.py:22
  63.1 0.0 collective-permute-done.5.block_ref
  63.1 2.9 %shard_map.53 = (f32[256,768]{1,0:T(8,128)S(1)}, f32[8,256]{1,0:T(8,128)S(1)}, f32[256,768]{1,0:T(8,128)S(1)}) custom-call(bf16[256,768]{1,0:T(8,128)(2,1)S(1)} %get-tuple-element.38.i_high_ref, bf16[256,768]{1,0:T(8,128)(2,1)S(1)} %get-tuple-element.39.i_low_ref, bf16[512,768]{1,0:T(8,128)(2,1)S(1)} %get-tuple-element.53.high_ref.t_high_ref, ...), custom_call_target="tpu_custom_call" | custom-call | flops 2000000000 | bytes 1000 | tf_op jit(solution)/shard_map/pallas_call | solution.py:192
  66.0 0.7 %collective-permute-done.8.block_ref = f32[256,768]{1,0:T(8,128)S(1)} collective-permute-done((f32[256,768]{1,0:T(8,128)S(1)}, f32[256,768]{1,0:T(8,128)S(1)}, u32[]{:S(2)}, u32[]{:S(2)}) %collective-permute-start.8) | collective-permute-done | bytes 786464 | tf_op jit(solution)/shard_map/ppermute | solution.py:22
  66.7 0.6 shard_map.54
  67.3 0.0 collective-permute-done.9.theirs
  67.4 1.7 %shard_map.55 = (f32[256,768]{1,0:T(8,128)}, f32[256,768]{1,0:T(8,128)}, f32[1,256]{1,0:T(1,128)}) custom-call(bf16[256,256]{1,0:T(8,128)(2,1)S(1)} %get-tuple-element.63.c_high_ref, bf16[256,256]{1,0:T(8,128)(2,1)S(1)} %get-tuple-element.64.c_low_ref, bf16[256,768]{1,0:T(8,128)(2,1)S(1)} %get-tuple-element.65.b_high_ref, ...), custom_call_target="tpu_custom_call" | custom-call | flops 1000 | bytes 1000 | tf_op jit(solution)/shard_map/pallas_call | solution.py:192
Async XLA Ops:
  0.6 36.4 %collective-permute-start = (f32[256,768]{1,0:T(8,128)}, f32[256,768]{1,0:T(8,128)S(1)}, u32[]{:S(2)}, u32[]{:S(2)}) collective-permute-start(f32[256,768]{1,0:T(8,128)} %t_hbm.1), channel_id=1, source_target_pairs={{0,510},{1,3},{2,0},{3,5},{4,2},{5,7},{6,4},{7,9},{8,6},{9,11},{10... | collective-permute-start | bytes 2359304 | tf_op jit(solution)/shard_map/ppermute | solution.py:22
  5.5 31.6 %collective-permute-start.1 = (f32[256,768]{1,0:T(8,128)}, f32[256,768]{1,0:T(8,128)S(1)}, u32[]{:S(2)}, u32[]{:S(2)}) collective-permute-start(f32[256,768]{1,0:T(8,128)} %t_hbm.1), channel_id=1, source_target_pairs={{0,2},{1,511},{2,4},{3,1},{4,6},{5,3},{6,8},{7,5},{8,10},{9,7},{10... | collective-permute-start | bytes 2359304 | tf_op jit(solution)/shard_map/ppermute | solution.py:22
  19.2 1.1 %copy-start = (f32[256,768]{1,0:T(8,128)S(1)}, f32[256,768]{1,0:T(8,128)}, u32[]{:S(2)}) copy-start(f32[256,768]{1,0:T(8,128)} %t_hbm.1) | copy-start | bytes 2359300
  23.1 13.9 %collective-permute-start.2 = (f32[256,768]{1,0:T(8,128)}, f32[256,768]{1,0:T(8,128)S(1)}, u32[]{:S(2)}, u32[]{:S(2)}) collective-permute-start(f32[256,768]{1,0:T(8,128)} %i_hbm.1), channel_id=1, source_target_pairs={{0,1},{1,0},{2,3},{3,2},{4,5},{5,4},{6,7},{7,6},{8,9},{9,8},{10,11... | collective-permute-start | bytes 2359304 | tf_op jit(solution)/shard_map/ppermute | solution.py:22
  26.0 27.1 %collective-permute-start.6 = (f32[256,768]{1,0:T(8,128)}, f32[256,768]{1,0:T(8,128)S(1)}, u32[]{:S(2)}, u32[]{:S(2)}) collective-permute-start(f32[256,768]{1,0:T(8,128)} %i_hbm.1), channel_id=1, source_target_pairs={{0,510},{1,3},{2,0},{3,5},{4,2},{5,7},{6,4},{7,9},{8,6},{9,11},{10... | collective-permute-start | bytes 2359304 | tf_op jit(solution)/shard_map/ppermute | solution.py:22
  27.9 29.6 %collective-permute-start.7 = (f32[256,768]{1,0:T(8,128)}, f32[256,768]{1,0:T(8,128)S(1)}, u32[]{:S(2)}, u32[]{:S(2)}) collective-permute-start(f32[256,768]{1,0:T(8,128)} %i_hbm.1), channel_id=1, source_target_pairs={{0,2},{1,511},{2,4},{3,1},{4,6},{5,3},{6,8},{7,5},{8,10},{9,7},{10... | collective-permute-start | bytes 2359304 | tf_op jit(solution)/shard_map/ppermute | solution.py:22
  39.5 15.6 %collective-permute-start.3 = (f32[192,768]{1,0:T(8,128)S(1)}, f32[192,768]{1,0:T(8,128)S(1)}, u32[]{:S(2)}, u32[]{:S(2)}) collective-permute-start(f32[192,768]{1,0:T(8,128)S(1)} %get-tuple-element.49), channel_id=1, source_target_pairs={{0,1},{1,0},{2,3},{3,2},{4,5},{5,4},{6,7},{7,6},{8,9},{9,8},{10,11... | collective-permute-start | bytes 1769480 | tf_op jit(solution)/shard_map/ppermute | solution.py:22
  42.8 20.2 %collective-permute-start.5 = (f32[256,768]{1,0:T(8,128)S(1)}, f32[256,768]{1,0:T(8,128)S(1)}, u32[]{:S(2)}, u32[]{:S(2)}) collective-permute-start(f32[256,768]{1,0:T(8,128)S(1)} %collective-permute-done.in_ref), channel_id=1, source_target_pairs={{0,511},{1,2},{2,1},{3,4},{4,3},{5,6},{6,5},{7,8},{8,7},{9,10},{10... | collective-permute-start | bytes 2359304 | tf_op jit(solution)/shard_map/ppermute | solution.py:22
  44.8 10.3 %collective-permute-start.4 = (f32[64,768]{1,0:T(8,128)S(1)}, f32[64,768]{1,0:T(8,128)S(1)}, u32[]{:S(2)}, u32[]{:S(2)}) collective-permute-start(f32[64,768]{1,0:T(8,128)S(1)} %get-tuple-element.51), channel_id=1, source_target_pairs={{0,1},{1,0},{2,3},{3,2},{4,5},{5,4},{6,7},{7,6},{8,9},{9,8},{10,11... | collective-permute-start | bytes 589832 | tf_op jit(solution)/shard_map/ppermute | solution.py:22
  53.1 13.6 %collective-permute-start.8 = (f32[256,768]{1,0:T(8,128)S(1)}, f32[256,768]{1,0:T(8,128)S(1)}, u32[]{:S(2)}, u32[]{:S(2)}) collective-permute-start(f32[256,768]{1,0:T(8,128)S(1)} %collective-permute-done.6.in_ref), channel_id=1, source_target_pairs={{0,511},{1,2},{2,1},{3,4},{4,3},{5,6},{6,5},{7,8},{8,7},{9,10},{10... | collective-permute-start | bytes 2359304 | tf_op jit(solution)/shard_map/ppermute | solution.py:22
  60.2 7.1 %collective-permute-start.9 = (f32[520,768]{1,0:T(8,128)S(1)}, f32[520,768]{1,0:T(8,128)S(1)}, u32[]{:S(2)}, u32[]{:S(2)}) collective-permute-start(f32[520,768]{1,0:T(8,128)S(1)} %get-tuple-element.69), channel_id=1, source_target_pairs={{0,1},{1,0},{2,3},{3,2},{4,5},{5,4},{6,7},{7,6},{8,9},{9,8},{10,11... | collective-permute-start | bytes 4792328 | tf_op jit(solution)/shard_map/ppermute | solution.py:22

commit v8 on v6

--- a/solution.py
+++ b/solution.py
@@ -107,15 +107,13 @@
 
 
 def texts_kernel(
-    i_high_ref, i_low_ref, t_high_ref, t_low_ref, in_ref, out_ref, i_sib_ref, i_given, l_given,
-    i_mine_ref, l_mine_ref, t_mine_ref, high_ref, low_ref,
-):
-    own, texts, images = (i_high_ref[...], i_low_ref[...]), (t_high_ref[...], t_low_ref[...]), halves(i_sib_ref[...])
-    high_ref[...], low_ref[...] = images
+    i_high_ref, i_low_ref, in_ref, out_ref, i_sib_ref, i_given, l_given,
+    i_mine_ref, l_mine_ref, high_ref, low_ref,
+):
+    own = i_high_ref[...], i_low_ref[...]
+    high_ref[...], low_ref[...] = halves(i_sib_ref[...])
     blocks = [halves(in_ref[...]), halves(out_ref[...])]
     found = [terms(own, block, False, True) for block in blocks]
-    coefs, _ = terms(texts, images)
-    t_mine_ref[...] = weighted(None, coefs, images)
     mine = i_given[...]
     for (coefs, _), block in zip(found, blocks):
         mine = weighted(mine, coefs, block)
@@ -143,7 +141,7 @@
     theirs_ref[rows:, :rows] = jnp.broadcast_to(as_row(found[0][1] + found[1][1]), (EXTRA, rows))
 
 
-def images_kernel(high_ref, low_ref, in_ref, out_ref, given_ref, i_theirs_ref, mine_ref, theirs_ref):
+def images_kernel(high_ref, low_ref, in_ref, out_ref, i_theirs_ref, mine_ref, theirs_ref):
     rows = in_ref.shape[0]
     both = high_ref[...], low_ref[...]
     total = None
@@ -151,13 +149,14 @@
     coefs = [terms(both, block)[0] for block in blocks]
     for coef, block in zip(coefs, blocks):
         total = weighted(total, coef, block)
-    mine_ref[...] = given_ref[...] + total[:rows]
+    mine_ref[...] = total[:rows]
     theirs_ref[:rows, :] = total[rows:]
     theirs_ref[rows:, :] = i_theirs_ref[...]
 
 
 def far_texts_kernel(
-    i_high_ref, i_low_ref, t_high_ref, t_low_ref, block_ref, i_given, l_given, t_given, i_mine_ref, l_mine_ref, t_mine_ref
+    i_high_ref, i_low_ref, t_high_ref, t_low_ref, sib_high_ref, sib_low_ref, block_ref, i_given, l_given, t_given,
+    i_mine_ref, l_mine_ref, t_mine_ref,
 ):
     rows = block_ref.shape[0]
     own, texts, block = (i_high_ref[...], i_low_ref[...]), (t_high_ref[:rows, :], t_low_ref[:rows, :]), halves(block_ref[...])
@@ -165,7 +164,10 @@
     i_mine_ref[...] = weighted(i_given[...], coefs, block)
     l_mine_ref[...] = l_given[...] + as_row(each)
     coefs, _ = terms(texts, own, True)
-    t_mine_ref[...] = weighted(t_given[...], coefs, own)
+    total = weighted(t_given[...], coefs, own)
+    images = sib_high_ref[...], sib_low_ref[...]
+    coefs, _ = terms(texts, images)
+    t_mine_ref[...] = weighted(total, coefs, images)
 
 
 def far_images_kernel(high_ref, low_ref, block_ref, c_high_ref, c_low_ref, b_high_ref, b_low_ref):
@@ -217,10 +219,10 @@
     )
     i_in, i_out = inward(after(images, l_mine)), outward(images)
     t_far = across(t_in)
-    i_mine, l_mine, t_mine, i_sib_high, i_sib_low = call(
+    i_mine, l_mine, i_sib_high, i_sib_low = call(
         texts_kernel,
-        (grad, loss, grad, low, low),
-        i_high, i_low, t_high, t_low, t_in, t_out, i_sib, i_mine, l_mine,
+        (grad, loss, low, low),
+        i_high, i_low, t_in, t_out, i_sib, i_mine, l_mine,
     )
     i_far = across(after(i_in, l_mine))
     t_sib = [sibling(after(part, l_mine)) for part in t_parts]
@@ -230,10 +232,10 @@
         i_sib_high, i_sib_low, *t_sib, t_in, t_out, i_high, i_low, t_high, t_low, i_mine, l_mine,
     )
     t_mine, theirs = call(
-        images_kernel, (grad, ((2 * rows + EXTRA, width), f32)), t_high, t_low, i_in, i_out, t_mine, i_theirs
+        images_kernel, (grad, ((2 * rows + EXTRA, width), f32)), t_high, t_low, i_in, i_out, i_theirs
     )
     i_mine, l_mine, t_mine = call(
-        far_texts_kernel, (grad, loss, grad), i_high, i_low, t_high, t_low, t_far, i_mine, l_mine, t_mine, flops=FLOPS_C
+        far_texts_kernel, (grad, loss, grad), i_high, i_low, t_high, t_low, i_sib_high, i_sib_low, t_far, i_mine, l_mine, t_mine, flops=FLOPS_C
     )
     theirs = sibling(theirs)
     square = ((rows, rows), bf16)

time: 69.5 us -> 69.5 us (level)
  no operation moved by 1% of the time
where the time goes in v8:
time: 69.5 us; the launch traced here: 68.4 us
  starting transfers between devices  50.7 us (73%)
  Pallas kernels  15.6 us (22%)
  local copies, waits for them, and re-layouts  1.13 us (2%)
  between operations  0.82 us (1%)
    ppermute x10, starting transfers between devices, permuted(): lax.ppermute(value, 'blk', [(i, target(i) % count) for i in range(count)])  50.7 us
    pallas_call x7, Pallas kernels, call(): pl.pallas_call(kernel, out_shape=[jax.ShapeDtypeStruct(shape, dtype) for...  15.6 us
  transfers between devices with their start and end apart: 10, of which 1 were waited for; matrix products, arithmetic and copies ran while one was open for 0% of the time, Pallas kernels for 20%

profile of v8, /device:TPU:1, one launch (start us, length us, event | category | flops | bytes accessed | tf_op | source)
XLA Modules:
  0.0 68.4 jit_solution(5926257605918807848)
XLA Ops:
  0.6 4.8 %collective-permute-start = (f32[256,768]{1,0:T(8,128)}, f32[256,768]{1,0:T(8,128)S(1)}, u32[]{:S(2)}, u32[]{:S(2)}) collective-permute-start(f32[256,768]{1,0:T(8,128)} %t_hbm.1), channel_id=1, source_target_pairs={{0,510},{1,3},{2,0},{3,5},{4,2},{5,7},{6,4},{7,9},{8,6},{9,11},{10... | collective-permute-start | bytes 2359304 | tf_op jit(solution)/shard_map/ppermute | solution.py:22
  5.5 13.7 %collective-permute-start.1 = (f32[256,768]{1,0:T(8,128)}, f32[256,768]{1,0:T(8,128)S(1)}, u32[]{:S(2)}, u32[]{:S(2)}) collective-permute-start(f32[256,768]{1,0:T(8,128)} %t_hbm.1), channel_id=1, source_target_pairs={{0,2},{1,511},{2,4},{3,1},{4,6},{5,3},{6,8},{7,5},{8,10},{9,7},{10... | collective-permute-start | bytes 2359304 | tf_op jit(solution)/shard_map/ppermute | solution.py:22
  19.2 2.9 %collective-permute-start.2 = (f32[256,768]{1,0:T(8,128)}, f32[256,768]{1,0:T(8,128)S(1)}, u32[]{:S(2)}, u32[]{:S(2)}) collective-permute-start(f32[256,768]{1,0:T(8,128)} %i_hbm.1), channel_id=1, source_target_pairs={{0,1},{1,0},{2,3},{3,2},{4,5},{5,4},{6,7},{7,6},{8,9},{9,8},{10,11... | collective-permute-start | bytes 2359304 | tf_op jit(solution)/shard_map/ppermute | solution.py:22
  22.0 0.0 copy-start
  22.0 1.1 %copy-done = f32[256,768]{1,0:T(8,128)S(1)} copy-done((f32[256,768]{1,0:T(8,128)S(1)}, f32[256,768]{1,0:T(8,128)}, u32[]{:S(2)}) %copy-start) | copy-done | bytes 786456
  23.2 2.8 %shard_map.49 = (f32[192,768]{1,0:T(8,128)S(1)}, f32[64,768]{1,0:T(8,128)S(1)}, f32[256,768]{1,0:T(8,128)S(1)}, f32[8,256]{1,0:T(8,128)S(1)}, bf16[256,768]{1,0:...) custom-call(f32[256,768]{1,0:T(8,128)} %i_hbm.1, ...), custom_call_target="tpu_custom_call" | custom-call | flops 1000 | bytes 1000 | tf_op jit(solution)/shard_map/pallas_call | solution.py:194
  26.0 1.9 %collective-permute-start.6 = (f32[256,768]{1,0:T(8,128)}, f32[256,768]{1,0:T(8,128)S(1)}, u32[]{:S(2)}, u32[]{:S(2)}) collective-permute-start(f32[256,768]{1,0:T(8,128)} %i_hbm.1), channel_id=1, source_target_pairs={{0,510},{1,3},{2,0},{3,5},{4,2},{5,7},{6,4},{7,9},{8,6},{9,11},{10... | collective-permute-start | bytes 2359304 | tf_op jit(solution)/shard_map/ppermute | solution.py:22
  27.9 9.1 %collective-permute-start.7 = (f32[256,768]{1,0:T(8,128)}, f32[256,768]{1,0:T(8,128)S(1)}, u32[]{:S(2)}, u32[]{:S(2)}) collective-permute-start(f32[256,768]{1,0:T(8,128)} %i_hbm.1), channel_id=1, source_target_pairs={{0,2},{1,511},{2,4},{3,1},{4,6},{5,3},{6,8},{7,5},{8,10},{9,7},{10... | collective-permute-start | bytes 2359304 | tf_op jit(solution)/shard_map/ppermute | solution.py:22
  37.0 0.0 collective-permute-done.in_ref
  37.0 0.0 collective-permute-done.1.out_ref
  37.0 0.0 collective-permute-done.2.i_sib_ref
  37.0 1.9 %shard_map.50 = (f32[256,768]{1,0:T(8,128)S(1)}, f32[8,256]{1,0:T(8,128)S(1)}, bf16[256,768]{1,0:T(8,128)(2,1)S(1)}, bf16[256,768]{1,0:T(8,128)(2,1)S(1)}) custom-call(bf16[256,768]{1,0:T(8,128)(2,1)S(1)} %get-tuple-element.37.i_high_ref, bf16[256,768]{1,0:T(8,128)(2,1)S(1)} %get-tuple-element.38.i_low_ref, f32[256,768]{1,0:T(8,128)S(1)} %collective-permute-done.in_ref, ...), custom_call_target="tpu_custom_call" | custom-call | flops 1000 | bytes 1000 | tf_op jit(solution)/shard_map/pallas_call | solution.py:194
  38.9 3.3 %collective-permute-start.3 = (f32[192,768]{1,0:T(8,128)S(1)}, f32[192,768]{1,0:T(8,128)S(1)}, u32[]{:S(2)}, u32[]{:S(2)}) collective-permute-start(f32[192,768]{1,0:T(8,128)S(1)} %get-tuple-element.45), channel_id=1, source_target_pairs={{0,1},{1,0},{2,3},{3,2},{4,5},{5,4},{6,7},{7,6},{8,9},{9,8},{10,11... | collective-permute-start | bytes 1769480 | tf_op jit(solution)/shard_map/ppermute | solution.py:22
  42.3 1.9 %collective-permute-start.5 = (f32[256,768]{1,0:T(8,128)S(1)}, f32[256,768]{1,0:T(8,128)S(1)}, u32[]{:S(2)}, u32[]{:S(2)}) collective-permute-start(f32[256,768]{1,0:T(8,128)S(1)} %collective-permute-done.in_ref), channel_id=1, source_target_pairs={{0,511},{1,2},{2,1},{3,4},{4,3},{5,6},{6,5},{7,8},{8,7},{9,10},{10... | collective-permute-start | bytes 2359304 | tf_op jit(solution)/shard_map/ppermute | solution.py:22
  44.2 8.3 %collective-permute-start.4 = (f32[64,768]{1,0:T(8,128)S(1)}, f32[64,768]{1,0:T(8,128)S(1)}, u32[]{:S(2)}, u32[]{:S(2)}) collective-permute-start(f32[64,768]{1,0:T(8,128)S(1)} %get-tuple-element.47), channel_id=1, source_target_pairs={{0,1},{1,0},{2,3},{3,2},{4,5},{5,4},{6,7},{7,6},{8,9},{9,8},{10,11... | collective-permute-start | bytes 589832 | tf_op jit(solution)/shard_map/ppermute | solution.py:22
  52.5 0.0 collective-permute-done.6.in_ref
  52.5 1.9 %collective-permute-start.8 = (f32[256,768]{1,0:T(8,128)S(1)}, f32[256,768]{1,0:T(8,128)S(1)}, u32[]{:S(2)}, u32[]{:S(2)}) collective-permute-start(f32[256,768]{1,0:T(8,128)S(1)} %collective-permute-done.6.in_ref), channel_id=1, source_target_pairs={{0,511},{1,2},{2,1},{3,4},{4,3},{5,6},{6,5},{7,8},{8,7},{9,10},{10... | collective-permute-start | bytes 2359304 | tf_op jit(solution)/shard_map/ppermute | solution.py:22
  54.5 0.0 collective-permute-done.4.t_sib_second
  54.5 0.0 collective-permute-done.3.t_sib_first
  54.5 2.4 %shard_map.51 = (f32[256,768]{1,0:T(8,128)S(1)}, f32[264,768]{1,0:T(8,128)S(1)}, f32[8,256]{1,0:T(8,128)S(1)}, bf16[512,768]{1,0:T(8,128)(2,1)S(1)}, bf16[512,768]{1,0:T(8,128)(2,1)S(1)}) custom-call(bf16[256,768]{1,0:T(8,128)(2,1)S(1)} %get-tuple-element.41.i_sib_high.sib_high_ref, bf16[256,768]{1,0:T(8,128)(2,1)S(1)} %get-tuple-element.42.i_sib_low.sib_low_ref, ...), custom_call_target="tpu_custom_call" | custom-call | flops 1000 | bytes 1000 | tf_op jit(solution)/shard_map/pallas_call | solution.py:194
  56.9 0.0 collective-permute-done.7.out_ref
  56.9 2.7 %shard_map.52 = (f32[256,768]{1,0:T(8,128)S(1)}, f32[520,768]{1,0:T(8,128)S(1)}) custom-call(bf16[512,768]{1,0:T(8,128)(2,1)S(1)} %get-tuple-element.51.high_ref.t_high_ref, bf16[512,768]{1,0:T(8,128)(2,1)S(1)} %get-tuple-element.59.low_ref.t_low_ref, f32[256,768]{1,0:T(8,128)S(1)} %collective-permute-done.6.in_ref, ...), custom_call_target="tpu_custom_call" | custom-call | flops 1000 | bytes 1000 | tf_op jit(solution)/shard_map/pallas_call | solution.py:194
  59.6 2.9 %collective-permute-start.9 = (f32[520,768]{1,0:T(8,128)S(1)}, f32[520,768]{1,0:T(8,128)S(1)}, u32[]{:S(2)}, u32[]{:S(2)}) collective-permute-start(f32[520,768]{1,0:T(8,128)S(1)} %get-tuple-element.67), channel_id=1, source_target_pairs={{0,1},{1,0},{2,3},{3,2},{4,5},{5,4},{6,7},{7,6},{8,9},{9,8},{10,11... | collective-permute-start | bytes 4792328 | tf_op jit(solution)/shard_map/ppermute | solution.py:22
  62.5 0.0 collective-permute-done.5.block_ref
  62.5 3.5 %shard_map.53 = (f32[256,768]{1,0:T(8,128)S(1)}, f32[8,256]{1,0:T(8,128)S(1)}, f32[256,768]{1,0:T(8,128)S(1)}) custom-call(bf16[256,768]{1,0:T(8,128)(2,1)S(1)} %get-tuple-element.37.i_high_ref, bf16[256,768]{1,0:T(8,128)(2,1)S(1)} %get-tuple-element.38.i_low_ref, bf16[512,768]{1,0:T(8,128)(2,1)S(1)} %get-tuple-element.51.high_ref.t_high_ref, ...), custom_call_target="tpu_custom_call" | custom-call | flops 2000000000 | bytes 1000 | tf_op jit(solution)/shard_map/pallas_call | solution.py:194
  66.0 0.1 collective-permute-done.8.block_ref
  66.1 0.6 shard_map.54
  66.8 0.0 collective-permute-done.9.theirs
  66.8 1.6 %shard_map.55 = (f32[256,768]{1,0:T(8,128)}, f32[256,768]{1,0:T(8,128)}, f32[1,256]{1,0:T(1,128)}) custom-call(bf16[256,256]{1,0:T(8,128)(2,1)S(1)} %get-tuple-element.61.c_high_ref, bf16[256,256]{1,0:T(8,128)(2,1)S(1)} %get-tuple-element.62.c_low_ref, bf16[256,768]{1,0:T(8,128)(2,1)S(1)} %get-tuple-element.63.b_high_ref, ...), custom_call_target="tpu_custom_call" | custom-call | flops 1000 | bytes 1000 | tf_op jit(solution)/shard_map/pallas_call | solution.py:194
Async XLA Ops:
  0.6 36.4 %collective-permute-start = (f32[256,768]{1,0:T(8,128)}, f32[256,768]{1,0:T(8,128)S(1)}, u32[]{:S(2)}, u32[]{:S(2)}) collective-permute-start(f32[256,768]{1,0:T(8,128)} %t_hbm.1), channel_id=1, source_target_pairs={{0,510},{1,3},{2,0},{3,5},{4,2},{5,7},{6,4},{7,9},{8,6},{9,11},{10... | collective-permute-start | bytes 2359304 | tf_op jit(solution)/shard_map/ppermute | solution.py:22
  5.5 31.5 %collective-permute-start.1 = (f32[256,768]{1,0:T(8,128)}, f32[256,768]{1,0:T(8,128)S(1)}, u32[]{:S(2)}, u32[]{:S(2)}) collective-permute-start(f32[256,768]{1,0:T(8,128)} %t_hbm.1), channel_id=1, source_target_pairs={{0,2},{1,511},{2,4},{3,1},{4,6},{5,3},{6,8},{7,5},{8,10},{9,7},{10... | collective-permute-start | bytes 2359304 | tf_op jit(solution)/shard_map/ppermute | solution.py:22
  19.2 17.9 %collective-permute-start.2 = (f32[256,768]{1,0:T(8,128)}, f32[256,768]{1,0:T(8,128)S(1)}, u32[]{:S(2)}, u32[]{:S(2)}) collective-permute-start(f32[256,768]{1,0:T(8,128)} %i_hbm.1), channel_id=1, source_target_pairs={{0,1},{1,0},{2,3},{3,2},{4,5},{5,4},{6,7},{7,6},{8,9},{9,8},{10,11... | collective-permute-start | bytes 2359304 | tf_op jit(solution)/shard_map/ppermute | solution.py:22
  22.0 1.1 %copy-start = (f32[256,768]{1,0:T(8,128)S(1)}, f32[256,768]{1,0:T(8,128)}, u32[]{:S(2)}) copy-start(f32[256,768]{1,0:T(8,128)} %t_hbm.1) | copy-start | bytes 2359300
  26.0 26.5 %collective-permute-start.6 = (f32[256,768]{1,0:T(8,128)}, f32[256,768]{1,0:T(8,128)S(1)}, u32[]{:S(2)}, u32[]{:S(2)}) collective-permute-start(f32[256,768]{1,0:T(8,128)} %i_hbm.1), channel_id=1, source_target_pairs={{0,510},{1,3},{2,0},{3,5},{4,2},{5,7},{6,4},{7,9},{8,6},{9,11},{10... | collective-permute-start | bytes 2359304 | tf_op jit(solution)/shard_map/ppermute | solution.py:22
  27.9 29.0 %collective-permute-start.7 = (f32[256,768]{1,0:T(8,128)}, f32[256,768]{1,0:T(8,128)S(1)}, u32[]{:S(2)}, u32[]{:S(2)}) collective-permute-start(f32[256,768]{1,0:T(8,128)} %i_hbm.1), channel_id=1, source_target_pairs={{0,2},{1,511},{2,4},{3,1},{4,6},{5,3},{6,8},{7,5},{8,10},{9,7},{10... | collective-permute-start | bytes 2359304 | tf_op jit(solution)/shard_map/ppermute | solution.py:22
  38.9 15.6 %collective-permute-start.3 = (f32[192,768]{1,0:T(8,128)S(1)}, f32[192,768]{1,0:T(8,128)S(1)}, u32[]{:S(2)}, u32[]{:S(2)}) collective-permute-start(f32[192,768]{1,0:T(8,128)S(1)} %get-tuple-element.45), channel_id=1, source_target_pairs={{0,1},{1,0},{2,3},{3,2},{4,5},{5,4},{6,7},{7,6},{8,9},{9,8},{10,11... | collective-permute-start | bytes 1769480 | tf_op jit(solution)/shard_map/ppermute | solution.py:22
  42.3 20.2 %collective-permute-start.5 = (f32[256,768]{1,0:T(8,128)S(1)}, f32[256,768]{1,0:T(8,128)S(1)}, u32[]{:S(2)}, u32[]{:S(2)}) collective-permute-start(f32[256,768]{1,0:T(8,128)S(1)} %collective-permute-done.in_ref), channel_id=1, source_target_pairs={{0,511},{1,2},{2,1},{3,4},{4,3},{5,6},{6,5},{7,8},{8,7},{9,10},{10... | collective-permute-start | bytes 2359304 | tf_op jit(solution)/shard_map/ppermute | solution.py:22
  44.2 10.3 %collective-permute-start.4 = (f32[64,768]{1,0:T(8,128)S(1)}, f32[64,768]{1,0:T(8,128)S(1)}, u32[]{:S(2)}, u32[]{:S(2)}) collective-permute-start(f32[64,768]{1,0:T(8,128)S(1)} %get-tuple-element.47), channel_id=1, source_target_pairs={{0,1},{1,0},{2,3},{3,2},{4,5},{5,4},{6,7},{7,6},{8,9},{9,8},{10,11... | collective-permute-start | bytes 589832 | tf_op jit(solution)/shard_map/ppermute | solution.py:22
  52.5 13.6 %collective-permute-start.8 = (f32[256,768]{1,0:T(8,128)S(1)}, f32[256,768]{1,0:T(8,128)S(1)}, u32[]{:S(2)}, u32[]{:S(2)}) collective-permute-start(f32[256,768]{1,0:T(8,128)S(1)} %collective-permute-done.6.in_ref), channel_id=1, source_target_pairs={{0,511},{1,2},{2,1},{3,4},{4,3},{5,6},{6,5},{7,8},{8,7},{9,10},{10... | collective-permute-start | bytes 2359304 | tf_op jit(solution)/shard_map/ppermute | solution.py:22
  59.6 7.1 %collective-permute-start.9 = (f32[520,768]{1,0:T(8,128)S(1)}, f32[520,768]{1,0:T(8,128)S(1)}, u32[]{:S(2)}, u32[]{:S(2)}) collective-permute-start(f32[520,768]{1,0:T(8,128)S(1)} %get-tuple-element.67), channel_id=1, source_target_pairs={{0,1},{1,0},{2,3},{3,2},{4,5},{5,4},{6,7},{7,6},{8,9},{9,8},{10,11... | collective-permute-start | bytes 4792328 | tf_op jit(solution)/shard_map/ppermute | solution.py:22
